TPU v7x, 256 devices: a whole 4x4x8 slice. The times are simulated.
256 devices in a mesh: date: 8 (over z_hi, x), space: 32 (over z_lo, y, core).
Axes of the slice: x: 4, y: 4, z: 8 (z_hi: 2, z_lo: 4; z = z_hi * 4 + z_lo), core: 2. Of those that a mesh axis runs over, the one named last changes fastest.
Arguments:
- stack: bfloat16 [32, 4096, 1280], P('date', 'space'), may hold values from -16 to 16
- w_qkv: bfloat16 [1280, 3840], P('space'), may hold values from -0.15625 to 0.15625
- w_out: bfloat16 [1280, 1280], P('space'), may hold values from -0.15625 to 0.15625
- conv_weight: float32 [3, 3, 1280], replicated, may hold values from -1 to 1
- conv_bias: float32 [1280], replicated, may hold values from -3 to 3
Outputs:
- output: bfloat16 [32, 4096, 1280], P('date', 'space')
All inputs are finite; a program needn't handle non-finite values.
Results may differ from a plain program's by a relative error of at most 0.013.
Values may be sent and summed in bfloat16 or wider, within the bound.
No kernel may reach another device: no remote copies, remote signals or barrier semaphores. Data moves between devices by JAX's collectives and lax.ppermute only.
A program may use at most 64 MiB of HBM per device.

v0:
```python
import math

import jax
import jax.numpy as jnp
from jax import lax
from jax.sharding import PartitionSpec as P

HEADS = 16
ROWS_DEV = 2


def with_halo(cells, sides, width):
    for axis, dim in sides:
        count = lax.axis_size(axis)
        ends = count - 1
        head = lax.slice_in_dim(cells, 0, width, axis=dim)
        tail = lax.slice_in_dim(cells, cells.shape[dim] - width, cells.shape[dim], axis=dim)
        cells = jnp.concatenate(
            [
                lax.ppermute(tail, axis, [(i, (i + 1) % count) for i in range(ends)]),
                cells,
                lax.ppermute(head, axis, [((i + 1) % count, i) for i in range(ends)]),
            ],
            axis=dim,
        )
    return cells


def attend_group(triple, head_size):
    queries, keys_all, values_all = triple
    dates, count, group = queries.shape
    shape4 = (dates, count, group // head_size, head_size)
    scores = jnp.einsum(
        "tphe,sphe->phts",
        queries.reshape(shape4),
        keys_all.reshape(shape4),
        preferred_element_type=jnp.float32,
    ) / math.sqrt(head_size)
    weights = jax.nn.softmax(scores, axis=-1).astype(jnp.bfloat16)
    attended = jnp.einsum(
        "phts,sphe->tphe", weights, values_all.reshape(shape4), preferred_element_type=jnp.float32
    )
    return attended.astype(jnp.bfloat16).reshape(dates, count, group)


def shards(stack, w_qkv, w_out, conv_weight, conv_bias):
    date_dev, patch_dev, width = stack.shape
    head_size = width // HEADS
    flat_rows = stack.reshape(date_dev * patch_dev, width)

    def add_rows(left, piece):
        return jnp.dot(left, piece, preferred_element_type=jnp.float32)

    projected = add_rows(flat_rows, lax.all_gather(w_qkv, "space", axis=0, tiled=True))
    projected = projected.astype(jnp.bfloat16).reshape(date_dev, patch_dev, 3 * width)
    queries = projected[:, :, :width]
    keys_all = projected[:, :, width : 2 * width]
    values_all = projected[:, :, 2 * width :]
    attended = attend_group(
        (
            lax.all_to_all(queries, "date", split_axis=2, concat_axis=0, tiled=True),
            lax.all_to_all(keys_all, "date", split_axis=2, concat_axis=0, tiled=True),
            lax.all_to_all(values_all, "date", split_axis=2, concat_axis=0, tiled=True),
        ),
        head_size,
    )
    returned = lax.all_to_all(attended, "date", split_axis=0, concat_axis=2, tiled=True)
    returned_rows = returned.reshape(date_dev * patch_dev, width)
    total = add_rows(returned_rows, lax.all_gather(w_out, "space", axis=0, tiled=True))
    mixed = (total + flat_rows.astype(jnp.float32)).astype(jnp.bfloat16)
    grid_cols = ROWS_DEV * lax.axis_size("space")
    band_rows = patch_dev // grid_cols
    band = mixed.reshape(date_dev, band_rows, grid_cols, width)
    widened = with_halo(band, (("space", 1),), 1)
    padded = jnp.pad(widened.astype(jnp.float32), ((0, 0), (0, 0), (1, 1), (0, 0)))
    result = band.astype(jnp.float32) + conv_bias
    for row_off in range(3):
        for col_off in range(3):
            result = (
                result
                + conv_weight[row_off, col_off]
                * padded[:, row_off : row_off + band_rows, col_off : col_off + grid_cols]
            )
    return result.astype(jnp.bfloat16).reshape(date_dev, patch_dev, width)


def solution(mesh):
    in_specs = (P("date", "space", None), P("space", None), P("space", None), P(), P())
    out_specs = P("date", "space", None)
    return jax.shard_map(shards, mesh=mesh, in_specs=in_specs, out_specs=out_specs, check_vma=False)
```

profile of v0, /device:TPU:221, one launch (start us, length us, event | category | flops | bytes accessed | tf_op | source)
XLA Modules:
  0.0 310.7 jit_solution(14526536935756123107)
XLA Ops:
  7.3 72.1 %all-gather.3.cloned.1.call-done = bf16[1280,3840]{1,0:T(8,128)(2,1)} async-done(((bf16[40,3840]{1,0:T(8,128)(2,1)}), bf16[1280,3840]{1,0:T(8,128)(2,1)}) %all-gather.3.cloned.1.call-update) | async-done | bytes 9830416 | tf_op jit(solution)/shard_map/all_gather | solution.py:54
  79.3 9.5 %convolution_convert_fusion = bf16[512,3840]{1,0:T(8,128)(2,1)S(1)} fusion(bf16[512,1280]{1,0:T(8,128)(2,1)} %bitcast.49, bf16[1280,3840]{1,0:T(8,128)(2,1)} %all-gather.3.cloned.1.call-done), kind=kOutput, calls=%fused_computation.1 | convolution fusion | flops 5035130880 | bytes 15073280 | tf_op jit(solution)/shard_map/dot_general | solution.py:52
  90.2 2.2 copy.37
  92.4 9.1 %all-to-all-start.2 = ((bf16[4,128,1280]{1,0,2:T(4,128)(2,1)}), bf16[4,128,1280]{1,0,2:T(4,128)(2,1)S(1)}, u32[]{:S(2)}, u32[]{:S(2)}) async-start(bf16[4,128,1280]{1,0,2:T(4,128)(2,1)} %copy.37), calls=%async_computation.2 | async-start | bytes 2621440 | tf_op jit(solution)/shard_map/all_to_all | solution.py:62
  101.4 2.2 copy.36
  103.6 26.8 %all-to-all-done.2 = bf16[4,128,1280]{1,0,2:T(4,128)(2,1)S(1)} async-done(((bf16[4,128,1280]{1,0,2:T(4,128)(2,1)}), bf16[4,128,1280]{1,0,2:T(4,128)(2,1)S(1)}, u32[]{:S(2)}, u32[]{:S(2)}) %all-to-all-start.2) | async-done | bytes 1310752 | tf_op jit(solution)/shard_map/all_to_all | solution.py:62
  130.4 9.3 %all-to-all-start.1 = ((bf16[4,128,1280]{1,0,2:T(4,128)(2,1)}), bf16[4,128,1280]{1,0,2:T(4,128)(2,1)S(1)}, u32[]{:S(2)}, u32[]{:S(2)}) async-start(bf16[4,128,1280]{1,0,2:T(4,128)(2,1)} %copy.36), calls=%async_computation.1 | async-start | bytes 2621440 | tf_op jit(solution)/shard_map/all_to_all | solution.py:61
  140.4 3.5 %copy.35 = bf16[4,128,1280]{1,0,2:T(4,128)(2,1)} copy(bf16[4,128,1280]{2,1,0:T(8,128)(2,1)} %get-tuple-element.16) | data formatting | bytes 2621440
  143.8 16.4 %all-to-all-done.1 = bf16[4,128,1280]{1,0,2:T(4,128)(2,1)S(1)} async-done(((bf16[4,128,1280]{1,0,2:T(4,128)(2,1)}), bf16[4,128,1280]{1,0,2:T(4,128)(2,1)S(1)}, u32[]{:S(2)}, u32[]{:S(2)}) %all-to-all-start.1) | async-done | bytes 1310752 | tf_op jit(solution)/shard_map/all_to_all | solution.py:61
  160.2 9.2 %all-to-all-start = ((bf16[4,128,1280]{1,0,2:T(4,128)(2,1)}), bf16[4,128,1280]{1,0,2:T(4,128)(2,1)}, u32[]{:S(2)}, u32[]{:S(2)}) async-start(bf16[4,128,1280]{1,0,2:T(4,128)(2,1)} %copy.35), calls=%async_computation | async-start | bytes 2621440 | tf_op jit(solution)/shard_map/all_to_all | solution.py:63
  169.7 3.0 copy.29
  173.0 3.0 copy.28
  176.0 23.7 %all-to-all-done = bf16[4,128,1280]{1,0,2:T(4,128)(2,1)} async-done(((bf16[4,128,1280]{1,0,2:T(4,128)(2,1)}), bf16[4,128,1280]{1,0,2:T(4,128)(2,1)}, u32[]{:S(2)}, u32[]{:S(2)}) %all-to-all-start) | async-done | bytes 1310752 | tf_op jit(solution)/shard_map/all_to_all | solution.py:63
  201.3 3.0 copy.30
  204.3 5.3 %fusion.31 = (f32[128,2,32]{2,1,0:T(2,128)S(1)}, f32[128,2,32,32]{2,3,1,0:T(8,128)}) fusion(bf16[32,128,2,80]{3,0,2,1:T(8,128)(2,1)} %copy.28, bf16[32,128,2,80]{3,0,2,1:T(8,128)(2,1)S(1)} %copy-done), kind=kOutput, calls=%fused_computation.53 | convolution fusion | flops 42729504 | bytes 3702784 | tf_op jit(solution)/shard_map/sub | solution.py:39
  209.5 3.7 %convert_bitcast_fusion = bf16[32,128,2,80]{3,0,2,1:T(8,128)(2,1)S(1)} fusion(bf16[32,128,2,80]{3,0,2,1:T(8,128)(2,1)} %copy.30, f32[128,2,32,32]{2,3,1,0:T(8,128)} %get-tuple-element.20, f32[128,2,32]{2,1,0:T(2,128)S(1)} %get-tuple-element.19), kind=kOutput, calls=%fused_computation.35 | convolution fusion | flops 43122688 | bytes 3702784 | tf_op jit(solution)/shard_map/phts,sphe->tphe/dot_general | solution.py:40
  213.2 2.2 copy.32
  215.4 39.0 %all_to_all.60 = bf16[32,128,160]{1,2,0:T(8,128)(2,1)S(1)} all-to-all(bf16[32,128,160]{1,2,0:T(8,128)(2,1)S(1)} %bitcast.45), channel_id=1, replica_groups=mesh['date'=8,'space'=32] {'date'}, dimensions={0} | all-to-all | bytes 2621440 | tf_op jit(solution)/shard_map/all_to_all | solution.py:67
  255.1 22.3 %all-gather.5.cloned.1.call-done = bf16[1280,1280]{1,0:T(8,128)(2,1)} async-done(((bf16[40,1280]{1,0:T(8,128)(2,1)}), bf16[1280,1280]{1,0:T(8,128)(2,1)}) %all-gather.5.cloned.1.call-update) | async-done | bytes 3276816 | tf_op jit(solution)/shard_map/all_gather | solution.py:69
  277.4 3.8 %fusion.4 = bf16[512,1280]{1,0:T(8,128)(2,1)S(1)} fusion(bf16[1280,1280]{1,0:T(8,128)(2,1)} %all-gather.5.cloned.1.call-done, bf16[512,1280]{1,0:T(8,128)(2,1)S(1)} %bitcast.50, bf16[160,8,4,128]{3,2,1,0:T(4,128)(2,1)S(1)} %bitcast.48), kind=kOutput, calls=%fused_computation.13 | convolution fusion | flops 1679687680 | bytes 7208960 | tf_op jit(solution)/shard_map/dot_general | solution.py:52
  281.4 4.2 %collective-permute-start = (bf16[4,1,64,1280]{3,2,1,0:T(8,128)(2,1)S(1)}, bf16[4,1,64,1280]{3,2,1,0:T(8,128)(2,1)S(1)}, u32[]{:S(2)}, u32[]{:S(2)}) collective-permute-start(bf16[4,1,64,1280]{3,2,1,0:T(8,128)(2,1)S(1)} %get-tuple-element.17), channel_id=1, source_target_pairs={{0,1},{1,2},{2,3},{3,4},{4,5},{5,6},{6,7},{7,8},{8,9},{9,10},{10,1... | collective-permute-start | bytes 1966088 | tf_op jit(solution)/shard_map/ppermute | solution.py:20
  287.7 5.4 %collective-permute-done = bf16[4,1,64,1280]{3,2,1,0:T(8,128)(2,1)S(1)} collective-permute-done((bf16[4,1,64,1280]{3,2,1,0:T(8,128)(2,1)S(1)}, bf16[4,1,64,1280]{3,2,1,0:T(8,128)(2,1)S(1)}, u32[]{:S(2)}, u32[]{:S(2)}) %collective-permute-start) | collective-permute-done | bytes 655392 | tf_op jit(solution)/shard_map/ppermute | solution.py:20
  293.1 6.5 %collective-permute-done.1 = bf16[4,1,64,1280]{3,2,1,0:T(8,128)(2,1)S(1)} collective-permute-done((bf16[4,1,64,1280]{3,2,1,0:T(8,128)(2,1)S(1)}, bf16[4,1,64,1280]{3,2,1,0:T(8,128)(2,1)S(1)}, u32[]{:S(2)}, u32[]{:S(2)}) %collective-permute-start.1) | collective-permute-done | bytes 655392 | tf_op jit(solution)/shard_map/ppermute | solution.py:22
  300.0 3.9 %fusion.20 = bf16[4,2,64,1280]{3,2,1,0:T(8,128)(2,1)} fusion(f32[4,4,64,1280]{3,2,1,0:T(8,128)S(1)} %maximum_convert_fusion, bf16[4,2,64,1280]{3,2,1,0:T(8,128)(2,1)S(1)} %bitcast.38, f32[1280]{0:T(1024)S(1)} %get-tuple-element.12, f32[1280]{0:T(1024)S(1)} %get-tuple-element.13, f32[1280]{0:T(1024)S(1)} %get-tuple-element.6, f32[1280]{0:T(1024)S(1)} %get-tuple-element.7, ...), kind=kLoop, calls=%fused_computation.33 | loop fusion | flops 13762560 | bytes 15810560 | tf_op jit(solution)/shard_map/convert_element_type | solution.py:84
  (24 shorter events, 8.2 us)
Async XLA Ops:
  6.5 72.8 %all-gather.3.cloned.1.call-start = ((), (), s32[]{:S(2)}) async-start(), calls=%async_computation.4 | async-start | bytes 10137600 | tf_op jit(solution)/shard_map/all_gather | solution.py:54
  92.4 38.0 %all-to-all-start.2 = ((bf16[4,128,1280]{1,0,2:T(4,128)(2,1)}), bf16[4,128,1280]{1,0,2:T(4,128)(2,1)S(1)}, u32[]{:S(2)}, u32[]{:S(2)}) async-start(bf16[4,128,1280]{1,0,2:T(4,128)(2,1)} %copy.37), calls=%async_computation.2 | async-start | bytes 2621440 | tf_op jit(solution)/shard_map/all_to_all | solution.py:62
  130.4 29.8 %all-to-all-start.1 = ((bf16[4,128,1280]{1,0,2:T(4,128)(2,1)}), bf16[4,128,1280]{1,0,2:T(4,128)(2,1)S(1)}, u32[]{:S(2)}, u32[]{:S(2)}) async-start(bf16[4,128,1280]{1,0,2:T(4,128)(2,1)} %copy.36), calls=%async_computation.1 | async-start | bytes 2621440 | tf_op jit(solution)/shard_map/all_to_all | solution.py:61
  139.6 137.8 %all-gather.5.cloned.1.call-start = ((), (), s32[]{:S(2)}) async-start(), calls=%async_computation.5 | async-start | bytes 3379200 | tf_op jit(solution)/shard_map/all_gather | solution.py:69
  160.2 39.5 %all-to-all-start = ((bf16[4,128,1280]{1,0,2:T(4,128)(2,1)}), bf16[4,128,1280]{1,0,2:T(4,128)(2,1)}, u32[]{:S(2)}, u32[]{:S(2)}) async-start(bf16[4,128,1280]{1,0,2:T(4,128)(2,1)} %copy.35), calls=%async_computation | async-start | bytes 2621440 | tf_op jit(solution)/shard_map/all_to_all | solution.py:63
  201.2 3.1 %copy-start = (bf16[32,128,2,80]{3,0,2,1:T(8,128)(2,1)S(1)}, bf16[32,128,2,80]{3,0,2,1:T(8,128)(2,1)}, u32[]{:S(2)}) copy-start(bf16[32,128,2,80]{3,0,2,1:T(8,128)(2,1)} %copy.29) | copy-start | bytes 3932164
  215.4 62.0 %copy-start.3 = (bf16[4,128,1280]{2,1,0:T(8,128)(2,1)S(1)}, bf16[4,128,1280]{2,1,0:T(8,128)(2,1)}, u32[]{:S(2)}) copy-start(bf16[4,128,1280]{2,1,0:T(8,128)(2,1)} %param.5) | copy-start | bytes 3932164
  281.2 6.3 %copy-start.1 = (f32[3,3,1280]{2,1,0:T(4,128)S(1)}, f32[3,3,1280]{2,1,0:T(4,128)}, u32[]{:S(2)}) copy-start(f32[3,3,1280]{2,1,0:T(4,128)} %param.8) | copy-start | bytes 138244
  281.4 11.8 %collective-permute-start = (bf16[4,1,64,1280]{3,2,1,0:T(8,128)(2,1)S(1)}, bf16[4,1,64,1280]{3,2,1,0:T(8,128)(2,1)S(1)}, u32[]{:S(2)}, u32[]{:S(2)}) collective-permute-start(bf16[4,1,64,1280]{3,2,1,0:T(8,128)(2,1)S(1)} %get-tuple-element.17), channel_id=1, source_target_pairs={{0,1},{1,2},{2,3},{3,4},{4,5},{5,6},{6,7},{7,8},{8,9},{9,10},{10,1... | collective-permute-start | bytes 1966088 | tf_op jit(solution)/shard_map/ppermute | solution.py:20
  285.6 14.0 %collective-permute-start.1 = (bf16[4,1,64,1280]{3,2,1,0:T(8,128)(2,1)S(1)}, bf16[4,1,64,1280]{3,2,1,0:T(8,128)(2,1)S(1)}, u32[]{:S(2)}, u32[]{:S(2)}) collective-permute-start(bf16[4,1,64,1280]{3,2,1,0:T(8,128)(2,1)S(1)} %get-tuple-element.18), channel_id=1, source_target_pairs={{1,0},{2,1},{3,2},{4,3},{5,4},{6,5},{7,6},{8,7},{9,8},{10,9},{11,1... | collective-permute-start | bytes 1966088 | tf_op jit(solution)/shard_map/ppermute | solution.py:22
  287.7 12.3 %copy-start.2 = (f32[1280]{0:T(1024)S(1)}, f32[1280]{0:T(1024)}, u32[]{:S(2)}) copy-start(f32[1280]{0:T(1024)} %param.9) | copy-start | bytes 15364
Sparse Core Ops, SparseCore 0:
  9.2 70.0 all-gather.2
  142.3 135.0 all-gather.4
where the time goes:
time: 311 us
  waiting for transfers between devices  175 us (56%)
  blocking collectives  39 us (13%)
  starting transfers between devices  33.7 us (11%)
  local copies, waits for them, and re-layouts  23.4 us (8%)
  matrix products  22.2 us (7%)
  between operations  13.6 us (4%)
  other arithmetic  4.26 us (1%)
    all_gather x1, waiting for transfers between devices, shards(): lax.all_gather(w_qkv, 'space', axis=0, tiled=True)  72.1 us
    all_to_all x1, blocking collectives, shards(): lax.all_to_all(attended, 'date', split_axis=0, concat_axis=2, tiled=True)  39 us
    all_to_all x1, waiting for transfers between devices, shards(): lax.all_to_all(keys_all, 'date', split_axis=2, concat_axis=0, tiled=True)  26.8 us
    all_to_all x1, waiting for transfers between devices, shards(): lax.all_to_all(values_all, 'date', split_axis=2, concat_axis=0, tiled=True)  23.7 us
    all_gather x1, waiting for transfers between devices, shards(): lax.all_gather(w_out, 'space', axis=0, tiled=True)  22.3 us
    all_to_all x1, waiting for transfers between devices, shards(): lax.all_to_all(queries, 'date', split_axis=2, concat_axis=0, tiled=True)  16.4 us
    dot_general x2, matrix products, add_rows(): return jnp.dot(left, piece, preferred_element_type=jnp.float32)  13.3 us
    all_to_all x1, starting transfers between devices, shards(): lax.all_to_all(queries, 'date', split_axis=2, concat_axis=0, tiled=True)  9.26 us
  transfers between devices with their start and end apart: 7, of which 7 were waited for; matrix products, arithmetic and copies ran while one was open for 9% of the time, Pallas kernels for 0%

commit v1 on v0

v1 whole, which is shorter than its diff:
```python
import functools
import math

import jax
import jax.numpy as jnp
from jax import lax
from jax.experimental import pallas as pl
from jax.experimental.pallas import tpu as pltpu
from jax.sharding import Mesh
from jax.sharding import PartitionSpec as P

HEADS = 16
GROUP = 8
BF16 = jnp.bfloat16
F32 = jnp.float32


def dot(a, b):
    return jnp.dot(a, b, preferred_element_type=F32)


def attend_rows(queries, keys, values, head_size):
    width = queries.shape[1]
    rows, cols = queries.shape[0], keys.shape[0]
    same = (
        lax.broadcasted_iota(jnp.int32, (rows, cols), 0) % GROUP
        == lax.broadcasted_iota(jnp.int32, (rows, cols), 1) % GROUP
    )
    tiles = [None] * (width // 128)
    for head in range(width // head_size):
        start, stop = head * head_size, (head + 1) * head_size
        first, last = start // 128, -(-stop // 128)
        window = slice(first * 128, last * 128)
        lane = lax.broadcasted_iota(jnp.int32, (rows, (last - first) * 128), 1) + first * 128
        inside = (lane >= start) & (lane < stop)
        query = jnp.where(inside, queries[:, window], jnp.zeros((), BF16))
        scores = lax.dot_general(
            query, keys[:, window], (((1,), (1,)), ((), ())), preferred_element_type=F32
        )
        scores = jnp.where(same, scores * (1.0 / math.sqrt(head_size)), -jnp.inf)
        exps = jnp.exp(scores - jnp.max(scores, axis=1, keepdims=True))
        weights = (exps * (1.0 / jnp.sum(exps, axis=1, keepdims=True))).astype(BF16)
        out = dot(weights, values[:, window])
        out = jnp.where(inside, out, 0.0)
        for tile in range(first, last):
            part = out[:, (tile - first) * 128 : (tile - first + 1) * 128]
            tiles[tile] = part if tiles[tile] is None else tiles[tile] + part
    return jnp.concatenate(tiles, axis=1).astype(BF16)


def block_kernel(head_size, *refs):
    blocks, w_hbm, out, x_vm, w_vm, q_vm, k_vm, v_vm, att, x_sem, w_sem = (
        refs[:8],
        *refs[8:],
    )
    half = w_vm.shape[-1]
    width = 2 * half
    x_copies = [
        pltpu.make_async_copy(block, x_vm.at[i], x_sem.at[i]) for i, block in enumerate(blocks)
    ]
    w_copies = {
        (mat, core, col): pltpu.make_async_copy(
            w_hbm.at[mat, col, core], w_vm.at[mat, core, :, col], w_sem.at[mat, core, col]
        )
        for core in range(2)
        for mat in range(4)
        for col in range(4)
    }
    for copy in x_copies:
        copy.start()
    for copy in w_copies.values():
        copy.start()
    for copy in x_copies:
        copy.wait()

    def wait_w(mat, core):
        for col in range(4):
            w_copies[mat, core, col].wait()

    for core in range(2):
        for mat, into, count in ((0, q_vm, 4), (1, k_vm, 8), (2, v_vm, 8)):
            wait_w(mat, core)

            def project(i, _, mat=mat, into=into):
                x = x_vm[pl.ds(i * 2, 2)].reshape(-1, width)
                w = w_vm[mat, core].reshape(width, half)
                into[pl.ds(i * 2, 2)] = dot(x, w).astype(BF16).reshape(2, 4, -1, half)
                return _

            lax.fori_loop(0, count // 2, project, 0)

        def attend(group, _):
            got = attend_rows(
                q_vm[:, pl.ds(group, 1)].reshape(-1, half),
                k_vm[:, pl.ds(group, 1)].reshape(-1, half),
                v_vm[:, pl.ds(group, 1)].reshape(-1, half),
                head_size,
            )
            att[:, pl.ds(group, 1), :, core * half : (core + 1) * half] = got.reshape(4, 1, -1, half)
            return _

        lax.fori_loop(0, 4, attend, 0)

    for core in range(2):
        wait_w(3, core)

        def mix(i, _):
            a = att[pl.ds(i * 2, 2)].reshape(-1, width)
            w = w_vm[3, core].reshape(width, half)
            cut = slice(core * half, (core + 1) * half)
            x = x_vm[pl.ds(i * 2, 2), :, cut].reshape(-1, half)
            total = dot(a, w) + x.astype(F32)
            out[pl.ds(i * 2, 2), :, cut] = total.astype(BF16).reshape(2, -1, half)
            return _

        lax.fori_loop(0, 2, mix, 0)


def run_block(blocks, w_all, head_size):
    rows, width = blocks[0].shape
    half = width // 2
    hbm = pl.BlockSpec(memory_space=pl.ANY)
    return pl.pallas_call(
        functools.partial(block_kernel, head_size),
        out_shape=jax.ShapeDtypeStruct((4, rows, width), BF16),
        in_specs=[hbm] * 9,
        out_specs=pl.BlockSpec(memory_space=pltpu.VMEM),
        scratch_shapes=[
            pltpu.VMEM((8, rows, width), BF16),
            pltpu.VMEM((4, 2, 4, 4, width // 16, half), BF16),
            pltpu.VMEM((4, 4, rows // 4, half), BF16),
            pltpu.VMEM((8, 4, rows // 4, half), BF16),
            pltpu.VMEM((8, 4, rows // 4, half), BF16),
            pltpu.VMEM((4, 4, rows // 4, width), BF16),
            pltpu.SemaphoreType.DMA((8,)),
            pltpu.SemaphoreType.DMA((4, 2, 4)),
        ],
        compiler_params=pltpu.CompilerParams(vmem_limit_bytes=48 * 1024 * 1024),
    )(*blocks, w_all)


def ring(count, shift):
    return [(i, (i + shift) % count) for i in range(count)]


def gather_weights(w_qkv, w_out):
    rows, width = w_out.shape
    half = width // 2
    x, zl, core = lax.axis_index("x"), lax.axis_index("zl"), lax.axis_index("c")
    joined = jnp.concatenate(
        [w_qkv.reshape(rows, 3, 2, half), w_out.reshape(rows, 1, 2, half)], axis=1
    )
    mine = lax.dynamic_index_in_dim(joined, x, 1, keepdims=False)
    keep = lax.dynamic_index_in_dim(mine, core, 1, keepdims=False)
    give = lax.dynamic_index_in_dim(mine, 1 - core, 1, keepdims=False)
    other = lax.ppermute(give, "c", ring(2, 1))
    piece = jnp.zeros((2, rows, half), BF16)
    piece = lax.dynamic_update_index_in_dim(piece, keep, core, 0)
    piece = lax.dynamic_update_index_in_dim(piece, other, 1 - core, 0).reshape(2 * rows, half)
    planes = jnp.zeros((4, 2 * rows, half), BF16)
    planes = lax.dynamic_update_index_in_dim(planes, piece, zl, 0)
    for shift in (1, 7, 2):
        got = lax.ppermute(piece, ("zh", "zl"), ring(8, shift))
        planes = lax.dynamic_update_index_in_dim(planes, got, (zl + 8 - shift) % 4, 0)
    gathered = lax.all_gather(planes, ("x", "y", "c"), axis=0, tiled=False)
    return gathered.reshape(4, 4, 2, 4, 2 * rows, half)


def shards(stack, w_qkv, w_out, conv_weight, conv_bias):
    date_dev, patch_dev, width = stack.shape
    head_size = width // HEADS
    x = lax.axis_index("x")
    part = patch_dev // 4

    def cut(shift):
        block = lax.dynamic_slice_in_dim(stack, ((x + shift) % 4) * part, part, axis=1)
        block = block.reshape(date_dev, part // GROUP, GROUP, width).transpose(1, 0, 2, 3)
        return block.reshape(date_dev * part, width)

    shifts = (0, 1, 3, 2)
    own = [cut(0)] + [lax.ppermute(cut(s), "x", ring(4, s)) for s in shifts[1:]]
    partner = [lax.ppermute(block, ("zh", "zl"), ring(8, 4)) for block in own]
    w_all = gather_weights(w_qkv, w_out)
    mixed_slots = run_block(own + partner, w_all, head_size)

    home = jnp.zeros((4, date_dev * part, width), BF16)
    for slot, s in enumerate(shifts):
        back = mixed_slots[slot]
        if s:
            back = lax.ppermute(back, "x", ring(4, 4 - s))
        home = lax.dynamic_update_index_in_dim(home, back, (x + s) % 4, 0)
    mixed = home.reshape(4, part // GROUP, date_dev, GROUP, width).transpose(2, 0, 1, 3, 4)

    band_rows = 2
    grid_cols = patch_dev // band_rows
    band = mixed.reshape(date_dev, band_rows, grid_cols, width)
    bands = 32
    axes = ("zl", "y", "c")
    above = lax.ppermute(band[:, -1:], axes, [(i, i + 1) for i in range(bands - 1)])
    below = lax.ppermute(band[:, :1], axes, [(i + 1, i) for i in range(bands - 1)])
    widened = jnp.concatenate([above, band, below], axis=1)
    padded = jnp.pad(widened.astype(F32), ((0, 0), (0, 0), (1, 1), (0, 0)))
    result = band.astype(F32) + conv_bias
    for row_off in range(3):
        for col_off in range(3):
            result = (
                result
                + conv_weight[row_off, col_off]
                * padded[:, row_off : row_off + band_rows, col_off : col_off + grid_cols]
            )
    return result.astype(BF16).reshape(date_dev, patch_dev, width)


def solution(mesh):
    fine = Mesh(mesh.devices.reshape(2, 4, 4, 4, 2), ("zh", "x", "zl", "y", "c"))
    date, space = ("zh", "x"), ("zl", "y", "c")
    in_specs = (P(date, space, None), P(space, None), P(space, None), P(), P())
    out_specs = P(date, space, None)
    return jax.shard_map(
        shards, mesh=fine, in_specs=in_specs, out_specs=out_specs, check_vma=False
    )
```

time: 311 us -> 184 us (0.59)
  the two profiles are of different devices: /device:TPU:221 before, /device:TPU:25 now
where the time goes in v1:
time: 184 us
  waiting for transfers between devices  81.9 us (45%)
  starting transfers between devices  41.7 us (23%)
  Pallas kernels  38.1 us (21%)
  between operations  13.7 us (7%)
  other arithmetic  4.92 us (3%)
  local copies, waits for them, and re-layouts  3.8 us (2%)
    ppermute x4, waiting for transfers between devices, shards(): partner = [lax.ppermute(block, ('zh', 'zl'), ring(8, 4)) for block in own]  42.5 us
    pallas_call x1, Pallas kernels, run_block(): pl.pallas_call(functools.partial(block_kernel, head_size), out_shape=jax....  38.1 us
    ppermute x4, starting transfers between devices, shards(): partner = [lax.ppermute(block, ('zh', 'zl'), ring(8, 4)) for block in own]  19 us
    ppermute x3, waiting for transfers between devices, shards(): back = lax.ppermute(back, 'x', ring(4, 4 - s))  14.3 us
    ppermute x1, starting transfers between devices, shards(): lax.ppermute(band[:, -1:], axes, [(i, i + 1) for i in range(bands - 1)])  7.22 us
    ppermute x3, waiting for transfers between devices, gather_weights(): got = lax.ppermute(piece, ('zh', 'zl'), ring(8, shift))  6.77 us
    ppermute x1, waiting for transfers between devices, shards(): lax.ppermute(band[:, :1], axes, [(i + 1, i) for i in range(bands - 1)])  6.51 us
    ppermute x3, starting transfers between devices, gather_weights(): got = lax.ppermute(piece, ('zh', 'zl'), ring(8, shift))  5.74 us
  transfers between devices with their start and end apart: 17, of which 14 were waited for; matrix products, arithmetic and copies ran while one was open for 0% of the time, Pallas kernels for 0%

profile of v1, /device:TPU:25, one launch (start us, length us, event | category | flops | bytes accessed | tf_op | source)
XLA Modules:
  0.0 184.1 jit_solution(1692382571437532709)
XLA Ops:
  11.0 1.7 collective-permute-start.8
  12.7 4.0 %collective-permute-start.9 = (bf16[80,640]{1,0:T(8,128)(2,1)S(1)}, bf16[80,640]{1,0:T(8,128)(2,1)S(1)}, u32[]{:S(2)}, u32[]{:S(2)}) collective-permute-start(bf16[80,640]{1,0:T(8,128)(2,1)S(1)} %bitcast.62), channel_id=1, source_target_pairs={{0,152},{8,0},{16,8},{24,16},{128,24},{136,128},{144,136},{152,144... | collective-permute-start | bytes 307208 | tf_op jit(solution)/shard_map/ppermute | solution.py:163
  16.8 2.8 %collective-permute-done.8 = bf16[80,640]{1,0:T(8,128)(2,1)S(1)} collective-permute-done((bf16[80,640]{1,0:T(8,128)(2,1)S(1)}, bf16[80,640]{1,0:T(8,128)(2,1)S(1)}, u32[]{:S(2)}, u32[]{:S(2)}) %collective-permute-start.8) | collective-permute-done | bytes 102432 | tf_op jit(solution)/shard_map/ppermute | solution.py:163
  19.6 3.9 %collective-permute-done.10 = bf16[80,640]{1,0:T(8,128)(2,1)S(1)} collective-permute-done((bf16[80,640]{1,0:T(8,128)(2,1)S(1)}, bf16[80,640]{1,0:T(8,128)(2,1)S(1)}, u32[]{:S(2)}, u32[]{:S(2)}) %collective-permute-start.10) | collective-permute-done | bytes 102432 | tf_op jit(solution)/shard_map/ppermute | solution.py:163
  24.6 1.3 collective-permute-start
  25.9 1.5 collective-permute-start.1
  27.5 1.6 collective-permute-start.2
  29.1 5.8 %collective-permute-start.3 = (bf16[128,1280]{1,0:T(8,128)(2,1)S(1)}, bf16[128,1280]{1,0:T(8,128)(2,1)S(1)}, u32[]{:S(2)}, u32[]{:S(2)}) collective-permute-start(bf16[128,1280]{1,0:T(8,128)(2,1)S(1)} %bitcast.54), channel_id=1, source_target_pairs={{0,128},{8,136},{16,144},{24,152},{128,0},{136,8},{144,16},{152,24... | collective-permute-start | bytes 983048 | tf_op jit(solution)/shard_map/ppermute | solution.py:182
  34.9 5.4 %collective-permute-start.4 = (bf16[128,1280]{1,0:T(8,128)(2,1)S(1)}, bf16[128,1280]{1,0:T(8,128)(2,1)S(1)}, u32[]{:S(2)}, u32[]{:S(2)}) collective-permute-start(bf16[128,1280]{1,0:T(8,128)(2,1)S(1)} %collective-permute-done.refs_1_), channel_id=1, source_target_pairs={{0,128},{8,136},{16,144},{24,152},{128,0},{136,8},{144,16},{152,24... | collective-permute-start | bytes 983048 | tf_op jit(solution)/shard_map/ppermute | solution.py:182
  40.4 7.8 %collective-permute-start.6 = (bf16[128,1280]{1,0:T(8,128)(2,1)S(1)}, bf16[128,1280]{1,0:T(8,128)(2,1)S(1)}, u32[]{:S(2)}, u32[]{:S(2)}) collective-permute-start(bf16[128,1280]{1,0:T(8,128)(2,1)S(1)} %collective-permute-done.2.refs_3_), channel_id=1, source_target_pairs={{0,128},{8,136},{16,144},{24,152},{128,0},{136,8},{144,16},{152,24... | collective-permute-start | bytes 983048 | tf_op jit(solution)/shard_map/ppermute | solution.py:182
  48.3 6.8 %collective-permute-done.3.refs_4_ = bf16[128,1280]{1,0:T(8,128)(2,1)S(1)} collective-permute-done((bf16[128,1280]{1,0:T(8,128)(2,1)S(1)}, bf16[128,1280]{1,0:T(8,128)(2,1)S(1)}, u32[]{:S(2)}, u32[]{:S(2)}) %collective-permute-start.3) | collective-permute-done | bytes 327712 | tf_op jit(solution)/shard_map/ppermute | solution.py:182
  55.1 20.8 %collective-permute-done.4.refs_5_ = bf16[128,1280]{1,0:T(8,128)(2,1)S(1)} collective-permute-done((bf16[128,1280]{1,0:T(8,128)(2,1)S(1)}, bf16[128,1280]{1,0:T(8,128)(2,1)S(1)}, u32[]{:S(2)}, u32[]{:S(2)}) %collective-permute-start.4) | collective-permute-done | bytes 327712 | tf_op jit(solution)/shard_map/ppermute | solution.py:182
  75.8 7.9 %collective-permute-done.5.refs_6_ = bf16[128,1280]{1,0:T(8,128)(2,1)S(1)} collective-permute-done((bf16[128,1280]{1,0:T(8,128)(2,1)S(1)}, bf16[128,1280]{1,0:T(8,128)(2,1)S(1)}, u32[]{:S(2)}, u32[]{:S(2)}) %collective-permute-start.5) | collective-permute-done | bytes 327712 | tf_op jit(solution)/shard_map/ppermute | solution.py:182
  83.7 7.0 %collective-permute-done.6.refs_7_ = bf16[128,1280]{1,0:T(8,128)(2,1)S(1)} collective-permute-done((bf16[128,1280]{1,0:T(8,128)(2,1)S(1)}, bf16[128,1280]{1,0:T(8,128)(2,1)S(1)}, u32[]{:S(2)}, u32[]{:S(2)}) %collective-permute-start.6) | collective-permute-done | bytes 327712 | tf_op jit(solution)/shard_map/ppermute | solution.py:182
  90.7 5.5 %all-gather.2.cloned.1.call-done = bf16[32,4,80,640]{3,2,1,0:T(8,128)(2,1)} async-done(((bf16[1,4,80,640]{3,2,1,0:T(8,128)(2,1)}), bf16[32,4,80,640]{3,2,1,0:T(8,128)(2,1)}) %all-gather.2.cloned.1.call-update) | async-done | bytes 13107216 | tf_op jit(solution)/shard_map/all_gather | solution.py:165
  96.2 38.1 %shard_map.55 = bf16[4,128,1280]{2,1,0:T(8,128)(2,1)S(1)} custom-call(bf16[128,1280]{1,0:T(8,128)(2,1)S(1)} %bitcast.55, bf16[128,1280]{1,0:T(8,128)(2,1)S(1)} %collective-permute-done.refs_1_, bf16[128,1280]{1,0:T(8,128)(2,1)S(1)} %collective-permute-done.1.refs_2_, bf16[128,1280]{1,0:T(8,128)(2,1)S(1)} %collective-permute-done.2.refs_3_, ...), custom_call_target="tpu_custom_call" | custom-call | tf_op jit(solution)/shard_map/pallas_call | solution.py:123
  137.2 6.5 %collective-permute-done.11 = bf16[128,1280]{1,0:T(8,128)(2,1)S(1)} collective-permute-done((bf16[128,1280]{1,0:T(8,128)(2,1)S(1)}, bf16[128,1280]{1,0:T(8,128)(2,1)S(1)}, u32[]{:S(2)}, u32[]{:S(2)}) %collective-permute-start.11) | collective-permute-done | bytes 327712 | tf_op jit(solution)/shard_map/ppermute | solution.py:190
  143.7 2.6 %collective-permute-done.12 = bf16[128,1280]{1,0:T(8,128)(2,1)S(1)} collective-permute-done((bf16[128,1280]{1,0:T(8,128)(2,1)S(1)}, bf16[128,1280]{1,0:T(8,128)(2,1)S(1)}, u32[]{:S(2)}, u32[]{:S(2)}) %collective-permute-start.12) | collective-permute-done | bytes 327712 | tf_op jit(solution)/shard_map/ppermute | solution.py:190
  146.3 5.2 %collective-permute-done.13 = bf16[128,1280]{1,0:T(8,128)(2,1)S(1)} collective-permute-done((bf16[128,1280]{1,0:T(8,128)(2,1)S(1)}, bf16[128,1280]{1,0:T(8,128)(2,1)S(1)}, u32[]{:S(2)}, u32[]{:S(2)}) %collective-permute-start.13) | collective-permute-done | bytes 327712 | tf_op jit(solution)/shard_map/ppermute | solution.py:190
  151.8 7.2 %collective-permute-start.14 = (bf16[4,1,64,1280]{3,2,1,0:T(8,128)(2,1)S(1)}, bf16[4,1,64,1280]{3,2,1,0:T(8,128)(2,1)S(1)}, u32[]{:S(2)}, u32[]{:S(2)}) collective-permute-start(bf16[4,1,64,1280]{3,2,1,0:T(8,128)(2,1)S(1)} %get-tuple-element.14), channel_id=1, source_target_pairs={{0,1},{1,2},{2,3},{3,4},{4,5},{5,6},{6,7},{7,8},{8,9},{9,10},{10,1... | collective-permute-start | bytes 1966088 | tf_op jit(solution)/shard_map/ppermute | solution.py:199
  159.0 1.9 %collective-permute-start.15 = (bf16[4,1,64,1280]{3,2,1,0:T(8,128)(2,1)S(1)}, bf16[4,1,64,1280]{3,2,1,0:T(8,128)(2,1)S(1)}, u32[]{:S(2)}, u32[]{:S(2)}) collective-permute-start(bf16[4,1,64,1280]{3,2,1,0:T(8,128)(2,1)S(1)} %get-tuple-element.15), channel_id=1, source_target_pairs={{1,0},{2,1},{3,2},{4,3},{5,4},{6,5},{7,6},{8,7},{9,8},{10,9},{11,1... | collective-permute-start | bytes 1966088 | tf_op jit(solution)/shard_map/ppermute | solution.py:200
  161.1 5.4 %collective-permute-done.14 = bf16[4,1,64,1280]{3,2,1,0:T(8,128)(2,1)S(1)} collective-permute-done((bf16[4,1,64,1280]{3,2,1,0:T(8,128)(2,1)S(1)}, bf16[4,1,64,1280]{3,2,1,0:T(8,128)(2,1)S(1)}, u32[]{:S(2)}, u32[]{:S(2)}) %collective-permute-start.14) | collective-permute-done | bytes 655392 | tf_op jit(solution)/shard_map/ppermute | solution.py:199
  166.5 6.5 %collective-permute-done.15 = bf16[4,1,64,1280]{3,2,1,0:T(8,128)(2,1)S(1)} collective-permute-done((bf16[4,1,64,1280]{3,2,1,0:T(8,128)(2,1)S(1)}, bf16[4,1,64,1280]{3,2,1,0:T(8,128)(2,1)S(1)}, u32[]{:S(2)}, u32[]{:S(2)}) %collective-permute-start.15) | collective-permute-done | bytes 655392 | tf_op jit(solution)/shard_map/ppermute | solution.py:200
  173.4 3.9 %fusion.15 = bf16[4,2,64,1280]{3,2,1,0:T(8,128)(2,1)} fusion(f32[4,4,64,1280]{3,2,1,0:T(8,128)S(1)} %maximum_convert_fusion, bf16[4,2,64,1280]{3,2,1,0:T(8,128)(2,1)S(1)} %bitcast.58, f32[1280]{0:T(1024)S(1)} %get-tuple-element.12, f32[1280]{0:T(1024)S(1)} %get-tuple-element.13, f32[1280]{0:T(1024)S(1)} %get-tuple-element.6, f32[1280]{0:T(1024)S(1)} %get-tuple-element.7, ...), kind=kLoop, calls=%fused_computation.25 | loop fusion | flops 13762560 | bytes 15810560 | tf_op jit(solution)/shard_map/convert_element_type | solution.py:211
  (47 shorter events, 9.3 us)
Async XLA Ops:
  6.5 17.9 %copy-start.1 = (bf16[4,128,1280]{2,1,0:T(8,128)(2,1)S(1)}, bf16[4,128,1280]{2,1,0:T(8,128)(2,1)}, u32[]{:S(2)}) copy-start(bf16[4,128,1280]{2,1,0:T(8,128)(2,1)} %param.5) | copy-start | bytes 3932164
  6.5 89.7 %all-gather.2.cloned.1.call-start = ((), (), s32[]{:S(2)}) async-start(), calls=%async_computation | async-start | bytes 13516800 | tf_op jit(solution)/shard_map/all_gather | solution.py:165
  9.3 1.6 collective-permute-start.7
  11.0 8.6 %collective-permute-start.8 = (bf16[80,640]{1,0:T(8,128)(2,1)S(1)}, bf16[80,640]{1,0:T(8,128)(2,1)S(1)}, u32[]{:S(2)}, u32[]{:S(2)}) collective-permute-start(bf16[80,640]{1,0:T(8,128)(2,1)S(1)} %bitcast.61), channel_id=1, source_target_pairs={{0,8},{8,16},{16,24},{24,128},{128,136},{136,144},{144,152},{152,0... | collective-permute-start | bytes 307208 | tf_op jit(solution)/shard_map/ppermute | solution.py:163
  12.7 6.9 %collective-permute-start.9 = (bf16[80,640]{1,0:T(8,128)(2,1)S(1)}, bf16[80,640]{1,0:T(8,128)(2,1)S(1)}, u32[]{:S(2)}, u32[]{:S(2)}) collective-permute-start(bf16[80,640]{1,0:T(8,128)(2,1)S(1)} %bitcast.62), channel_id=1, source_target_pairs={{0,152},{8,0},{16,8},{24,16},{128,24},{136,128},{144,136},{152,144... | collective-permute-start | bytes 307208 | tf_op jit(solution)/shard_map/ppermute | solution.py:163
  16.7 6.9 %collective-permute-start.10 = (bf16[80,640]{1,0:T(8,128)(2,1)S(1)}, bf16[80,640]{1,0:T(8,128)(2,1)S(1)}, u32[]{:S(2)}, u32[]{:S(2)}) collective-permute-start(bf16[80,640]{1,0:T(8,128)(2,1)S(1)} %bitcast.63), channel_id=1, source_target_pairs={{0,16},{8,24},{16,128},{24,136},{128,144},{136,152},{144,0},{152,8... | collective-permute-start | bytes 307208 | tf_op jit(solution)/shard_map/ppermute | solution.py:163
  23.6 0.8 copy-start
  24.6 10.3 %collective-permute-start = (bf16[128,1280]{1,0:T(8,128)(2,1)S(1)}, bf16[128,1280]{1,0:T(8,128)(2,1)S(1)}, u32[]{:S(2)}, u32[]{:S(2)}) collective-permute-start(bf16[128,1280]{1,0:T(8,128)(2,1)S(1)} %bitcast.68), channel_id=1, source_target_pairs={{0,32},{32,64},{64,96},{96,0},{1,33},{33,65},{65,97},{97,1},{2,34}... | collective-permute-start | bytes 983048 | tf_op jit(solution)/shard_map/ppermute | solution.py:181
  25.9 14.3 %collective-permute-start.1 = (bf16[128,1280]{1,0:T(8,128)(2,1)S(1)}, bf16[128,1280]{1,0:T(8,128)(2,1)S(1)}, u32[]{:S(2)}, u32[]{:S(2)}) collective-permute-start(bf16[128,1280]{1,0:T(8,128)(2,1)S(1)} %bitcast.67), channel_id=1, source_target_pairs={{0,96},{32,0},{64,32},{96,64},{1,97},{33,1},{65,33},{97,65},{2,98}... | collective-permute-start | bytes 983048 | tf_op jit(solution)/shard_map/ppermute | solution.py:181
  27.5 13.0 %collective-permute-start.2 = (bf16[128,1280]{1,0:T(8,128)(2,1)S(1)}, bf16[128,1280]{1,0:T(8,128)(2,1)S(1)}, u32[]{:S(2)}, u32[]{:S(2)}) collective-permute-start(bf16[128,1280]{1,0:T(8,128)(2,1)S(1)} %bitcast.66), channel_id=1, source_target_pairs={{0,64},{32,96},{64,0},{96,32},{1,65},{33,97},{65,1},{97,33},{2,66}... | collective-permute-start | bytes 983048 | tf_op jit(solution)/shard_map/ppermute | solution.py:181
  29.1 25.9 %collective-permute-start.3 = (bf16[128,1280]{1,0:T(8,128)(2,1)S(1)}, bf16[128,1280]{1,0:T(8,128)(2,1)S(1)}, u32[]{:S(2)}, u32[]{:S(2)}) collective-permute-start(bf16[128,1280]{1,0:T(8,128)(2,1)S(1)} %bitcast.54), channel_id=1, source_target_pairs={{0,128},{8,136},{16,144},{24,152},{128,0},{136,8},{144,16},{152,24... | collective-permute-start | bytes 983048 | tf_op jit(solution)/shard_map/ppermute | solution.py:182
  34.9 40.9 %collective-permute-start.4 = (bf16[128,1280]{1,0:T(8,128)(2,1)S(1)}, bf16[128,1280]{1,0:T(8,128)(2,1)S(1)}, u32[]{:S(2)}, u32[]{:S(2)}) collective-permute-start(bf16[128,1280]{1,0:T(8,128)(2,1)S(1)} %collective-permute-done.refs_1_), channel_id=1, source_target_pairs={{0,128},{8,136},{16,144},{24,152},{128,0},{136,8},{144,16},{152,24... | collective-permute-start | bytes 983048 | tf_op jit(solution)/shard_map/ppermute | solution.py:182
  40.2 43.5 %collective-permute-start.5 = (bf16[128,1280]{1,0:T(8,128)(2,1)S(1)}, bf16[128,1280]{1,0:T(8,128)(2,1)S(1)}, u32[]{:S(2)}, u32[]{:S(2)}) collective-permute-start(bf16[128,1280]{1,0:T(8,128)(2,1)S(1)} %collective-permute-done.1.refs_2_), channel_id=1, source_target_pairs={{0,128},{8,136},{16,144},{24,152},{128,0},{136,8},{144,16},{152,24... | collective-permute-start | bytes 983048 | tf_op jit(solution)/shard_map/ppermute | solution.py:182
  40.4 50.3 %collective-permute-start.6 = (bf16[128,1280]{1,0:T(8,128)(2,1)S(1)}, bf16[128,1280]{1,0:T(8,128)(2,1)S(1)}, u32[]{:S(2)}, u32[]{:S(2)}) collective-permute-start(bf16[128,1280]{1,0:T(8,128)(2,1)S(1)} %collective-permute-done.2.refs_3_), channel_id=1, source_target_pairs={{0,128},{8,136},{16,144},{24,152},{128,0},{136,8},{144,16},{152,24... | collective-permute-start | bytes 983048 | tf_op jit(solution)/shard_map/ppermute | solution.py:182
  134.5 9.1 %collective-permute-start.11 = (bf16[128,1280]{1,0:T(8,128)(2,1)S(1)}, bf16[128,1280]{1,0:T(8,128)(2,1)S(1)}, u32[]{:S(2)}, u32[]{:S(2)}) collective-permute-start(bf16[128,1280]{1,0:T(8,128)(2,1)S(1)} %get-tuple-element.18), channel_id=1, source_target_pairs={{0,96},{32,0},{64,32},{96,64},{1,97},{33,1},{65,33},{97,65},{2,98}... | collective-permute-start | bytes 983048 | tf_op jit(solution)/shard_map/ppermute | solution.py:190
  135.4 10.9 %collective-permute-start.12 = (bf16[128,1280]{1,0:T(8,128)(2,1)S(1)}, bf16[128,1280]{1,0:T(8,128)(2,1)S(1)}, u32[]{:S(2)}, u32[]{:S(2)}) collective-permute-start(bf16[128,1280]{1,0:T(8,128)(2,1)S(1)} %get-tuple-element.17), channel_id=1, source_target_pairs={{0,32},{32,64},{64,96},{96,0},{1,33},{33,65},{65,97},{97,1},{2,34}... | collective-permute-start | bytes 983048 | tf_op jit(solution)/shard_map/ppermute | solution.py:190
  136.1 15.5 %collective-permute-start.13 = (bf16[128,1280]{1,0:T(8,128)(2,1)S(1)}, bf16[128,1280]{1,0:T(8,128)(2,1)S(1)}, u32[]{:S(2)}, u32[]{:S(2)}) collective-permute-start(bf16[128,1280]{1,0:T(8,128)(2,1)S(1)} %get-tuple-element.16), channel_id=1, source_target_pairs={{0,64},{32,96},{64,0},{96,32},{1,65},{33,97},{65,1},{97,33},{2,66}... | collective-permute-start | bytes 983048 | tf_op jit(solution)/shard_map/ppermute | solution.py:190
  151.5 9.4 %copy-start.2 = (f32[3,3,1280]{2,1,0:T(4,128)S(1)}, f32[3,3,1280]{2,1,0:T(4,128)}, u32[]{:S(2)}) copy-start(f32[3,3,1280]{2,1,0:T(4,128)} %param.8) | copy-start | bytes 138244
  151.8 14.7 %collective-permute-start.14 = (bf16[4,1,64,1280]{3,2,1,0:T(8,128)(2,1)S(1)}, bf16[4,1,64,1280]{3,2,1,0:T(8,128)(2,1)S(1)}, u32[]{:S(2)}, u32[]{:S(2)}) collective-permute-start(bf16[4,1,64,1280]{3,2,1,0:T(8,128)(2,1)S(1)} %get-tuple-element.14), channel_id=1, source_target_pairs={{0,1},{1,2},{2,3},{3,4},{4,5},{5,6},{6,7},{7,8},{8,9},{9,10},{10,1... | collective-permute-start | bytes 1966088 | tf_op jit(solution)/shard_map/ppermute | solution.py:199
  159.0 14.0 %collective-permute-start.15 = (bf16[4,1,64,1280]{3,2,1,0:T(8,128)(2,1)S(1)}, bf16[4,1,64,1280]{3,2,1,0:T(8,128)(2,1)S(1)}, u32[]{:S(2)}, u32[]{:S(2)}) collective-permute-start(bf16[4,1,64,1280]{3,2,1,0:T(8,128)(2,1)S(1)} %get-tuple-element.15), channel_id=1, source_target_pairs={{1,0},{2,1},{3,2},{4,3},{5,4},{6,5},{7,6},{8,7},{9,8},{10,9},{11,1... | collective-permute-start | bytes 1966088 | tf_op jit(solution)/shard_map/ppermute | solution.py:200
  161.1 12.3 %copy-start.3 = (f32[1280]{0:T(1024)S(1)}, f32[1280]{0:T(1024)}, u32[]{:S(2)}) copy-start(f32[1280]{0:T(1024)} %param.9) | copy-start | bytes 15364
Sparse Core Ops, SparseCore 0:
  24.5 71.6 all-gather.1

commit v2 on v1

--- a/solution.py
+++ b/solution.py
@@ -13,6 +13,7 @@
 GROUP = 8
 BF16 = jnp.bfloat16
 F32 = jnp.float32
+Z_SHIFTS = (0, 1, 3, 2)
 
 
 def dot(a, b):
@@ -48,24 +49,23 @@
     return jnp.concatenate(tiles, axis=1).astype(BF16)
 
 
-def block_kernel(head_size, *refs):
-    blocks, w_hbm, out, x_vm, w_vm, q_vm, k_vm, v_vm, att, x_sem, w_sem = (
-        refs[:8],
-        *refs[8:],
-    )
+def block_kernel(head_size, place, *refs):
+    blocks, (own_a, other_a, own_b, other_b) = refs[:8], refs[8:12]
+    out, x_vm, w_vm, q_vm, k_vm, v_vm, att, x_sem, w_sem = refs[12:]
     half = w_vm.shape[-1]
     width = 2 * half
+    core, zl = place[0], place[1]
     x_copies = [
         pltpu.make_async_copy(block, x_vm.at[i], x_sem.at[i]) for i, block in enumerate(blocks)
     ]
-    w_copies = {
-        (mat, core, col): pltpu.make_async_copy(
-            w_hbm.at[mat, col, core], w_vm.at[mat, core, :, col], w_sem.at[mat, core, col]
-        )
-        for core in range(2)
-        for mat in range(4)
-        for col in range(4)
-    }
+    w_copies = {}
+    for side, (part_a, part_b) in enumerate(((own_a, own_b), (other_a, other_b))):
+        for mat in range(4):
+            for slot, shift in enumerate(Z_SHIFTS):
+                part = part_a.at[mat, :, slot] if slot < 2 else part_b.at[:, mat, slot - 2]
+                w_copies[side, mat, slot] = pltpu.make_async_copy(
+                    part, w_vm.at[side, mat, (zl + 4 - shift) % 4], w_sem.at[side, mat, slot]
+                )
     for copy in x_copies:
         copy.start()
     for copy in w_copies.values():
@@ -73,17 +73,18 @@
     for copy in x_copies:
         copy.wait()
 
-    def wait_w(mat, core):
-        for col in range(4):
-            w_copies[mat, core, col].wait()
-
-    for core in range(2):
+    def wait_w(side, mat):
+        for slot in range(4):
+            w_copies[side, mat, slot].wait()
+
+    for side in range(2):
+        at = core if side == 0 else 1 - core
         for mat, into, count in ((0, q_vm, 4), (1, k_vm, 8), (2, v_vm, 8)):
-            wait_w(mat, core)
+            wait_w(side, mat)
 
             def project(i, _, mat=mat, into=into):
                 x = x_vm[pl.ds(i * 2, 2)].reshape(-1, width)
-                w = w_vm[mat, core].reshape(width, half)
+                w = w_vm[side, mat].reshape(width, half)
                 into[pl.ds(i * 2, 2)] = dot(x, w).astype(BF16).reshape(2, 4, -1, half)
                 return _
 
@@ -96,57 +97,85 @@
                 v_vm[:, pl.ds(group, 1)].reshape(-1, half),
                 head_size,
             )
-            att[:, pl.ds(group, 1), :, core * half : (core + 1) * half] = got.reshape(4, 1, -1, half)
+            att[pl.ds(at, 1), :, pl.ds(group, 1)] = got.reshape(1, 4, 1, -1, half)
             return _
 
         lax.fori_loop(0, 4, attend, 0)
 
-    for core in range(2):
-        wait_w(3, core)
+    for side in range(2):
+        wait_w(side, 3)
+        at = core if side == 0 else 1 - core
 
         def mix(i, _):
-            a = att[pl.ds(i * 2, 2)].reshape(-1, width)
-            w = w_vm[3, core].reshape(width, half)
-            cut = slice(core * half, (core + 1) * half)
-            x = x_vm[pl.ds(i * 2, 2), :, cut].reshape(-1, half)
-            total = dot(a, w) + x.astype(F32)
+            w = w_vm[side, 3].reshape(2, half, half)
+            total = dot(att[0, pl.ds(i * 2, 2)].reshape(-1, half), w[0])
+            total += dot(att[1, pl.ds(i * 2, 2)].reshape(-1, half), w[1])
+            cut = pl.ds(pl.multiple_of(at * half, 128), half)
+            total += x_vm[pl.ds(i * 2, 2), :, cut].reshape(-1, half).astype(F32)
             out[pl.ds(i * 2, 2), :, cut] = total.astype(BF16).reshape(2, -1, half)
             return _
 
         lax.fori_loop(0, 2, mix, 0)
 
 
-def run_block(blocks, w_all, head_size):
+def run_block(place, blocks, weights, head_size):
     rows, width = blocks[0].shape
     half = width // 2
     hbm = pl.BlockSpec(memory_space=pl.ANY)
     return pl.pallas_call(
         functools.partial(block_kernel, head_size),
         out_shape=jax.ShapeDtypeStruct((4, rows, width), BF16),
-        in_specs=[hbm] * 9,
+        in_specs=[pl.BlockSpec(memory_space=pltpu.SMEM)] + [hbm] * 12,
         out_specs=pl.BlockSpec(memory_space=pltpu.VMEM),
         scratch_shapes=[
             pltpu.VMEM((8, rows, width), BF16),
-            pltpu.VMEM((4, 2, 4, 4, width // 16, half), BF16),
+            pltpu.VMEM((2, 4, 4, 4, width // 16, half), BF16),
             pltpu.VMEM((4, 4, rows // 4, half), BF16),
             pltpu.VMEM((8, 4, rows // 4, half), BF16),
             pltpu.VMEM((8, 4, rows // 4, half), BF16),
-            pltpu.VMEM((4, 4, rows // 4, width), BF16),
+            pltpu.VMEM((2, 4, 4, rows // 4, half), BF16),
             pltpu.SemaphoreType.DMA((8,)),
-            pltpu.SemaphoreType.DMA((4, 2, 4)),
+            pltpu.SemaphoreType.DMA((2, 4, 4)),
         ],
         compiler_params=pltpu.CompilerParams(vmem_limit_bytes=48 * 1024 * 1024),
-    )(*blocks, w_all)
+    )(place, *blocks, *weights)
 
 
 def ring(count, shift):
     return [(i, (i + shift) % count) for i in range(count)]
+
+
+def put(into, piece, at):
+    return lax.dynamic_update_index_in_dim(into, piece, at, 0)
+
+
+def spread(piece, axis):
+    me = lax.axis_index(axis)
+    whole = put(jnp.zeros((4, *piece.shape), piece.dtype), piece, me)
+    for shift in (1, 3, 2):
+        whole = put(whole, lax.ppermute(piece, axis, ring(4, shift)), (me + 4 - shift) % 4)
+    return whole
+
+
+def spread_ring(piece, axis):
+    me = lax.axis_index(axis)
+    half = piece.shape[0] // 2
+    left = lax.ppermute(piece, axis, ring(4, 1))
+    right = lax.ppermute(piece, axis, ring(4, 3))
+    far_low = lax.ppermute(left[:half], axis, ring(4, 1))
+    far_high = lax.ppermute(right[half:], axis, ring(4, 3))
+    whole = put(jnp.zeros((4, *piece.shape), piece.dtype), piece, me)
+    whole = put(whole, left, (me + 3) % 4)
+    whole = put(whole, right, (me + 1) % 4)
+    zeros = (0,) * (piece.ndim - 1)
+    whole = lax.dynamic_update_slice(whole, far_low[None], ((me + 2) % 4, 0) + zeros)
+    return lax.dynamic_update_slice(whole, far_high[None], ((me + 2) % 4, half) + zeros)
 
 
 def gather_weights(w_qkv, w_out):
     rows, width = w_out.shape
     half = width // 2
-    x, zl, core = lax.axis_index("x"), lax.axis_index("zl"), lax.axis_index("c")
+    x, core = lax.axis_index("x"), lax.axis_index("c")
     joined = jnp.concatenate(
         [w_qkv.reshape(rows, 3, 2, half), w_out.reshape(rows, 1, 2, half)], axis=1
     )
@@ -154,16 +183,12 @@
     keep = lax.dynamic_index_in_dim(mine, core, 1, keepdims=False)
     give = lax.dynamic_index_in_dim(mine, 1 - core, 1, keepdims=False)
     other = lax.ppermute(give, "c", ring(2, 1))
-    piece = jnp.zeros((2, rows, half), BF16)
-    piece = lax.dynamic_update_index_in_dim(piece, keep, core, 0)
-    piece = lax.dynamic_update_index_in_dim(piece, other, 1 - core, 0).reshape(2 * rows, half)
-    planes = jnp.zeros((4, 2 * rows, half), BF16)
-    planes = lax.dynamic_update_index_in_dim(planes, piece, zl, 0)
-    for shift in (1, 7, 2):
-        got = lax.ppermute(piece, ("zh", "zl"), ring(8, shift))
-        planes = lax.dynamic_update_index_in_dim(planes, got, (zl + 8 - shift) % 4, 0)
-    gathered = lax.all_gather(planes, ("x", "y", "c"), axis=0, tiled=False)
-    return gathered.reshape(4, 4, 2, 4, 2 * rows, half)
+    piece = put(put(jnp.zeros((2, rows, half), BF16), keep, core), other, 1 - core)
+    piece = piece.reshape(2 * rows, half)
+    planes = [piece] + [lax.ppermute(piece, ("zh", "zl"), ring(8, s if s < 3 else 7)) for s in Z_SHIFTS[1:]]
+    part_a = spread_ring(spread(jnp.stack(planes[:2]), "y"), "x")
+    part_b = spread_ring(spread(jnp.stack(planes[2:]), "x"), "y")
+    return part_a, lax.ppermute(part_a, "c", ring(2, 1)), part_b, lax.ppermute(part_b, "c", ring(2, 1))
 
 
 def shards(stack, w_qkv, w_out, conv_weight, conv_bias):
@@ -180,8 +205,10 @@
     shifts = (0, 1, 3, 2)
     own = [cut(0)] + [lax.ppermute(cut(s), "x", ring(4, s)) for s in shifts[1:]]
     partner = [lax.ppermute(block, ("zh", "zl"), ring(8, 4)) for block in own]
-    w_all = gather_weights(w_qkv, w_out)
-    mixed_slots = run_block(own + partner, w_all, head_size)
+    own_a, other_a, own_b, other_b = gather_weights(w_qkv, w_out)
+    place = jnp.stack([lax.axis_index("c"), lax.axis_index("zl")]).astype(jnp.int32)
+    weights = (own_a, other_a, own_b, other_b)
+    mixed_slots = run_block(place, own + partner, weights, head_size)
 
     home = jnp.zeros((4, date_dev * part, width), BF16)
     for slot, s in enumerate(shifts):

time: 184 us -> 220 us (1.20)
  starting transfers between devices: 41.7 us -> 61.7 us
  waiting for transfers between devices: 81.9 us -> 97.8 us
  between operations: 13.7 us -> 0.34 us
  local copies, waits for them, and re-layouts: 3.8 us -> 16.5 us
    ppermute x3 -> x19, starting transfers between devices: 5.74 us -> 28.2 us  [the longest x6 6.86 us: spread(): lax.ppermute(piece, axis, ring(4, shift))]
    ppermute x3 -> x19, waiting for transfers between devices: 6.77 us -> 18.1 us  [the longest x2 7.59 us: spread_ring(): left = lax.ppermute(piece, axis, ring(4, 1))]
    dynamic_update_slice x6 -> x18, local copies, waits for them, and re-layouts: 0.11 us -> 9.34 us  [the longest x14 6.06 us: put(): return lax.dynamic_update_index_in_dim(into, piece, at, 0)]
    ppermute x3, waiting for transfers between devices: 0.16 us -> 9.17 us  [shards(): own = [cut(0)] + [lax.ppermute(cut(s), 'x', ring(4, s)) for s in shifts[1:]]]
    all_gather x1 -> x0, waiting for transfers between devices: 5.51 us -> none  [gather_weights(): gathered = lax.all_gather(planes, ('x', 'y', 'c'), axis=0, tiled=False)]
    another operation x0 -> x4, local copies, waits for them, and re-layouts: none -> 4.21 us
    ppermute x4, starting transfers between devices: 19 us -> 15.1 us  [shards(): partner = [lax.ppermute(block, ('zh', 'zl'), ring(8, 4)) for block in own]]
    ppermute x1, starting transfers between devices: 7.22 us -> 10.3 us  [shards(): lax.ppermute(band[:, -1:], axes, [(i, i + 1) for i in range(bands - 1)])]
  transfers between devices with their start and end apart: 17 -> 32, of which waited for: 14 -> 18; matrix products, arithmetic and copies ran while one was open for 0% -> 6% of each run, Pallas kernels for 0% -> 0%
where the time goes in v2:
time: 220 us
  waiting for transfers between devices  97.8 us (44%)
  starting transfers between devices  61.7 us (28%)
  Pallas kernels  38.9 us (18%)
  local copies, waits for them, and re-layouts  16.5 us (8%)
  other arithmetic  5.11 us (2%)
    ppermute x4, waiting for transfers between devices, shards(): partner = [lax.ppermute(block, ('zh', 'zl'), ring(8, 4)) for block in own]  44.5 us
    pallas_call x1, Pallas kernels, run_block(): pl.pallas_call(functools.partial(block_kernel, head_size), out_shape=jax....  38.9 us
    ppermute x4, starting transfers between devices, shards(): partner = [lax.ppermute(block, ('zh', 'zl'), ring(8, 4)) for block in own]  15.1 us
    ppermute x3, waiting for transfers between devices, shards(): back = lax.ppermute(back, 'x', ring(4, 4 - s))  13.2 us
    ppermute x1, starting transfers between devices, shards(): lax.ppermute(band[:, -1:], axes, [(i, i + 1) for i in range(bands - 1)])  10.3 us
    ppermute x3, waiting for transfers between devices, shards(): own = [cut(0)] + [lax.ppermute(cut(s), 'x', ring(4, s)) for s in shifts[1:]]  9.17 us
    ppermute x2, waiting for transfers between devices, spread_ring(): left = lax.ppermute(piece, axis, ring(4, 1))  7.59 us
    ppermute x6, starting transfers between devices, spread(): lax.ppermute(piece, axis, ring(4, shift))  6.86 us
  transfers between devices with their start and end apart: 32, of which 18 were waited for; matrix products, arithmetic and copies ran while one was open for 6% of the time, Pallas kernels for 0%

profile of v2, /device:TPU:25, one launch (start us, length us, event | category | flops | bytes accessed | tf_op | source)
XLA Modules:
  0.0 220.3 jit_solution(17602099900385602803)
XLA Ops:
  4.3 5.7 %collective-permute-start.17 = (bf16[80,640]{1,0:T(8,128)(2,1)S(1)}, bf16[80,640]{1,0:T(8,128)(2,1)S(1)}, u32[]{:S(2)}, u32[]{:S(2)}) collective-permute-start(bf16[80,640]{1,0:T(8,128)(2,1)S(1)} %bitcast.94), channel_id=1, source_target_pairs={{0,152},{8,0},{16,8},{24,16},{128,24},{136,128},{144,136},{152,144... | collective-permute-start | bytes 307208 | tf_op jit(solution)/shard_map/ppermute | solution.py:188
  11.9 4.3 %collective-permute-done.18 = bf16[80,640]{1,0:T(8,128)(2,1)S(1)} collective-permute-done((bf16[80,640]{1,0:T(8,128)(2,1)S(1)}, bf16[80,640]{1,0:T(8,128)(2,1)S(1)}, u32[]{:S(2)}, u32[]{:S(2)}) %collective-permute-start.18) | collective-permute-done | bytes 102432 | tf_op jit(solution)/shard_map/ppermute | solution.py:188
  29.3 2.5 %collective-permute-start.13 = (bf16[4,2,80,640]{3,2,1,0:T(8,128)(2,1)S(1)}, bf16[4,2,80,640]{3,2,1,0:T(8,128)(2,1)S(1)}, u32[]{:S(2)}, u32[]{:S(2)}) collective-permute-start(bf16[4,2,80,640]{3,2,1,0:T(8,128)(2,1)S(1)} %bitcast_dynamic-update-slice_fusion.17), channel_id=1, source_target_pairs={{0,96},{32,0},{64,32},{96,64},{1,97},{33,1},{65,33},{97,65},{2,98}... | collective-permute-start | bytes 2457608 | tf_op jit(solution)/shard_map/ppermute | solution.py:164
  37.9 7.6 %collective-permute-done.22 = bf16[4,2,80,640]{3,2,1,0:T(8,128)(2,1)S(1)} collective-permute-done((bf16[4,2,80,640]{3,2,1,0:T(8,128)(2,1)S(1)}, bf16[4,2,80,640]{3,2,1,0:T(8,128)(2,1)S(1)}, u32[]{:S(2)}, u32[]{:S(2)}) %collective-permute-start.22) | collective-permute-done | bytes 819232 | tf_op jit(solution)/shard_map/ppermute | solution.py:163
  45.5 3.3 %collective-permute-start.24 = (bf16[2,2,80,640]{3,2,1,0:T(8,128)(2,1)S(1)}, bf16[2,2,80,640]{3,2,1,0:T(8,128)(2,1)S(1)}, u32[]{:S(2)}, u32[]{:S(2)}) collective-permute-start(bf16[2,2,80,640]{3,2,1,0:T(8,128)(2,1)S(1)} %slice.117), channel_id=1, source_target_pairs={{0,2},{2,4},{4,6},{6,0},{1,3},{3,5},{5,7},{7,1},{8,10},{10,12},{12... | collective-permute-start | bytes 1228808 | tf_op jit(solution)/shard_map/ppermute | solution.py:165
  49.5 2.3 %collective-permute-start.15 = (bf16[2,2,80,640]{3,2,1,0:T(8,128)(2,1)S(1)}, bf16[2,2,80,640]{3,2,1,0:T(8,128)(2,1)S(1)}, u32[]{:S(2)}, u32[]{:S(2)}) collective-permute-start(bf16[2,2,80,640]{3,2,1,0:T(8,128)(2,1)S(1)} %slice.116), channel_id=1, source_target_pairs={{0,96},{32,0},{64,32},{96,64},{1,97},{33,1},{65,33},{97,65},{2,98}... | collective-permute-start | bytes 1228808 | tf_op jit(solution)/shard_map/ppermute | solution.py:166
  57.7 5.2 %collective-permute-start.26 = (bf16[4,4,2,80,640]{4,3,2,1,0:T(8,128)(2,1)}, bf16[4,4,2,80,640]{4,3,2,1,0:T(8,128)(2,1)}, u32[]{:S(2)}, u32[]{:S(2)}) collective-permute-start(bf16[4,4,2,80,640]{4,3,2,1,0:T(8,128)(2,1)} %bitcast_dynamic-update-slice_fusion.6.refs_10_), channel_id=1, source_target_pairs={{0,1},{1,0},{2,3},{3,2},{4,5},{5,4},{6,7},{7,6},{8,9},{9,8},{10,11... | collective-permute-start | bytes 9830408 | tf_op jit(solution)/shard_map/ppermute | solution.py:191
  65.1 2.5 %collective-permute-start.1 = (bf16[128,1280]{1,0:T(8,128)(2,1)S(1)}, bf16[128,1280]{1,0:T(8,128)(2,1)S(1)}, u32[]{:S(2)}, u32[]{:S(2)}) collective-permute-start(bf16[128,1280]{1,0:T(8,128)(2,1)S(1)} %bitcast.107), channel_id=1, source_target_pairs={{0,96},{32,0},{64,32},{96,64},{1,97},{33,1},{65,33},{97,65},{2,98}... | collective-permute-start | bytes 983048 | tf_op jit(solution)/shard_map/ppermute | solution.py:206
  67.9 6.9 %collective-permute-done.refs_1_ = bf16[128,1280]{1,0:T(8,128)(2,1)S(1)} collective-permute-done((bf16[128,1280]{1,0:T(8,128)(2,1)S(1)}, bf16[128,1280]{1,0:T(8,128)(2,1)S(1)}, u32[]{:S(2)}, u32[]{:S(2)}) %collective-permute-start) | collective-permute-done | bytes 327712 | tf_op jit(solution)/shard_map/ppermute | solution.py:206
  74.8 5.1 %collective-permute-start.3 = (bf16[128,1280]{1,0:T(8,128)(2,1)S(1)}, bf16[128,1280]{1,0:T(8,128)(2,1)S(1)}, u32[]{:S(2)}, u32[]{:S(2)}) collective-permute-start(bf16[128,1280]{1,0:T(8,128)(2,1)S(1)} %bitcast.88), channel_id=1, source_target_pairs={{0,128},{8,136},{16,144},{24,152},{128,0},{136,8},{144,16},{152,24... | collective-permute-start | bytes 983048 | tf_op jit(solution)/shard_map/ppermute | solution.py:207
  82.4 4.9 %collective-permute-start.5 = (bf16[128,1280]{1,0:T(8,128)(2,1)S(1)}, bf16[128,1280]{1,0:T(8,128)(2,1)S(1)}, u32[]{:S(2)}, u32[]{:S(2)}) collective-permute-start(bf16[128,1280]{1,0:T(8,128)(2,1)S(1)} %collective-permute-done.1.refs_2_), channel_id=1, source_target_pairs={{0,128},{8,136},{16,144},{24,152},{128,0},{136,8},{144,16},{152,24... | collective-permute-start | bytes 983048 | tf_op jit(solution)/shard_map/ppermute | solution.py:207
  87.3 10.3 %collective-permute-done.3.refs_4_ = bf16[128,1280]{1,0:T(8,128)(2,1)S(1)} collective-permute-done((bf16[128,1280]{1,0:T(8,128)(2,1)S(1)}, bf16[128,1280]{1,0:T(8,128)(2,1)S(1)}, u32[]{:S(2)}, u32[]{:S(2)}) %collective-permute-start.3) | collective-permute-done | bytes 327712 | tf_op jit(solution)/shard_map/ppermute | solution.py:207
  97.6 4.8 %collective-permute-start.6 = (bf16[128,1280]{1,0:T(8,128)(2,1)S(1)}, bf16[128,1280]{1,0:T(8,128)(2,1)S(1)}, u32[]{:S(2)}, u32[]{:S(2)}) collective-permute-start(bf16[128,1280]{1,0:T(8,128)(2,1)S(1)} %collective-permute-done.2.refs_3_), channel_id=1, source_target_pairs={{0,128},{8,136},{16,144},{24,152},{128,0},{136,8},{144,16},{152,24... | collective-permute-start | bytes 983048 | tf_op jit(solution)/shard_map/ppermute | solution.py:207
  102.5 15.8 %collective-permute-done.4.refs_5_ = bf16[128,1280]{1,0:T(8,128)(2,1)S(1)} collective-permute-done((bf16[128,1280]{1,0:T(8,128)(2,1)S(1)}, bf16[128,1280]{1,0:T(8,128)(2,1)S(1)}, u32[]{:S(2)}, u32[]{:S(2)}) %collective-permute-start.4) | collective-permute-done | bytes 327712 | tf_op jit(solution)/shard_map/ppermute | solution.py:207
  118.3 11.4 %collective-permute-done.5.refs_6_ = bf16[128,1280]{1,0:T(8,128)(2,1)S(1)} collective-permute-done((bf16[128,1280]{1,0:T(8,128)(2,1)S(1)}, bf16[128,1280]{1,0:T(8,128)(2,1)S(1)}, u32[]{:S(2)}, u32[]{:S(2)}) %collective-permute-start.5) | collective-permute-done | bytes 327712 | tf_op jit(solution)/shard_map/ppermute | solution.py:207
  129.7 7.0 %collective-permute-done.6.refs_7_ = bf16[128,1280]{1,0:T(8,128)(2,1)S(1)} collective-permute-done((bf16[128,1280]{1,0:T(8,128)(2,1)S(1)}, bf16[128,1280]{1,0:T(8,128)(2,1)S(1)}, u32[]{:S(2)}, u32[]{:S(2)}) %collective-permute-start.6) | collective-permute-done | bytes 327712 | tf_op jit(solution)/shard_map/ppermute | solution.py:207
  136.7 38.9 %shard_map.55 = bf16[4,128,1280]{2,1,0:T(8,128)(2,1)S(1)} custom-call(s32[2]{0:T(128)S(1)} %pad_add_fusion.place, bf16[128,1280]{1,0:T(8,128)(2,1)S(1)} %bitcast.89, bf16[128,1280]{1,0:T(8,128)(2,1)S(1)} %collective-permute-done.refs_1_, bf16[128,1280]{1,0:T(8,128)(2,1)S(1)} %collective-permute-done.1.refs_2_, ...), custom_call_target="tpu_custom_call" | custom-call | tf_op jit(solution)/shard_map/pallas_call | solution.py:125
  178.1 5.4 %collective-permute-done.27 = bf16[128,1280]{1,0:T(8,128)(2,1)S(1)} collective-permute-done((bf16[128,1280]{1,0:T(8,128)(2,1)S(1)}, bf16[128,1280]{1,0:T(8,128)(2,1)S(1)}, u32[]{:S(2)}, u32[]{:S(2)}) %collective-permute-start.27) | collective-permute-done | bytes 327712 | tf_op jit(solution)/shard_map/ppermute | solution.py:217
  183.5 3.2 %collective-permute-done.28 = bf16[128,1280]{1,0:T(8,128)(2,1)S(1)} collective-permute-done((bf16[128,1280]{1,0:T(8,128)(2,1)S(1)}, bf16[128,1280]{1,0:T(8,128)(2,1)S(1)}, u32[]{:S(2)}, u32[]{:S(2)}) %collective-permute-start.28) | collective-permute-done | bytes 327712 | tf_op jit(solution)/shard_map/ppermute | solution.py:217
  186.7 4.7 %collective-permute-done.29 = bf16[128,1280]{1,0:T(8,128)(2,1)S(1)} collective-permute-done((bf16[128,1280]{1,0:T(8,128)(2,1)S(1)}, bf16[128,1280]{1,0:T(8,128)(2,1)S(1)}, u32[]{:S(2)}, u32[]{:S(2)}) %collective-permute-start.29) | collective-permute-done | bytes 327712 | tf_op jit(solution)/shard_map/ppermute | solution.py:217
  191.7 10.3 %collective-permute-start.30 = (bf16[4,1,64,1280]{3,2,1,0:T(8,128)(2,1)S(1)}, bf16[4,1,64,1280]{3,2,1,0:T(8,128)(2,1)S(1)}, u32[]{:S(2)}, u32[]{:S(2)}) collective-permute-start(bf16[4,1,64,1280]{3,2,1,0:T(8,128)(2,1)S(1)} %get-tuple-element.14), channel_id=1, source_target_pairs={{0,1},{1,2},{2,3},{3,4},{4,5},{5,6},{6,7},{7,8},{8,9},{9,10},{10,1... | collective-permute-start | bytes 1966088 | tf_op jit(solution)/shard_map/ppermute | solution.py:226
  204.1 5.4 %collective-permute-done.30 = bf16[4,1,64,1280]{3,2,1,0:T(8,128)(2,1)S(1)} collective-permute-done((bf16[4,1,64,1280]{3,2,1,0:T(8,128)(2,1)S(1)}, bf16[4,1,64,1280]{3,2,1,0:T(8,128)(2,1)S(1)}, u32[]{:S(2)}, u32[]{:S(2)}) %collective-permute-start.30) | collective-permute-done | bytes 655392 | tf_op jit(solution)/shard_map/ppermute | solution.py:226
  209.5 6.5 %collective-permute-done.31 = bf16[4,1,64,1280]{3,2,1,0:T(8,128)(2,1)S(1)} collective-permute-done((bf16[4,1,64,1280]{3,2,1,0:T(8,128)(2,1)S(1)}, bf16[4,1,64,1280]{3,2,1,0:T(8,128)(2,1)S(1)}, u32[]{:S(2)}, u32[]{:S(2)}) %collective-permute-start.31) | collective-permute-done | bytes 655392 | tf_op jit(solution)/shard_map/ppermute | solution.py:227
  216.4 3.9 %fusion.15 = bf16[4,2,64,1280]{3,2,1,0:T(8,128)(2,1)} fusion(f32[4,4,64,1280]{3,2,1,0:T(8,128)S(1)} %maximum_convert_fusion, bf16[4,2,64,1280]{3,2,1,0:T(8,128)(2,1)S(1)} %bitcast.92, f32[1280]{0:T(1024)S(1)} %get-tuple-element.12, f32[1280]{0:T(1024)S(1)} %get-tuple-element.13, f32[1280]{0:T(1024)S(1)} %get-tuple-element.6, f32[1280]{0:T(1024)S(1)} %get-tuple-element.7, ...), kind=kLoop, calls=%fused_computation.25 | loop fusion | flops 13762560 | bytes 15810560 | tf_op jit(solution)/shard_map/convert_element_type | solution.py:238
  (98 shorter events, 42.3 us)
Async XLA Ops:
  10.0 10.5 %collective-permute-start.8 = (bf16[80,640]{1,0:T(8,128)(2,1)S(1)}, bf16[80,640]{1,0:T(8,128)(2,1)S(1)}, u32[]{:S(2)}, u32[]{:S(2)}) collective-permute-start(bf16[80,640]{1,0:T(8,128)(2,1)S(1)} %bitcast.96), channel_id=1, source_target_pairs={{0,8},{8,16},{16,24},{24,128},{128,136},{136,144},{144,152},{152,0... | collective-permute-start | bytes 307208 | tf_op jit(solution)/shard_map/ppermute | solution.py:188
  20.6 8.4 %collective-permute-start.10 = (bf16[2,80,640]{2,1,0:T(8,128)(2,1)S(1)}, bf16[2,80,640]{2,1,0:T(8,128)(2,1)S(1)}, u32[]{:S(2)}, u32[]{:S(2)}) collective-permute-start(bf16[2,80,640]{2,1,0:T(8,128)(2,1)S(1)} %pad_maximum_fusion), channel_id=1, source_target_pairs={{0,6},{2,0},{4,2},{6,4},{1,7},{3,1},{5,3},{7,5},{8,14},{10,8},{12,... | collective-permute-start | bytes 614408 | tf_op jit(solution)/shard_map/ppermute | solution.py:156
  25.4 20.1 %collective-permute-start.22 = (bf16[4,2,80,640]{3,2,1,0:T(8,128)(2,1)S(1)}, bf16[4,2,80,640]{3,2,1,0:T(8,128)(2,1)S(1)}, u32[]{:S(2)}, u32[]{:S(2)}) collective-permute-start(bf16[4,2,80,640]{3,2,1,0:T(8,128)(2,1)S(1)} %bitcast_dynamic-update-slice_fusion.13), channel_id=1, source_target_pairs={{0,2},{2,4},{4,6},{6,0},{1,3},{3,5},{5,7},{7,1},{8,10},{10,12},{12... | collective-permute-start | bytes 2457608 | tf_op jit(solution)/shard_map/ppermute | solution.py:163
  25.5 23.3 %collective-permute-start.23 = (bf16[4,2,80,640]{3,2,1,0:T(8,128)(2,1)S(1)}, bf16[4,2,80,640]{3,2,1,0:T(8,128)(2,1)S(1)}, u32[]{:S(2)}, u32[]{:S(2)}) collective-permute-start(bf16[4,2,80,640]{3,2,1,0:T(8,128)(2,1)S(1)} %bitcast_dynamic-update-slice_fusion.13), channel_id=1, source_target_pairs={{0,6},{2,0},{4,2},{6,4},{1,7},{3,1},{5,3},{7,5},{8,14},{10,8},{12,... | collective-permute-start | bytes 2457608 | tf_op jit(solution)/shard_map/ppermute | solution.py:164
  29.0 19.9 %collective-permute-start.12 = (bf16[4,2,80,640]{3,2,1,0:T(8,128)(2,1)S(1)}, bf16[4,2,80,640]{3,2,1,0:T(8,128)(2,1)S(1)}, u32[]{:S(2)}, u32[]{:S(2)}) collective-permute-start(bf16[4,2,80,640]{3,2,1,0:T(8,128)(2,1)S(1)} %bitcast_dynamic-update-slice_fusion.17), channel_id=1, source_target_pairs={{0,32},{32,64},{64,96},{96,0},{1,33},{33,65},{65,97},{97,1},{2,34}... | collective-permute-start | bytes 2457608 | tf_op jit(solution)/shard_map/ppermute | solution.py:163
  29.3 20.2 %collective-permute-start.13 = (bf16[4,2,80,640]{3,2,1,0:T(8,128)(2,1)S(1)}, bf16[4,2,80,640]{3,2,1,0:T(8,128)(2,1)S(1)}, u32[]{:S(2)}, u32[]{:S(2)}) collective-permute-start(bf16[4,2,80,640]{3,2,1,0:T(8,128)(2,1)S(1)} %bitcast_dynamic-update-slice_fusion.17), channel_id=1, source_target_pairs={{0,96},{32,0},{64,32},{96,64},{1,97},{33,1},{65,33},{97,65},{2,98}... | collective-permute-start | bytes 2457608 | tf_op jit(solution)/shard_map/ppermute | solution.py:164
  45.5 10.3 %collective-permute-start.24 = (bf16[2,2,80,640]{3,2,1,0:T(8,128)(2,1)S(1)}, bf16[2,2,80,640]{3,2,1,0:T(8,128)(2,1)S(1)}, u32[]{:S(2)}, u32[]{:S(2)}) collective-permute-start(bf16[2,2,80,640]{3,2,1,0:T(8,128)(2,1)S(1)} %slice.117), channel_id=1, source_target_pairs={{0,2},{2,4},{4,6},{6,0},{1,3},{3,5},{5,7},{7,1},{8,10},{10,12},{12... | collective-permute-start | bytes 1228808 | tf_op jit(solution)/shard_map/ppermute | solution.py:165
  48.8 8.1 %collective-permute-start.25 = (bf16[2,2,80,640]{3,2,1,0:T(8,128)(2,1)S(1)}, bf16[2,2,80,640]{3,2,1,0:T(8,128)(2,1)S(1)}, u32[]{:S(2)}, u32[]{:S(2)}) collective-permute-start(bf16[2,2,80,640]{3,2,1,0:T(8,128)(2,1)S(1)} %slice.118), channel_id=1, source_target_pairs={{0,6},{2,0},{4,2},{6,4},{1,7},{3,1},{5,3},{7,5},{8,14},{10,8},{12,... | collective-permute-start | bytes 1228808 | tf_op jit(solution)/shard_map/ppermute | solution.py:166
  49.0 13.9 %collective-permute-start.14 = (bf16[2,2,80,640]{3,2,1,0:T(8,128)(2,1)S(1)}, bf16[2,2,80,640]{3,2,1,0:T(8,128)(2,1)S(1)}, u32[]{:S(2)}, u32[]{:S(2)}) collective-permute-start(bf16[2,2,80,640]{3,2,1,0:T(8,128)(2,1)S(1)} %slice.115), channel_id=1, source_target_pairs={{0,32},{32,64},{64,96},{96,0},{1,33},{33,65},{65,97},{97,1},{2,34}... | collective-permute-start | bytes 1228808 | tf_op jit(solution)/shard_map/ppermute | solution.py:165
  49.5 14.2 %collective-permute-start.15 = (bf16[2,2,80,640]{3,2,1,0:T(8,128)(2,1)S(1)}, bf16[2,2,80,640]{3,2,1,0:T(8,128)(2,1)S(1)}, u32[]{:S(2)}, u32[]{:S(2)}) collective-permute-start(bf16[2,2,80,640]{3,2,1,0:T(8,128)(2,1)S(1)} %slice.116), channel_id=1, source_target_pairs={{0,96},{32,0},{64,32},{96,64},{1,97},{33,1},{65,33},{97,65},{2,98}... | collective-permute-start | bytes 1228808 | tf_op jit(solution)/shard_map/ppermute | solution.py:166
  57.7 79.0 %collective-permute-start.26 = (bf16[4,4,2,80,640]{4,3,2,1,0:T(8,128)(2,1)}, bf16[4,4,2,80,640]{4,3,2,1,0:T(8,128)(2,1)}, u32[]{:S(2)}, u32[]{:S(2)}) collective-permute-start(bf16[4,4,2,80,640]{4,3,2,1,0:T(8,128)(2,1)} %bitcast_dynamic-update-slice_fusion.6.refs_10_), channel_id=1, source_target_pairs={{0,1},{1,0},{2,3},{3,2},{4,5},{5,4},{6,7},{7,6},{8,9},{9,8},{10,11... | collective-permute-start | bytes 9830408 | tf_op jit(solution)/shard_map/ppermute | solution.py:191
  64.6 72.2 %collective-permute-start.16 = (bf16[4,4,2,80,640]{4,3,2,1,0:T(8,128)(2,1)}, bf16[4,4,2,80,640]{4,3,2,1,0:T(8,128)(2,1)}, u32[]{:S(2)}, u32[]{:S(2)}) collective-permute-start(bf16[4,4,2,80,640]{4,3,2,1,0:T(8,128)(2,1)} %bitcast_dynamic-update-slice_fusion.8.refs_8_), channel_id=1, source_target_pairs={{0,1},{1,0},{2,3},{3,2},{4,5},{5,4},{6,7},{7,6},{8,9},{9,8},{10,11... | collective-permute-start | bytes 9830408 | tf_op jit(solution)/shard_map/ppermute | solution.py:191
  64.7 10.1 %collective-permute-start = (bf16[128,1280]{1,0:T(8,128)(2,1)S(1)}, bf16[128,1280]{1,0:T(8,128)(2,1)S(1)}, u32[]{:S(2)}, u32[]{:S(2)}) collective-permute-start(bf16[128,1280]{1,0:T(8,128)(2,1)S(1)} %bitcast.108), channel_id=1, source_target_pairs={{0,32},{32,64},{64,96},{96,0},{1,33},{33,65},{65,97},{97,1},{2,34}... | collective-permute-start | bytes 983048 | tf_op jit(solution)/shard_map/ppermute | solution.py:206
  65.1 14.7 %collective-permute-start.1 = (bf16[128,1280]{1,0:T(8,128)(2,1)S(1)}, bf16[128,1280]{1,0:T(8,128)(2,1)S(1)}, u32[]{:S(2)}, u32[]{:S(2)}) collective-permute-start(bf16[128,1280]{1,0:T(8,128)(2,1)S(1)} %bitcast.107), channel_id=1, source_target_pairs={{0,96},{32,0},{64,32},{96,64},{1,97},{33,1},{65,33},{97,65},{2,98}... | collective-permute-start | bytes 983048 | tf_op jit(solution)/shard_map/ppermute | solution.py:206
  67.6 14.8 %collective-permute-start.2 = (bf16[128,1280]{1,0:T(8,128)(2,1)S(1)}, bf16[128,1280]{1,0:T(8,128)(2,1)S(1)}, u32[]{:S(2)}, u32[]{:S(2)}) collective-permute-start(bf16[128,1280]{1,0:T(8,128)(2,1)S(1)} %bitcast.106), channel_id=1, source_target_pairs={{0,64},{32,96},{64,0},{96,32},{1,65},{33,97},{65,1},{97,33},{2,66}... | collective-permute-start | bytes 983048 | tf_op jit(solution)/shard_map/ppermute | solution.py:206
  74.8 22.8 %collective-permute-start.3 = (bf16[128,1280]{1,0:T(8,128)(2,1)S(1)}, bf16[128,1280]{1,0:T(8,128)(2,1)S(1)}, u32[]{:S(2)}, u32[]{:S(2)}) collective-permute-start(bf16[128,1280]{1,0:T(8,128)(2,1)S(1)} %bitcast.88), channel_id=1, source_target_pairs={{0,128},{8,136},{16,144},{24,152},{128,0},{136,8},{144,16},{152,24... | collective-permute-start | bytes 983048 | tf_op jit(solution)/shard_map/ppermute | solution.py:207
  79.9 38.5 %collective-permute-start.4 = (bf16[128,1280]{1,0:T(8,128)(2,1)S(1)}, bf16[128,1280]{1,0:T(8,128)(2,1)S(1)}, u32[]{:S(2)}, u32[]{:S(2)}) collective-permute-start(bf16[128,1280]{1,0:T(8,128)(2,1)S(1)} %collective-permute-done.refs_1_), channel_id=1, source_target_pairs={{0,128},{8,136},{16,144},{24,152},{128,0},{136,8},{144,16},{152,24... | collective-permute-start | bytes 983048 | tf_op jit(solution)/shard_map/ppermute | solution.py:207
  82.4 47.3 %collective-permute-start.5 = (bf16[128,1280]{1,0:T(8,128)(2,1)S(1)}, bf16[128,1280]{1,0:T(8,128)(2,1)S(1)}, u32[]{:S(2)}, u32[]{:S(2)}) collective-permute-start(bf16[128,1280]{1,0:T(8,128)(2,1)S(1)} %collective-permute-done.1.refs_2_), channel_id=1, source_target_pairs={{0,128},{8,136},{16,144},{24,152},{128,0},{136,8},{144,16},{152,24... | collective-permute-start | bytes 983048 | tf_op jit(solution)/shard_map/ppermute | solution.py:207
  97.6 39.1 %collective-permute-start.6 = (bf16[128,1280]{1,0:T(8,128)(2,1)S(1)}, bf16[128,1280]{1,0:T(8,128)(2,1)S(1)}, u32[]{:S(2)}, u32[]{:S(2)}) collective-permute-start(bf16[128,1280]{1,0:T(8,128)(2,1)S(1)} %collective-permute-done.2.refs_3_), channel_id=1, source_target_pairs={{0,128},{8,136},{16,144},{24,152},{128,0},{136,8},{144,16},{152,24... | collective-permute-start | bytes 983048 | tf_op jit(solution)/shard_map/ppermute | solution.py:207
  175.8 7.7 %collective-permute-start.27 = (bf16[128,1280]{1,0:T(8,128)(2,1)S(1)}, bf16[128,1280]{1,0:T(8,128)(2,1)S(1)}, u32[]{:S(2)}, u32[]{:S(2)}) collective-permute-start(bf16[128,1280]{1,0:T(8,128)(2,1)S(1)} %get-tuple-element.18), channel_id=1, source_target_pairs={{0,96},{32,0},{64,32},{96,64},{1,97},{33,1},{65,33},{97,65},{2,98}... | collective-permute-start | bytes 983048 | tf_op jit(solution)/shard_map/ppermute | solution.py:217
  176.9 9.8 %collective-permute-start.28 = (bf16[128,1280]{1,0:T(8,128)(2,1)S(1)}, bf16[128,1280]{1,0:T(8,128)(2,1)S(1)}, u32[]{:S(2)}, u32[]{:S(2)}) collective-permute-start(bf16[128,1280]{1,0:T(8,128)(2,1)S(1)} %get-tuple-element.17), channel_id=1, source_target_pairs={{0,32},{32,64},{64,96},{96,0},{1,33},{33,65},{65,97},{97,1},{2,34}... | collective-permute-start | bytes 983048 | tf_op jit(solution)/shard_map/ppermute | solution.py:217
  177.3 14.1 %collective-permute-start.29 = (bf16[128,1280]{1,0:T(8,128)(2,1)S(1)}, bf16[128,1280]{1,0:T(8,128)(2,1)S(1)}, u32[]{:S(2)}, u32[]{:S(2)}) collective-permute-start(bf16[128,1280]{1,0:T(8,128)(2,1)S(1)} %get-tuple-element.16), channel_id=1, source_target_pairs={{0,64},{32,96},{64,0},{96,32},{1,65},{33,97},{65,1},{97,33},{2,66}... | collective-permute-start | bytes 983048 | tf_op jit(solution)/shard_map/ppermute | solution.py:217
  191.7 17.8 %collective-permute-start.30 = (bf16[4,1,64,1280]{3,2,1,0:T(8,128)(2,1)S(1)}, bf16[4,1,64,1280]{3,2,1,0:T(8,128)(2,1)S(1)}, u32[]{:S(2)}, u32[]{:S(2)}) collective-permute-start(bf16[4,1,64,1280]{3,2,1,0:T(8,128)(2,1)S(1)} %get-tuple-element.14), channel_id=1, source_target_pairs={{0,1},{1,2},{2,3},{3,4},{4,5},{5,6},{6,7},{7,8},{8,9},{9,10},{10,1... | collective-permute-start | bytes 1966088 | tf_op jit(solution)/shard_map/ppermute | solution.py:226
  202.0 14.0 %collective-permute-start.31 = (bf16[4,1,64,1280]{3,2,1,0:T(8,128)(2,1)S(1)}, bf16[4,1,64,1280]{3,2,1,0:T(8,128)(2,1)S(1)}, u32[]{:S(2)}, u32[]{:S(2)}) collective-permute-start(bf16[4,1,64,1280]{3,2,1,0:T(8,128)(2,1)S(1)} %get-tuple-element.15), channel_id=1, source_target_pairs={{1,0},{2,1},{3,2},{4,3},{5,4},{6,5},{7,6},{8,7},{9,8},{10,9},{11,1... | collective-permute-start | bytes 1966088 | tf_op jit(solution)/shard_map/ppermute | solution.py:227
  (11 other events, 81.6 us)

commit v3 on v1

v3 whole, which is shorter than its diff:
```python
import functools
import math

import jax
import jax.numpy as jnp
from jax import lax
from jax.experimental import pallas as pl
from jax.experimental.pallas import tpu as pltpu
from jax.sharding import Mesh
from jax.sharding import PartitionSpec as P

HEADS = 16
GROUP = 8
BF16 = jnp.bfloat16
F32 = jnp.float32


def dot(a, b):
    return jnp.dot(a, b, preferred_element_type=F32)


def attend_rows(queries, keys, values, head_size):
    width = queries.shape[1]
    rows, cols = queries.shape[0], keys.shape[0]
    scale = math.log2(math.e) / math.sqrt(head_size)
    same = (
        lax.broadcasted_iota(jnp.int32, (GROUP, cols), 0)
        == lax.broadcasted_iota(jnp.int32, (GROUP, cols), 1) % GROUP
    )
    others = jnp.where(same, 0.0, -jnp.inf)[None]
    ones = jnp.ones((cols, 128), BF16)
    tiles = [None] * (width // 128)
    head, heads = 0, width // head_size
    while head < heads:
        base = head * head_size // 128 * 128
        count = max(1, min((base + 256) // head_size, heads) - head)
        if base + 256 > width:
            base = width - 256
        lane = lax.broadcasted_iota(jnp.int32, (rows, 256), 1) + base
        query = queries[:, base : base + 256]
        stacked = jnp.concatenate(
            [
                jnp.where(
                    (lane >= h * head_size) & (lane < (h + 1) * head_size),
                    query,
                    jnp.zeros((), BF16),
                )
                for h in range(head, head + count)
            ]
        )
        scores = lax.dot_general(
            stacked,
            keys[:, base : base + 256],
            (((1,), (1,)), ((), ())),
            preferred_element_type=F32,
        )
        scores = (scores.reshape(-1, GROUP, cols) + others).reshape(-1, cols)
        top = jnp.max(scores, axis=1, keepdims=True)
        weights = jnp.exp2((scores - top) * scale).astype(BF16)
        total = 1.0 / dot(weights, ones)
        out = dot(weights, values[:, base : base + 256])
        for i, h in enumerate(range(head, head + count)):
            part = slice(i * rows, (i + 1) * rows)
            for tile in range(h * head_size // 128, -(-(h + 1) * head_size // 128)):
                at = tile * 128 - base
                got = out[part, at : at + 128] * total[part]
                if tiles[tile] is None:
                    tiles[tile] = got
                else:
                    lanes = lax.broadcasted_iota(jnp.int32, (rows, 128), 1) + tile * 128
                    tiles[tile] = jnp.where(lanes < h * head_size, tiles[tile], got)
        head += count
    return jnp.concatenate(tiles, axis=1).astype(BF16)


def block_kernel(head_size, first, *refs):
    blocks, w_hbm, out, x_vm, wp_vm, wo_vm, q_vm, k_vm, v_vm, att, x_sem, w_sem = (
        refs[:8],
        *refs[8:],
    )
    width = x_vm.shape[-1]
    half = width // 2
    rows = out.shape[1]
    groups = q_vm.shape[1]
    x_copies = [
        pltpu.make_async_copy(
            block.at[first * rows : (first + 1) * rows],
            x_vm.at[i * rows : (i + 1) * rows],
            x_sem.at[i],
        )
        for i, block in enumerate(blocks)
    ]
    w_copies = {}
    for core in range(2):
        for mat in range(4):
            lanes = slice(mat * half, (mat + 1) * half) if mat < 3 else slice(core * half, (core + 1) * half)
            for col in range(4):
                target = (wp_vm.at[core] if mat < 3 else wo_vm).at[:, col, :, lanes]
                w_copies[mat, core, col] = pltpu.make_async_copy(
                    w_hbm.at[mat, col, core], target, w_sem.at[mat, core, col]
                )
    for copy in x_copies:
        copy.start()
    for copy in w_copies.values():
        copy.start()
    for copy in x_copies:
        copy.wait()

    def wait_w(mat, core):
        for col in range(4):
            w_copies[mat, core, col].wait()

    for core in range(2):
        for mat in range(3):
            wait_w(mat, core)
        w = wp_vm[core].reshape(width, 3 * half)
        got = dot(x_vm[: 4 * rows], w).astype(BF16)
        q_vm[...] = got[:, :half].reshape(q_vm.shape)
        k_vm[:4] = got[:, half:width].reshape(q_vm.shape)
        v_vm[:4] = got[:, width:].reshape(q_vm.shape)
        got = dot(x_vm[4 * rows :], w[:, half:]).astype(BF16)
        k_vm[4:] = got[:, :half].reshape(q_vm.shape)
        v_vm[4:] = got[:, half:].reshape(q_vm.shape)

        def attend(group, _):
            got = attend_rows(
                q_vm[:, pl.ds(group, 1)].reshape(-1, half),
                k_vm[:, pl.ds(group, 1)].reshape(-1, half),
                v_vm[:, pl.ds(group, 1)].reshape(-1, half),
                head_size,
            )
            att[:, pl.ds(group, 1), :, core * half : (core + 1) * half] = got.reshape(4, 1, -1, half)
            return _

        lax.fori_loop(0, groups, attend, 0)

    wait_w(3, 0)
    wait_w(3, 1)
    total = dot(att[...].reshape(-1, width), wo_vm[...].reshape(width, width))
    total += x_vm[: 4 * rows].astype(F32)
    out[...] = total.astype(BF16).reshape(4, rows, width)


def run_block(blocks, w_all, head_size, first, parts):
    rows, width = blocks[0].shape
    half, rows, groups = width // 2, rows // parts, 4 // parts
    hbm = pl.BlockSpec(memory_space=pl.ANY)
    return pl.pallas_call(
        functools.partial(block_kernel, head_size, first),
        out_shape=jax.ShapeDtypeStruct((4, rows, width), BF16),
        in_specs=[hbm] * 9,
        out_specs=pl.BlockSpec(memory_space=pltpu.VMEM),
        scratch_shapes=[
            pltpu.VMEM((8 * rows, width), BF16),
            pltpu.VMEM((2, 4, 4, width // 16, 3 * half), BF16),
            pltpu.VMEM((4, 4, width // 16, width), BF16),
            pltpu.VMEM((4, groups, rows // groups, half), BF16),
            pltpu.VMEM((8, groups, rows // groups, half), BF16),
            pltpu.VMEM((8, groups, rows // groups, half), BF16),
            pltpu.VMEM((4, groups, rows // groups, width), BF16),
            pltpu.SemaphoreType.DMA((8,)),
            pltpu.SemaphoreType.DMA((4, 2, 4)),
        ],
        compiler_params=pltpu.CompilerParams(vmem_limit_bytes=48 * 1024 * 1024),
    )(*blocks, w_all)


def ring(count, shift):
    return [(i, (i + shift) % count) for i in range(count)]


def gather_weights(w_qkv, w_out):
    rows, width = w_out.shape
    half = width // 2
    x, zl, core = lax.axis_index("x"), lax.axis_index("zl"), lax.axis_index("c")
    joined = jnp.concatenate([w_qkv, w_out], axis=1)
    keep = lax.dynamic_slice_in_dim(joined, x * width + core * half, half, 1)
    give = lax.dynamic_slice_in_dim(joined, x * width + (1 - core) * half, half, 1)
    other = lax.ppermute(give, "c", ring(2, 1))
    piece = jnp.where(
        core == 0, jnp.concatenate([keep, other]), jnp.concatenate([other, keep])
    )
    planes = jnp.zeros((4, 2 * rows, half), BF16)
    planes = lax.dynamic_update_index_in_dim(planes, piece, zl, 0)
    for shift in (1, 7, 2):
        got = lax.ppermute(piece, ("zh", "zl"), ring(8, shift))
        planes = lax.dynamic_update_index_in_dim(planes, got, (zl + 8 - shift) % 4, 0)
    gathered = lax.all_gather(planes, ("x", "y", "c"), axis=0, tiled=False)
    return gathered.reshape(4, 4, 2, 4, 2 * rows, half)


def shards(stack, w_qkv, w_out, conv_weight, conv_bias):
    date_dev, patch_dev, width = stack.shape
    head_size = width // HEADS
    x = lax.axis_index("x")
    part = patch_dev // 4

    def cut(shift):
        block = lax.dynamic_slice_in_dim(stack, ((x + shift) % 4) * part, part, axis=1)
        block = block.reshape(date_dev, part // GROUP, GROUP, width).transpose(1, 0, 2, 3)
        return block.reshape(date_dev * part, width)

    shifts = (0, 1, 3, 2)
    own = [cut(0)] + [lax.ppermute(cut(s), "x", ring(4, s)) for s in shifts[1:]]
    partner = [lax.ppermute(block, ("zh", "zl"), ring(8, 4)) for block in own]
    w_all = gather_weights(w_qkv, w_out)
    mixed_slots = run_block(own + partner, w_all, head_size, 0, 1)

    home = jnp.zeros((4, date_dev * part, width), BF16)
    for slot, s in enumerate(shifts):
        back = mixed_slots[slot]
        if s:
            back = lax.ppermute(back, "x", ring(4, 4 - s))
        home = lax.dynamic_update_index_in_dim(home, back, (x + s) % 4, 0)
    mixed = home.reshape(4, part // GROUP, date_dev, GROUP, width).transpose(2, 0, 1, 3, 4)

    band_rows = 2
    grid_cols = patch_dev // band_rows
    band = mixed.reshape(date_dev, band_rows, grid_cols, width)
    bands = 32
    axes = ("zl", "y", "c")
    above = lax.ppermute(band[:, -1:], axes, [(i, i + 1) for i in range(bands - 1)])
    below = lax.ppermute(band[:, :1], axes, [(i + 1, i) for i in range(bands - 1)])
    widened = jnp.concatenate([above, band, below], axis=1)
    padded = jnp.pad(widened.astype(F32), ((0, 0), (0, 0), (1, 1), (0, 0)))
    result = band.astype(F32) + conv_bias
    for row_off in range(3):
        for col_off in range(3):
            result = (
                result
                + conv_weight[row_off, col_off]
                * padded[:, row_off : row_off + band_rows, col_off : col_off + grid_cols]
            )
    return result.astype(BF16).reshape(date_dev, patch_dev, width)


def solution(mesh):
    fine = Mesh(mesh.devices.reshape(2, 4, 4, 4, 2), ("zh", "x", "zl", "y", "c"))
    date, space = ("zh", "x"), ("zl", "y", "c")
    in_specs = (P(date, space, None), P(space, None), P(space, None), P(), P())
    out_specs = P(date, space, None)
    return jax.shard_map(
        shards, mesh=fine, in_specs=in_specs, out_specs=out_specs, check_vma=False
    )
```

time: 184 us -> 170 us (0.924)
  Pallas kernels: 38.1 us -> 24.2 us
    pallas_call x1, Pallas kernels: 38.1 us -> 24.2 us  [run_block(): pl.pallas_call(functools.partial(block_kernel, head_size, first), out_sha...]
    reshape x2 -> x0, local copies, waits for them, and re-layouts: 2.07 us -> none  [the longest x1 1.14 us: gather_weights(): w_qkv.reshape(rows, 3, 2, half)]
where the time goes in v3:
time: 170 us
  waiting for transfers between devices  82 us (48%)
  starting transfers between devices  41.7 us (25%)
  Pallas kernels  24.2 us (14%)
  between operations  13.7 us (8%)
  other arithmetic  4.32 us (3%)
  local copies, waits for them, and re-layouts  3.65 us (2%)
    ppermute x4, waiting for transfers between devices, shards(): partner = [lax.ppermute(block, ('zh', 'zl'), ring(8, 4)) for block in own]  42.5 us
    pallas_call x1, Pallas kernels, run_block(): pl.pallas_call(functools.partial(block_kernel, head_size, first), out_sha...  24.2 us
    ppermute x4, starting transfers between devices, shards(): partner = [lax.ppermute(block, ('zh', 'zl'), ring(8, 4)) for block in own]  19 us
    ppermute x3, waiting for transfers between devices, shards(): back = lax.ppermute(back, 'x', ring(4, 4 - s))  14.3 us
    ppermute x1, starting transfers between devices, shards(): lax.ppermute(band[:, -1:], axes, [(i, i + 1) for i in range(bands - 1)])  7.21 us
    ppermute x3, waiting for transfers between devices, gather_weights(): got = lax.ppermute(piece, ('zh', 'zl'), ring(8, shift))  6.76 us
    ppermute x1, waiting for transfers between devices, shards(): lax.ppermute(band[:, :1], axes, [(i + 1, i) for i in range(bands - 1)])  6.51 us
    ppermute x3, starting transfers between devices, gather_weights(): got = lax.ppermute(piece, ('zh', 'zl'), ring(8, shift))  5.74 us
  transfers between devices with their start and end apart: 17, of which 14 were waited for; matrix products, arithmetic and copies ran while one was open for 0% of the time, Pallas kernels for 0%

profile of v3, /device:TPU:25, one launch (start us, length us, event | category | flops | bytes accessed | tf_op | source)
XLA Modules:
  0.0 169.5 jit_solution(3521175282093020001)
XLA Ops:
  10.2 1.7 %collective-permute-start.8 = (bf16[80,640]{1,0:T(8,128)(2,1)S(1)}, bf16[80,640]{1,0:T(8,128)(2,1)S(1)}, u32[]{:S(2)}, u32[]{:S(2)}) collective-permute-start(bf16[80,640]{1,0:T(8,128)(2,1)S(1)} %maximum_select_fusion.1), channel_id=1, source_target_pairs={{0,8},{8,16},{16,24},{24,128},{128,136},{136,144},{144,152},{152,0... | collective-permute-start | bytes 307208 | tf_op jit(solution)/shard_map/ppermute | solution.py:186
  11.9 4.0 %collective-permute-start.9 = (bf16[80,640]{1,0:T(8,128)(2,1)S(1)}, bf16[80,640]{1,0:T(8,128)(2,1)S(1)}, u32[]{:S(2)}, u32[]{:S(2)}) collective-permute-start(bf16[80,640]{1,0:T(8,128)(2,1)S(1)} %maximum_select_fusion.1), channel_id=1, source_target_pairs={{0,152},{8,0},{16,8},{24,16},{128,24},{136,128},{144,136},{152,144... | collective-permute-start | bytes 307208 | tf_op jit(solution)/shard_map/ppermute | solution.py:186
  16.0 2.8 %collective-permute-done.8 = bf16[80,640]{1,0:T(8,128)(2,1)S(1)} collective-permute-done((bf16[80,640]{1,0:T(8,128)(2,1)S(1)}, bf16[80,640]{1,0:T(8,128)(2,1)S(1)}, u32[]{:S(2)}, u32[]{:S(2)}) %collective-permute-start.8) | collective-permute-done | bytes 102432 | tf_op jit(solution)/shard_map/ppermute | solution.py:186
  18.9 3.9 %collective-permute-done.10 = bf16[80,640]{1,0:T(8,128)(2,1)S(1)} collective-permute-done((bf16[80,640]{1,0:T(8,128)(2,1)S(1)}, bf16[80,640]{1,0:T(8,128)(2,1)S(1)}, u32[]{:S(2)}, u32[]{:S(2)}) %collective-permute-start.10) | collective-permute-done | bytes 102432 | tf_op jit(solution)/shard_map/ppermute | solution.py:186
  23.9 1.3 collective-permute-start
  25.2 1.5 collective-permute-start.1
  26.8 1.6 collective-permute-start.2
  28.4 5.8 %collective-permute-start.3 = (bf16[128,1280]{1,0:T(8,128)(2,1)S(1)}, bf16[128,1280]{1,0:T(8,128)(2,1)S(1)}, u32[]{:S(2)}, u32[]{:S(2)}) collective-permute-start(bf16[128,1280]{1,0:T(8,128)(2,1)S(1)} %bitcast.46), channel_id=1, source_target_pairs={{0,128},{8,136},{16,144},{24,152},{128,0},{136,8},{144,16},{152,24... | collective-permute-start | bytes 983048 | tf_op jit(solution)/shard_map/ppermute | solution.py:205
  34.2 5.4 %collective-permute-start.4 = (bf16[128,1280]{1,0:T(8,128)(2,1)S(1)}, bf16[128,1280]{1,0:T(8,128)(2,1)S(1)}, u32[]{:S(2)}, u32[]{:S(2)}) collective-permute-start(bf16[128,1280]{1,0:T(8,128)(2,1)S(1)} %collective-permute-done.refs_1_), channel_id=1, source_target_pairs={{0,128},{8,136},{16,144},{24,152},{128,0},{136,8},{144,16},{152,24... | collective-permute-start | bytes 983048 | tf_op jit(solution)/shard_map/ppermute | solution.py:205
  39.7 7.8 %collective-permute-start.6 = (bf16[128,1280]{1,0:T(8,128)(2,1)S(1)}, bf16[128,1280]{1,0:T(8,128)(2,1)S(1)}, u32[]{:S(2)}, u32[]{:S(2)}) collective-permute-start(bf16[128,1280]{1,0:T(8,128)(2,1)S(1)} %collective-permute-done.2.refs_3_), channel_id=1, source_target_pairs={{0,128},{8,136},{16,144},{24,152},{128,0},{136,8},{144,16},{152,24... | collective-permute-start | bytes 983048 | tf_op jit(solution)/shard_map/ppermute | solution.py:205
  47.5 6.8 %collective-permute-done.3.refs_4_ = bf16[128,1280]{1,0:T(8,128)(2,1)S(1)} collective-permute-done((bf16[128,1280]{1,0:T(8,128)(2,1)S(1)}, bf16[128,1280]{1,0:T(8,128)(2,1)S(1)}, u32[]{:S(2)}, u32[]{:S(2)}) %collective-permute-start.3) | collective-permute-done | bytes 327712 | tf_op jit(solution)/shard_map/ppermute | solution.py:205
  54.3 20.8 %collective-permute-done.4.refs_5_ = bf16[128,1280]{1,0:T(8,128)(2,1)S(1)} collective-permute-done((bf16[128,1280]{1,0:T(8,128)(2,1)S(1)}, bf16[128,1280]{1,0:T(8,128)(2,1)S(1)}, u32[]{:S(2)}, u32[]{:S(2)}) %collective-permute-start.4) | collective-permute-done | bytes 327712 | tf_op jit(solution)/shard_map/ppermute | solution.py:205
  75.1 7.9 %collective-permute-done.5.refs_6_ = bf16[128,1280]{1,0:T(8,128)(2,1)S(1)} collective-permute-done((bf16[128,1280]{1,0:T(8,128)(2,1)S(1)}, bf16[128,1280]{1,0:T(8,128)(2,1)S(1)}, u32[]{:S(2)}, u32[]{:S(2)}) %collective-permute-start.5) | collective-permute-done | bytes 327712 | tf_op jit(solution)/shard_map/ppermute | solution.py:205
  83.0 7.0 %collective-permute-done.6.refs_7_ = bf16[128,1280]{1,0:T(8,128)(2,1)S(1)} collective-permute-done((bf16[128,1280]{1,0:T(8,128)(2,1)S(1)}, bf16[128,1280]{1,0:T(8,128)(2,1)S(1)}, u32[]{:S(2)}, u32[]{:S(2)}) %collective-permute-start.6) | collective-permute-done | bytes 327712 | tf_op jit(solution)/shard_map/ppermute | solution.py:205
  90.0 5.5 %all-gather.2.cloned.1.call-done = bf16[32,4,80,640]{3,2,1,0:T(8,128)(2,1)} async-done(((bf16[1,4,80,640]{3,2,1,0:T(8,128)(2,1)}), bf16[32,4,80,640]{3,2,1,0:T(8,128)(2,1)}) %all-gather.2.cloned.1.call-update) | async-done | bytes 13107216 | tf_op jit(solution)/shard_map/all_gather | solution.py:188
  95.5 24.2 %shard_map.55 = bf16[4,128,1280]{2,1,0:T(8,128)(2,1)S(1)} custom-call(bf16[128,1280]{1,0:T(8,128)(2,1)S(1)} %bitcast.47, bf16[128,1280]{1,0:T(8,128)(2,1)S(1)} %collective-permute-done.refs_1_, bf16[128,1280]{1,0:T(8,128)(2,1)S(1)} %collective-permute-done.1.refs_2_, bf16[128,1280]{1,0:T(8,128)(2,1)S(1)} %collective-permute-done.2.refs_3_, ...), custom_call_target="tpu_custom_call" | custom-call | tf_op jit(solution)/shard_map/pallas_call | solution.py:148
  122.6 6.5 %collective-permute-done.11 = bf16[128,1280]{1,0:T(8,128)(2,1)S(1)} collective-permute-done((bf16[128,1280]{1,0:T(8,128)(2,1)S(1)}, bf16[128,1280]{1,0:T(8,128)(2,1)S(1)}, u32[]{:S(2)}, u32[]{:S(2)}) %collective-permute-start.11) | collective-permute-done | bytes 327712 | tf_op jit(solution)/shard_map/ppermute | solution.py:213
  129.1 2.6 %collective-permute-done.12 = bf16[128,1280]{1,0:T(8,128)(2,1)S(1)} collective-permute-done((bf16[128,1280]{1,0:T(8,128)(2,1)S(1)}, bf16[128,1280]{1,0:T(8,128)(2,1)S(1)}, u32[]{:S(2)}, u32[]{:S(2)}) %collective-permute-start.12) | collective-permute-done | bytes 327712 | tf_op jit(solution)/shard_map/ppermute | solution.py:213
  131.7 5.2 %collective-permute-done.13 = bf16[128,1280]{1,0:T(8,128)(2,1)S(1)} collective-permute-done((bf16[128,1280]{1,0:T(8,128)(2,1)S(1)}, bf16[128,1280]{1,0:T(8,128)(2,1)S(1)}, u32[]{:S(2)}, u32[]{:S(2)}) %collective-permute-start.13) | collective-permute-done | bytes 327712 | tf_op jit(solution)/shard_map/ppermute | solution.py:213
  137.2 7.2 %collective-permute-start.14 = (bf16[4,1,64,1280]{3,2,1,0:T(8,128)(2,1)S(1)}, bf16[4,1,64,1280]{3,2,1,0:T(8,128)(2,1)S(1)}, u32[]{:S(2)}, u32[]{:S(2)}) collective-permute-start(bf16[4,1,64,1280]{3,2,1,0:T(8,128)(2,1)S(1)} %get-tuple-element.14), channel_id=1, source_target_pairs={{0,1},{1,2},{2,3},{3,4},{4,5},{5,6},{6,7},{7,8},{8,9},{9,10},{10,1... | collective-permute-start | bytes 1966088 | tf_op jit(solution)/shard_map/ppermute | solution.py:222
  144.4 1.9 %collective-permute-start.15 = (bf16[4,1,64,1280]{3,2,1,0:T(8,128)(2,1)S(1)}, bf16[4,1,64,1280]{3,2,1,0:T(8,128)(2,1)S(1)}, u32[]{:S(2)}, u32[]{:S(2)}) collective-permute-start(bf16[4,1,64,1280]{3,2,1,0:T(8,128)(2,1)S(1)} %get-tuple-element.15), channel_id=1, source_target_pairs={{1,0},{2,1},{3,2},{4,3},{5,4},{6,5},{7,6},{8,7},{9,8},{10,9},{11,1... | collective-permute-start | bytes 1966088 | tf_op jit(solution)/shard_map/ppermute | solution.py:223
  146.5 5.4 %collective-permute-done.14 = bf16[4,1,64,1280]{3,2,1,0:T(8,128)(2,1)S(1)} collective-permute-done((bf16[4,1,64,1280]{3,2,1,0:T(8,128)(2,1)S(1)}, bf16[4,1,64,1280]{3,2,1,0:T(8,128)(2,1)S(1)}, u32[]{:S(2)}, u32[]{:S(2)}) %collective-permute-start.14) | collective-permute-done | bytes 655392 | tf_op jit(solution)/shard_map/ppermute | solution.py:222
  151.9 6.5 %collective-permute-done.15 = bf16[4,1,64,1280]{3,2,1,0:T(8,128)(2,1)S(1)} collective-permute-done((bf16[4,1,64,1280]{3,2,1,0:T(8,128)(2,1)S(1)}, bf16[4,1,64,1280]{3,2,1,0:T(8,128)(2,1)S(1)}, u32[]{:S(2)}, u32[]{:S(2)}) %collective-permute-start.15) | collective-permute-done | bytes 655392 | tf_op jit(solution)/shard_map/ppermute | solution.py:223
  158.8 3.9 %fusion.15 = bf16[4,2,64,1280]{3,2,1,0:T(8,128)(2,1)} fusion(f32[4,4,64,1280]{3,2,1,0:T(8,128)S(1)} %maximum_convert_fusion, bf16[4,2,64,1280]{3,2,1,0:T(8,128)(2,1)S(1)} %bitcast.50, f32[1280]{0:T(1024)S(1)} %get-tuple-element.12, f32[1280]{0:T(1024)S(1)} %get-tuple-element.13, f32[1280]{0:T(1024)S(1)} %get-tuple-element.6, f32[1280]{0:T(1024)S(1)} %get-tuple-element.7, ...), kind=kLoop, calls=%fused_computation.25 | loop fusion | flops 13762560 | bytes 15810560 | tf_op jit(solution)/shard_map/convert_element_type | solution.py:234
  (44 shorter events, 8.6 us)
Async XLA Ops:
  6.5 17.2 %copy-start.1 = (bf16[4,128,1280]{2,1,0:T(8,128)(2,1)S(1)}, bf16[4,128,1280]{2,1,0:T(8,128)(2,1)}, u32[]{:S(2)}) copy-start(bf16[4,128,1280]{2,1,0:T(8,128)(2,1)} %param.5) | copy-start | bytes 3932164
  6.5 89.0 %all-gather.2.cloned.1.call-start = ((), (), s32[]{:S(2)}) async-start(), calls=%async_computation | async-start | bytes 13516800 | tf_op jit(solution)/shard_map/all_gather | solution.py:188
  8.6 1.6 collective-permute-start.7
  10.2 8.6 %collective-permute-start.8 = (bf16[80,640]{1,0:T(8,128)(2,1)S(1)}, bf16[80,640]{1,0:T(8,128)(2,1)S(1)}, u32[]{:S(2)}, u32[]{:S(2)}) collective-permute-start(bf16[80,640]{1,0:T(8,128)(2,1)S(1)} %maximum_select_fusion.1), channel_id=1, source_target_pairs={{0,8},{8,16},{16,24},{24,128},{128,136},{136,144},{144,152},{152,0... | collective-permute-start | bytes 307208 | tf_op jit(solution)/shard_map/ppermute | solution.py:186
  11.9 6.9 %collective-permute-start.9 = (bf16[80,640]{1,0:T(8,128)(2,1)S(1)}, bf16[80,640]{1,0:T(8,128)(2,1)S(1)}, u32[]{:S(2)}, u32[]{:S(2)}) collective-permute-start(bf16[80,640]{1,0:T(8,128)(2,1)S(1)} %maximum_select_fusion.1), channel_id=1, source_target_pairs={{0,152},{8,0},{16,8},{24,16},{128,24},{136,128},{144,136},{152,144... | collective-permute-start | bytes 307208 | tf_op jit(solution)/shard_map/ppermute | solution.py:186
  16.0 6.9 %collective-permute-start.10 = (bf16[80,640]{1,0:T(8,128)(2,1)S(1)}, bf16[80,640]{1,0:T(8,128)(2,1)S(1)}, u32[]{:S(2)}, u32[]{:S(2)}) collective-permute-start(bf16[80,640]{1,0:T(8,128)(2,1)S(1)} %maximum_select_fusion.1), channel_id=1, source_target_pairs={{0,16},{8,24},{16,128},{24,136},{128,144},{136,152},{144,0},{152,8... | collective-permute-start | bytes 307208 | tf_op jit(solution)/shard_map/ppermute | solution.py:186
  22.9 0.8 copy-start
  23.9 10.3 %collective-permute-start = (bf16[128,1280]{1,0:T(8,128)(2,1)S(1)}, bf16[128,1280]{1,0:T(8,128)(2,1)S(1)}, u32[]{:S(2)}, u32[]{:S(2)}) collective-permute-start(bf16[128,1280]{1,0:T(8,128)(2,1)S(1)} %bitcast.56), channel_id=1, source_target_pairs={{0,32},{32,64},{64,96},{96,0},{1,33},{33,65},{65,97},{97,1},{2,34}... | collective-permute-start | bytes 983048 | tf_op jit(solution)/shard_map/ppermute | solution.py:204
  25.2 14.3 %collective-permute-start.1 = (bf16[128,1280]{1,0:T(8,128)(2,1)S(1)}, bf16[128,1280]{1,0:T(8,128)(2,1)S(1)}, u32[]{:S(2)}, u32[]{:S(2)}) collective-permute-start(bf16[128,1280]{1,0:T(8,128)(2,1)S(1)} %bitcast.55), channel_id=1, source_target_pairs={{0,96},{32,0},{64,32},{96,64},{1,97},{33,1},{65,33},{97,65},{2,98}... | collective-permute-start | bytes 983048 | tf_op jit(solution)/shard_map/ppermute | solution.py:204
  26.8 13.0 %collective-permute-start.2 = (bf16[128,1280]{1,0:T(8,128)(2,1)S(1)}, bf16[128,1280]{1,0:T(8,128)(2,1)S(1)}, u32[]{:S(2)}, u32[]{:S(2)}) collective-permute-start(bf16[128,1280]{1,0:T(8,128)(2,1)S(1)} %bitcast.54), channel_id=1, source_target_pairs={{0,64},{32,96},{64,0},{96,32},{1,65},{33,97},{65,1},{97,33},{2,66}... | collective-permute-start | bytes 983048 | tf_op jit(solution)/shard_map/ppermute | solution.py:204
  28.4 25.9 %collective-permute-start.3 = (bf16[128,1280]{1,0:T(8,128)(2,1)S(1)}, bf16[128,1280]{1,0:T(8,128)(2,1)S(1)}, u32[]{:S(2)}, u32[]{:S(2)}) collective-permute-start(bf16[128,1280]{1,0:T(8,128)(2,1)S(1)} %bitcast.46), channel_id=1, source_target_pairs={{0,128},{8,136},{16,144},{24,152},{128,0},{136,8},{144,16},{152,24... | collective-permute-start | bytes 983048 | tf_op jit(solution)/shard_map/ppermute | solution.py:205
  34.2 40.9 %collective-permute-start.4 = (bf16[128,1280]{1,0:T(8,128)(2,1)S(1)}, bf16[128,1280]{1,0:T(8,128)(2,1)S(1)}, u32[]{:S(2)}, u32[]{:S(2)}) collective-permute-start(bf16[128,1280]{1,0:T(8,128)(2,1)S(1)} %collective-permute-done.refs_1_), channel_id=1, source_target_pairs={{0,128},{8,136},{16,144},{24,152},{128,0},{136,8},{144,16},{152,24... | collective-permute-start | bytes 983048 | tf_op jit(solution)/shard_map/ppermute | solution.py:205
  39.5 43.5 %collective-permute-start.5 = (bf16[128,1280]{1,0:T(8,128)(2,1)S(1)}, bf16[128,1280]{1,0:T(8,128)(2,1)S(1)}, u32[]{:S(2)}, u32[]{:S(2)}) collective-permute-start(bf16[128,1280]{1,0:T(8,128)(2,1)S(1)} %collective-permute-done.1.refs_2_), channel_id=1, source_target_pairs={{0,128},{8,136},{16,144},{24,152},{128,0},{136,8},{144,16},{152,24... | collective-permute-start | bytes 983048 | tf_op jit(solution)/shard_map/ppermute | solution.py:205
  39.7 50.3 %collective-permute-start.6 = (bf16[128,1280]{1,0:T(8,128)(2,1)S(1)}, bf16[128,1280]{1,0:T(8,128)(2,1)S(1)}, u32[]{:S(2)}, u32[]{:S(2)}) collective-permute-start(bf16[128,1280]{1,0:T(8,128)(2,1)S(1)} %collective-permute-done.2.refs_3_), channel_id=1, source_target_pairs={{0,128},{8,136},{16,144},{24,152},{128,0},{136,8},{144,16},{152,24... | collective-permute-start | bytes 983048 | tf_op jit(solution)/shard_map/ppermute | solution.py:205
  119.9 9.1 %collective-permute-start.11 = (bf16[128,1280]{1,0:T(8,128)(2,1)S(1)}, bf16[128,1280]{1,0:T(8,128)(2,1)S(1)}, u32[]{:S(2)}, u32[]{:S(2)}) collective-permute-start(bf16[128,1280]{1,0:T(8,128)(2,1)S(1)} %get-tuple-element.18), channel_id=1, source_target_pairs={{0,96},{32,0},{64,32},{96,64},{1,97},{33,1},{65,33},{97,65},{2,98}... | collective-permute-start | bytes 983048 | tf_op jit(solution)/shard_map/ppermute | solution.py:213
  120.8 10.9 %collective-permute-start.12 = (bf16[128,1280]{1,0:T(8,128)(2,1)S(1)}, bf16[128,1280]{1,0:T(8,128)(2,1)S(1)}, u32[]{:S(2)}, u32[]{:S(2)}) collective-permute-start(bf16[128,1280]{1,0:T(8,128)(2,1)S(1)} %get-tuple-element.17), channel_id=1, source_target_pairs={{0,32},{32,64},{64,96},{96,0},{1,33},{33,65},{65,97},{97,1},{2,34}... | collective-permute-start | bytes 983048 | tf_op jit(solution)/shard_map/ppermute | solution.py:213
  121.5 15.5 %collective-permute-start.13 = (bf16[128,1280]{1,0:T(8,128)(2,1)S(1)}, bf16[128,1280]{1,0:T(8,128)(2,1)S(1)}, u32[]{:S(2)}, u32[]{:S(2)}) collective-permute-start(bf16[128,1280]{1,0:T(8,128)(2,1)S(1)} %get-tuple-element.16), channel_id=1, source_target_pairs={{0,64},{32,96},{64,0},{96,32},{1,65},{33,97},{65,1},{97,33},{2,66}... | collective-permute-start | bytes 983048 | tf_op jit(solution)/shard_map/ppermute | solution.py:213
  136.9 9.4 %copy-start.2 = (f32[3,3,1280]{2,1,0:T(4,128)S(1)}, f32[3,3,1280]{2,1,0:T(4,128)}, u32[]{:S(2)}) copy-start(f32[3,3,1280]{2,1,0:T(4,128)} %param.8) | copy-start | bytes 138244
  137.2 14.7 %collective-permute-start.14 = (bf16[4,1,64,1280]{3,2,1,0:T(8,128)(2,1)S(1)}, bf16[4,1,64,1280]{3,2,1,0:T(8,128)(2,1)S(1)}, u32[]{:S(2)}, u32[]{:S(2)}) collective-permute-start(bf16[4,1,64,1280]{3,2,1,0:T(8,128)(2,1)S(1)} %get-tuple-element.14), channel_id=1, source_target_pairs={{0,1},{1,2},{2,3},{3,4},{4,5},{5,6},{6,7},{7,8},{8,9},{9,10},{10,1... | collective-permute-start | bytes 1966088 | tf_op jit(solution)/shard_map/ppermute | solution.py:222
  144.4 14.0 %collective-permute-start.15 = (bf16[4,1,64,1280]{3,2,1,0:T(8,128)(2,1)S(1)}, bf16[4,1,64,1280]{3,2,1,0:T(8,128)(2,1)S(1)}, u32[]{:S(2)}, u32[]{:S(2)}) collective-permute-start(bf16[4,1,64,1280]{3,2,1,0:T(8,128)(2,1)S(1)} %get-tuple-element.15), channel_id=1, source_target_pairs={{1,0},{2,1},{3,2},{4,3},{5,4},{6,5},{7,6},{8,7},{9,8},{10,9},{11,1... | collective-permute-start | bytes 1966088 | tf_op jit(solution)/shard_map/ppermute | solution.py:223
  146.5 12.3 %copy-start.3 = (f32[1280]{0:T(1024)S(1)}, f32[1280]{0:T(1024)}, u32[]{:S(2)}) copy-start(f32[1280]{0:T(1024)} %param.9) | copy-start | bytes 15364
Sparse Core Ops, SparseCore 0:
  23.8 71.6 all-gather.1

commit v4 on v3

--- a/solution.py
+++ b/solution.py
@@ -73,100 +73,124 @@
     return jnp.concatenate(tiles, axis=1).astype(BF16)
 
 
-def block_kernel(head_size, first, *refs):
-    blocks, w_hbm, out, x_vm, wp_vm, wo_vm, q_vm, k_vm, v_vm, att, x_sem, w_sem = (
-        refs[:8],
-        *refs[8:],
-    )
-    width = x_vm.shape[-1]
+def weight_copies(w_hbm, core, target, sem):
+    half = w_hbm.shape[-1]
+    return [
+        pltpu.make_async_copy(
+            w_hbm.at[mat, row, core],
+            target.at[:, row, :, mat * half : (mat + 1) * half],
+            sem.at[mat, row],
+        )
+        for mat in range(3)
+        for row in range(4)
+    ]
+
+
+def attend_half(head_size, x_ref, w_ref, out, q_vm, k_vm, v_vm):
+    width = x_ref.shape[1]
     half = width // 2
-    rows = out.shape[1]
-    groups = q_vm.shape[1]
-    x_copies = [
-        pltpu.make_async_copy(
-            block.at[first * rows : (first + 1) * rows],
-            x_vm.at[i * rows : (i + 1) * rows],
-            x_sem.at[i],
-        )
-        for i, block in enumerate(blocks)
+    own = x_ref.shape[0] // 2
+    w = w_ref[...].reshape(width, 3 * half)
+    got = dot(x_ref[:own], w).astype(BF16)
+    q_vm[...] = got[:, :half].reshape(q_vm.shape)
+    k_vm[:4] = got[:, half:width].reshape(q_vm.shape)
+    v_vm[:4] = got[:, width:].reshape(q_vm.shape)
+    got = dot(x_ref[own:], w[:, half:]).astype(BF16)
+    k_vm[4:] = got[:, :half].reshape(q_vm.shape)
+    v_vm[4:] = got[:, half:].reshape(q_vm.shape)
+
+    def attend(group, _):
+        got = attend_rows(
+            q_vm[:, pl.ds(group, 1)].reshape(-1, half),
+            k_vm[:, pl.ds(group, 1)].reshape(-1, half),
+            v_vm[:, pl.ds(group, 1)].reshape(-1, half),
+            head_size,
+        )
+        out[:, pl.ds(group, 1)] = got.reshape(4, 1, -1, half)
+        return _
+
+    lax.fori_loop(0, 4, attend, 0)
+
+
+def first_kernel(head_size, x_ref, w_hbm, out, w_next, w_home, w_vm, q_vm, k_vm, v_vm, *sems):
+    sem, next_sem, home_sem = sems
+    half = w_hbm.shape[-1]
+    now = weight_copies(w_hbm, 0, w_vm, sem)
+    later = weight_copies(w_hbm, 1, w_next, next_sem)
+    for core in range(2):
+        for row in range(4):
+            later.append(
+                pltpu.make_async_copy(
+                    w_hbm.at[3, row, core],
+                    w_home.at[:, row, :, core * half : (core + 1) * half],
+                    home_sem.at[core, row],
+                )
+            )
+    for copy in now + later:
+        copy.start()
+    for copy in now:
+        copy.wait()
+    attend_half(head_size, x_ref, w_vm, out, q_vm, k_vm, v_vm)
+    for copy in later:
+        copy.wait()
+
+
+def second_kernel(head_size, x_ref, w_ref, out, q_vm, k_vm, v_vm):
+    attend_half(head_size, x_ref, w_ref, out, q_vm, k_vm, v_vm)
+
+
+def run_halves(x, w_all, head_size):
+    rows, width = x.shape
+    half, part = width // 2, rows // 32
+    vmem = pl.BlockSpec(memory_space=pltpu.VMEM)
+    attended = jax.ShapeDtypeStruct((4, 4, part, half), BF16)
+    columns = (4, 4, width // 16, 3 * half)
+    scratch = [
+        pltpu.VMEM((4, 4, part, half), BF16),
+        pltpu.VMEM((8, 4, part, half), BF16),
+        pltpu.VMEM((8, 4, part, half), BF16),
     ]
-    w_copies = {}
-    for core in range(2):
-        for mat in range(4):
-            lanes = slice(mat * half, (mat + 1) * half) if mat < 3 else slice(core * half, (core + 1) * half)
-            for col in range(4):
-                target = (wp_vm.at[core] if mat < 3 else wo_vm).at[:, col, :, lanes]
-                w_copies[mat, core, col] = pltpu.make_async_copy(
-                    w_hbm.at[mat, col, core], target, w_sem.at[mat, core, col]
-                )
-    for copy in x_copies:
-        copy.start()
-    for copy in w_copies.values():
-        copy.start()
-    for copy in x_copies:
-        copy.wait()
-
-    def wait_w(mat, core):
-        for col in range(4):
-            w_copies[mat, core, col].wait()
-
-    for core in range(2):
-        for mat in range(3):
-            wait_w(mat, core)
-        w = wp_vm[core].reshape(width, 3 * half)
-        got = dot(x_vm[: 4 * rows], w).astype(BF16)
-        q_vm[...] = got[:, :half].reshape(q_vm.shape)
-        k_vm[:4] = got[:, half:width].reshape(q_vm.shape)
-        v_vm[:4] = got[:, width:].reshape(q_vm.shape)
-        got = dot(x_vm[4 * rows :], w[:, half:]).astype(BF16)
-        k_vm[4:] = got[:, :half].reshape(q_vm.shape)
-        v_vm[4:] = got[:, half:].reshape(q_vm.shape)
-
-        def attend(group, _):
-            got = attend_rows(
-                q_vm[:, pl.ds(group, 1)].reshape(-1, half),
-                k_vm[:, pl.ds(group, 1)].reshape(-1, half),
-                v_vm[:, pl.ds(group, 1)].reshape(-1, half),
-                head_size,
-            )
-            att[:, pl.ds(group, 1), :, core * half : (core + 1) * half] = got.reshape(4, 1, -1, half)
-            return _
-
-        lax.fori_loop(0, groups, attend, 0)
-
-    wait_w(3, 0)
-    wait_w(3, 1)
-    total = dot(att[...].reshape(-1, width), wo_vm[...].reshape(width, width))
-    total += x_vm[: 4 * rows].astype(F32)
-    out[...] = total.astype(BF16).reshape(4, rows, width)
-
-
-def run_block(blocks, w_all, head_size, first, parts):
-    rows, width = blocks[0].shape
-    half, rows, groups = width // 2, rows // parts, 4 // parts
-    hbm = pl.BlockSpec(memory_space=pl.ANY)
-    return pl.pallas_call(
-        functools.partial(block_kernel, head_size, first),
-        out_shape=jax.ShapeDtypeStruct((4, rows, width), BF16),
-        in_specs=[hbm] * 9,
-        out_specs=pl.BlockSpec(memory_space=pltpu.VMEM),
+    params = pltpu.CompilerParams(vmem_limit_bytes=36 * 1024 * 1024)
+    cost = pl.CostEstimate(
+        flops=5 * rows * width * half, bytes_accessed=8 * width * half, transcendentals=0
+    )
+    first, w_next, w_home = pl.pallas_call(
+        functools.partial(first_kernel, head_size),
+        out_shape=(
+            attended,
+            pltpu.VMEM(columns, BF16),
+            jax.ShapeDtypeStruct((4, 4, width // 16, width), BF16),
+        ),
+        in_specs=[vmem, pl.BlockSpec(memory_space=pltpu.HBM)],
+        out_specs=(vmem, vmem, vmem),
         scratch_shapes=[
-            pltpu.VMEM((8 * rows, width), BF16),
-            pltpu.VMEM((2, 4, 4, width // 16, 3 * half), BF16),
-            pltpu.VMEM((4, 4, width // 16, width), BF16),
-            pltpu.VMEM((4, groups, rows // groups, half), BF16),
-            pltpu.VMEM((8, groups, rows // groups, half), BF16),
-            pltpu.VMEM((8, groups, rows // groups, half), BF16),
-            pltpu.VMEM((4, groups, rows // groups, width), BF16),
-            pltpu.SemaphoreType.DMA((8,)),
-            pltpu.SemaphoreType.DMA((4, 2, 4)),
+            pltpu.VMEM(columns, BF16),
+            *scratch,
+            pltpu.SemaphoreType.DMA((3, 4)),
+            pltpu.SemaphoreType.DMA((3, 4)),
+            pltpu.SemaphoreType.DMA((2, 4)),
         ],
-        compiler_params=pltpu.CompilerParams(vmem_limit_bytes=48 * 1024 * 1024),
-    )(*blocks, w_all)
+        compiler_params=params,
+        cost_estimate=cost,
+    )(x, w_all)
+    second = pl.pallas_call(
+        functools.partial(second_kernel, head_size),
+        out_shape=attended,
+        in_specs=[vmem, vmem],
+        out_specs=vmem,
+        scratch_shapes=scratch,
+        compiler_params=params,
+        cost_estimate=pl.CostEstimate(flops=1 << 20, bytes_accessed=1 << 12, transcendentals=0),
+    )(x, w_next)
+    return [first, second], w_home.reshape(width, width)
 
 
 def ring(count, shift):
     return [(i, (i + shift) % count) for i in range(count)]
+
+
+def tied(*values):
+    return lax.optimization_barrier(values)
 
 
 def gather_weights(w_qkv, w_out):
@@ -204,15 +228,25 @@
     own = [cut(0)] + [lax.ppermute(cut(s), "x", ring(4, s)) for s in shifts[1:]]
     partner = [lax.ppermute(block, ("zh", "zl"), ring(8, 4)) for block in own]
     w_all = gather_weights(w_qkv, w_out)
-    mixed_slots = run_block(own + partner, w_all, head_size, 0, 1)
-
-    home = jnp.zeros((4, date_dev * part, width), BF16)
-    for slot, s in enumerate(shifts):
-        back = mixed_slots[slot]
-        if s:
-            back = lax.ppermute(back, "x", ring(4, 4 - s))
-        home = lax.dynamic_update_index_in_dim(home, back, (x + s) % 4, 0)
-    mixed = home.reshape(4, part // GROUP, date_dev, GROUP, width).transpose(2, 0, 1, 3, 4)
+    tokens = jnp.concatenate(own + partner)
+    halves, w_home = run_halves(tokens, w_all, head_size)
+
+    whole = (4, part // GROUP, date_dev, GROUP)
+    total = stack.reshape(date_dev, *whole[:2], GROUP, width).transpose(1, 2, 0, 3, 4)
+    total = total.reshape(-1, width).astype(F32)
+    for core in range(2):
+        attended = halves[core]
+        home = jnp.zeros((4, date_dev * part, width // 2), BF16)
+        for slot, s in enumerate(shifts):
+            back = attended[slot].reshape(date_dev * part, width // 2)
+            if s:
+                back = lax.ppermute(back, "x", ring(4, 4 - s))
+            home = lax.dynamic_update_index_in_dim(home, back, (x + s) % 4, 0)
+        if core == 0:
+            home, halves[1] = tied(home, halves[1])
+        columns = slice(core * width // 2, (core + 1) * width // 2)
+        total += dot(home.reshape(-1, width // 2), w_home[columns])
+    mixed = total.astype(BF16).reshape(*whole, width).transpose(2, 0, 1, 3, 4)
 
     band_rows = 2
     grid_cols = patch_dev // band_rows

time: 170 us -> 166 us (0.976)
  waiting for transfers between devices: 82 us -> 70.7 us
  local copies, waits for them, and re-layouts: 3.65 us -> 12.5 us
  Pallas kernels: 24.2 us -> 21.4 us
  matrix products: 0 us -> 2.42 us
    ppermute x3 -> x6, waiting for transfers between devices: 14.3 us -> 4.72 us  [shards(): back = lax.ppermute(back, 'x', ring(4, 4 - s))]
    ppermute x4, starting transfers between devices: 19 us -> 13.5 us  [shards(): partner = [lax.ppermute(block, ('zh', 'zl'), ring(8, 4)) for block in own]]
    ppermute x3 -> x6, starting transfers between devices: 2.66 us -> 6.06 us  [shards(): back = lax.ppermute(back, 'x', ring(4, 4 - s))]
    unnamed x9 -> x18, local copies, waits for them, and re-layouts: 1.85 us -> 4.99 us
    convert_element_type x0 -> x1, local copies, waits for them, and re-layouts: none -> 3.09 us  [shards(): total = total.reshape(-1, width).astype(F32)]
    pallas_call x1 -> x2, Pallas kernels: 24.2 us -> 21.4 us  [the longest x1 12.1 us: run_halves(): pl.pallas_call(functools.partial(first_kernel, head_size), out_shape=(att...]
    dot_general x0 -> x2, matrix products: none -> 2.42 us  [dot(): return jnp.dot(a, b, preferred_element_type=F32)]
    transpose x5, local copies, waits for them, and re-layouts: 0.2 us -> 2.39 us  [cut(): block.reshape(date_dev, part // GROUP, GROUP, width).transpose(1, 0, 2, 3)]
  transfers between devices with their start and end apart: 17 -> 20, of which waited for: 14 -> 13; matrix products, arithmetic and copies ran while one was open for 0% -> 6% of each run, Pallas kernels for 0% -> 6%
where the time goes in v4:
time: 166 us; the launch traced here: 165 us
  waiting for transfers between devices  70.7 us (43%)
  starting transfers between devices  40.1 us (24%)
  Pallas kernels  21.4 us (13%)
  between operations  13.8 us (8%)
  local copies, waits for them, and re-layouts  12.5 us (8%)
  other arithmetic  4.32 us (3%)
  matrix products  2.42 us (1%)
    ppermute x4, waiting for transfers between devices, shards(): partner = [lax.ppermute(block, ('zh', 'zl'), ring(8, 4)) for block in own]  41.8 us
    ppermute x4, starting transfers between devices, shards(): partner = [lax.ppermute(block, ('zh', 'zl'), ring(8, 4)) for block in own]  13.5 us
    pallas_call x1, Pallas kernels, run_halves(): pl.pallas_call(functools.partial(first_kernel, head_size), out_shape=(att...  12.1 us
    pallas_call x1, Pallas kernels, run_halves(): pl.pallas_call(functools.partial(second_kernel, head_size), out_shape=att...  9.38 us
    ppermute x1, starting transfers between devices, shards(): lax.ppermute(band[:, -1:], axes, [(i, i + 1) for i in range(bands - 1)])  7.81 us
    ppermute x3, waiting for transfers between devices, gather_weights(): got = lax.ppermute(piece, ('zh', 'zl'), ring(8, shift))  6.76 us
    ppermute x1, waiting for transfers between devices, shards(): lax.ppermute(band[:, :1], axes, [(i + 1, i) for i in range(bands - 1)])  6.51 us
    ppermute x6, starting transfers between devices, shards(): back = lax.ppermute(back, 'x', ring(4, 4 - s))  6.06 us
  transfers between devices with their start and end apart: 20, of which 13 were waited for; matrix products, arithmetic and copies ran while one was open for 6% of the time, Pallas kernels for 6%

profile of v4, /device:TPU:25, one launch (start us, length us, event | category | flops | bytes accessed | tf_op | source)
XLA Modules:
  0.0 165.2 jit_solution(7033452987651138484)
XLA Ops:
  10.2 1.7 %collective-permute-start.8 = (bf16[80,640]{1,0:T(8,128)(2,1)S(1)}, bf16[80,640]{1,0:T(8,128)(2,1)S(1)}, u32[]{:S(2)}, u32[]{:S(2)}) collective-permute-start(bf16[80,640]{1,0:T(8,128)(2,1)S(1)} %maximum_select_fusion.1), channel_id=1, source_target_pairs={{0,8},{8,16},{16,24},{24,128},{128,136},{136,144},{144,152},{152,0... | collective-permute-start | bytes 307208 | tf_op jit(solution)/shard_map/ppermute | solution.py:210
  11.9 4.0 %collective-permute-start.9 = (bf16[80,640]{1,0:T(8,128)(2,1)S(1)}, bf16[80,640]{1,0:T(8,128)(2,1)S(1)}, u32[]{:S(2)}, u32[]{:S(2)}) collective-permute-start(bf16[80,640]{1,0:T(8,128)(2,1)S(1)} %maximum_select_fusion.1), channel_id=1, source_target_pairs={{0,152},{8,0},{16,8},{24,16},{128,24},{136,128},{144,136},{152,144... | collective-permute-start | bytes 307208 | tf_op jit(solution)/shard_map/ppermute | solution.py:210
  16.0 2.8 %collective-permute-done.8 = bf16[80,640]{1,0:T(8,128)(2,1)S(1)} collective-permute-done((bf16[80,640]{1,0:T(8,128)(2,1)S(1)}, bf16[80,640]{1,0:T(8,128)(2,1)S(1)}, u32[]{:S(2)}, u32[]{:S(2)}) %collective-permute-start.8) | collective-permute-done | bytes 102432 | tf_op jit(solution)/shard_map/ppermute | solution.py:210
  18.9 3.9 %collective-permute-done.10 = bf16[80,640]{1,0:T(8,128)(2,1)S(1)} collective-permute-done((bf16[80,640]{1,0:T(8,128)(2,1)S(1)}, bf16[80,640]{1,0:T(8,128)(2,1)S(1)}, u32[]{:S(2)}, u32[]{:S(2)}) %collective-permute-start.10) | collective-permute-done | bytes 102432 | tf_op jit(solution)/shard_map/ppermute | solution.py:210
  26.6 1.5 collective-permute-start.1
  28.8 1.5 collective-permute-start.2
  30.3 5.8 %collective-permute-start.3 = (bf16[128,1280]{1,0:T(8,128)(2,1)S(1)}, bf16[128,1280]{1,0:T(8,128)(2,1)}, u32[]{:S(2)}, u32[]{:S(2)}) collective-permute-start(bf16[128,1280]{1,0:T(8,128)(2,1)S(1)} %bitcast.78), channel_id=1, source_target_pairs={{0,128},{8,136},{16,144},{24,152},{128,0},{136,8},{144,16},{152,24... | collective-permute-start | bytes 983048 | tf_op jit(solution)/shard_map/ppermute | solution.py:229
  36.1 3.1 %copy.13 = f32[4,4,4,8,1280]{4,3,0,2,1:T(8,128)} copy(bf16[4,4,4,8,1280]{4,3,2,1,0:T(8,128)(2,1)} %bitcast.75) | data formatting | bytes 3932160 | tf_op jit(solution)/shard_map/convert_element_type | solution.py:236
  41.5 4.2 %collective-permute-start.5 = (bf16[128,1280]{1,0:T(8,128)(2,1)}, bf16[128,1280]{1,0:T(8,128)(2,1)S(1)}, u32[]{:S(2)}, u32[]{:S(2)}) collective-permute-start(bf16[128,1280]{1,0:T(8,128)(2,1)} %collective-permute-done.1), channel_id=1, source_target_pairs={{0,128},{8,136},{16,144},{24,152},{128,0},{136,8},{144,16},{152,24... | collective-permute-start | bytes 983048 | tf_op jit(solution)/shard_map/ppermute | solution.py:229
  46.8 2.3 %collective-permute-start.6 = (bf16[128,1280]{1,0:T(8,128)(2,1)S(1)}, bf16[128,1280]{1,0:T(8,128)(2,1)S(1)}, u32[]{:S(2)}, u32[]{:S(2)}) collective-permute-start(bf16[128,1280]{1,0:T(8,128)(2,1)S(1)} %collective-permute-done.2), channel_id=1, source_target_pairs={{0,128},{8,136},{16,144},{24,152},{128,0},{136,8},{144,16},{152,24... | collective-permute-start | bytes 983048 | tf_op jit(solution)/shard_map/ppermute | solution.py:229
  49.1 7.1 %collective-permute-done.3 = bf16[128,1280]{1,0:T(8,128)(2,1)} collective-permute-done((bf16[128,1280]{1,0:T(8,128)(2,1)S(1)}, bf16[128,1280]{1,0:T(8,128)(2,1)}, u32[]{:S(2)}, u32[]{:S(2)}) %collective-permute-start.3) | collective-permute-done | bytes 327712 | tf_op jit(solution)/shard_map/ppermute | solution.py:229
  57.3 19.9 %collective-permute-done.4 = bf16[128,1280]{1,0:T(8,128)(2,1)S(1)} collective-permute-done((bf16[128,1280]{1,0:T(8,128)(2,1)}, bf16[128,1280]{1,0:T(8,128)(2,1)S(1)}, u32[]{:S(2)}, u32[]{:S(2)}) %collective-permute-start.4) | collective-permute-done | bytes 327712 | tf_op jit(solution)/shard_map/ppermute | solution.py:229
  77.2 7.9 %collective-permute-done.5 = bf16[128,1280]{1,0:T(8,128)(2,1)S(1)} collective-permute-done((bf16[128,1280]{1,0:T(8,128)(2,1)}, bf16[128,1280]{1,0:T(8,128)(2,1)S(1)}, u32[]{:S(2)}, u32[]{:S(2)}) %collective-permute-start.5) | collective-permute-done | bytes 327712 | tf_op jit(solution)/shard_map/ppermute | solution.py:229
  85.0 6.9 %collective-permute-done.6 = bf16[128,1280]{1,0:T(8,128)(2,1)S(1)} collective-permute-done((bf16[128,1280]{1,0:T(8,128)(2,1)S(1)}, bf16[128,1280]{1,0:T(8,128)(2,1)S(1)}, u32[]{:S(2)}, u32[]{:S(2)}) %collective-permute-start.6) | collective-permute-done | bytes 327712 | tf_op jit(solution)/shard_map/ppermute | solution.py:229
  92.0 4.6 %all-gather.2.cloned.1.call-done = bf16[32,4,80,640]{3,2,1,0:T(8,128)(2,1)} async-done(((bf16[1,4,80,640]{3,2,1,0:T(8,128)(2,1)}), bf16[32,4,80,640]{3,2,1,0:T(8,128)(2,1)}) %all-gather.2.cloned.1.call-update) | async-done | bytes 13107216 | tf_op jit(solution)/shard_map/all_gather | solution.py:212
  96.6 12.1 %shard_map.55 = (bf16[4,4,32,640]{3,2,1,0:T(8,128)(2,1)S(1)}, bf16[4,4,80,1920]{3,2,1,0:T(8,128)(2,1)S(1)}, bf16[4,4,80,1280]{3,2,1,0:T(8,128)(2,1)S(1)}) custom-call(bf16[1024,1280]{1,0:T(8,128)(2,1)S(1)} %constant_dynamic-update-slice_fusion.x_ref, bf16[4,4,2,4,80,640]{5,4,3,2,1,0:T(8,128)(2,1)} %bitcast.70), custom_call_target="tpu_custom_call" | custom-call | flops 4194304000 | bytes 6553600 | tf_op jit(solution)/shard_map/pallas_call | solution.py:157
  111.6 9.4 %shard_map.56 = bf16[4,4,32,640]{3,2,1,0:T(8,128)(2,1)S(1)} custom-call(bf16[1024,1280]{1,0:T(8,128)(2,1)S(1)} %constant_dynamic-update-slice_fusion.x_ref, bf16[4,4,80,1920]{3,2,1,0:T(8,128)(2,1)S(1)} %get-tuple-element.11.w_ref), custom_call_target="tpu_custom_call" | custom-call | flops 1048576 | bytes 4096 | tf_op jit(solution)/shard_map/pallas_call | solution.py:176
  123.2 1.5 collective-permute-start.16
  126.1 3.7 %collective-permute-done.15 = bf16[128,640]{1,0:T(8,128)(2,1)S(1)} collective-permute-done((bf16[128,640]{1,0:T(8,128)(2,1)S(1)}, bf16[128,640]{1,0:T(8,128)(2,1)S(1)}, u32[]{:S(2)}, u32[]{:S(2)}) %collective-permute-start.15) | collective-permute-done | bytes 163872 | tf_op jit(solution)/shard_map/ppermute | solution.py:243
  132.3 7.8 %collective-permute-start.17 = (bf16[4,1,64,1280]{3,2,1,0:T(8,128)(2,1)S(1)}, bf16[4,1,64,1280]{3,2,1,0:T(8,128)(2,1)S(1)}, u32[]{:S(2)}, u32[]{:S(2)}) collective-permute-start(bf16[4,1,64,1280]{3,2,1,0:T(8,128)(2,1)S(1)} %get-tuple-element.26), channel_id=1, source_target_pairs={{0,1},{1,2},{2,3},{3,4},{4,5},{5,6},{6,7},{7,8},{8,9},{9,10},{10,1... | collective-permute-start | bytes 1966088 | tf_op jit(solution)/shard_map/ppermute | solution.py:256
  140.1 1.9 %collective-permute-start.18 = (bf16[4,1,64,1280]{3,2,1,0:T(8,128)(2,1)S(1)}, bf16[4,1,64,1280]{3,2,1,0:T(8,128)(2,1)S(1)}, u32[]{:S(2)}, u32[]{:S(2)}) collective-permute-start(bf16[4,1,64,1280]{3,2,1,0:T(8,128)(2,1)S(1)} %get-tuple-element.27), channel_id=1, source_target_pairs={{1,0},{2,1},{3,2},{4,3},{5,4},{6,5},{7,6},{8,7},{9,8},{10,9},{11,1... | collective-permute-start | bytes 1966088 | tf_op jit(solution)/shard_map/ppermute | solution.py:257
  142.2 5.4 %collective-permute-done.17 = bf16[4,1,64,1280]{3,2,1,0:T(8,128)(2,1)S(1)} collective-permute-done((bf16[4,1,64,1280]{3,2,1,0:T(8,128)(2,1)S(1)}, bf16[4,1,64,1280]{3,2,1,0:T(8,128)(2,1)S(1)}, u32[]{:S(2)}, u32[]{:S(2)}) %collective-permute-start.17) | collective-permute-done | bytes 655392 | tf_op jit(solution)/shard_map/ppermute | solution.py:256
  147.6 6.5 %collective-permute-done.18 = bf16[4,1,64,1280]{3,2,1,0:T(8,128)(2,1)S(1)} collective-permute-done((bf16[4,1,64,1280]{3,2,1,0:T(8,128)(2,1)S(1)}, bf16[4,1,64,1280]{3,2,1,0:T(8,128)(2,1)S(1)}, u32[]{:S(2)}, u32[]{:S(2)}) %collective-permute-start.18) | collective-permute-done | bytes 655392 | tf_op jit(solution)/shard_map/ppermute | solution.py:257
  154.5 3.9 %fusion.16 = bf16[4,2,64,1280]{3,2,1,0:T(8,128)(2,1)} fusion(f32[4,4,64,1280]{3,2,1,0:T(8,128)S(1)} %maximum_convert_fusion, bf16[4,2,64,1280]{3,2,1,0:T(8,128)(2,1)S(1)} %bitcast.69, f32[1280]{0:T(1024)S(1)} %get-tuple-element.22, f32[1280]{0:T(1024)S(1)} %get-tuple-element.23, f32[1280]{0:T(1024)S(1)} %get-tuple-element.16, ...), kind=kLoop, calls=%fused_computation.28 | loop fusion | flops 13762560 | bytes 15810560 | tf_op jit(solution)/shard_map/convert_element_type | solution.py:268
  (72 shorter events, 22.0 us)
Async XLA Ops:
  6.5 17.2 %copy-start.1 = (bf16[4,128,1280]{2,1,0:T(8,128)(2,1)S(1)}, bf16[4,128,1280]{2,1,0:T(8,128)(2,1)}, u32[]{:S(2)}) copy-start(bf16[4,128,1280]{2,1,0:T(8,128)(2,1)} %param.5) | copy-start | bytes 3932164
  6.5 90.1 %all-gather.2.cloned.1.call-start = ((), (), s32[]{:S(2)}) async-start(), calls=%async_computation | async-start | bytes 13516800 | tf_op jit(solution)/shard_map/all_gather | solution.py:212
  8.6 1.6 collective-permute-start.7
  10.2 8.6 %collective-permute-start.8 = (bf16[80,640]{1,0:T(8,128)(2,1)S(1)}, bf16[80,640]{1,0:T(8,128)(2,1)S(1)}, u32[]{:S(2)}, u32[]{:S(2)}) collective-permute-start(bf16[80,640]{1,0:T(8,128)(2,1)S(1)} %maximum_select_fusion.1), channel_id=1, source_target_pairs={{0,8},{8,16},{16,24},{24,128},{128,136},{136,144},{144,152},{152,0... | collective-permute-start | bytes 307208 | tf_op jit(solution)/shard_map/ppermute | solution.py:210
  11.9 6.9 %collective-permute-start.9 = (bf16[80,640]{1,0:T(8,128)(2,1)S(1)}, bf16[80,640]{1,0:T(8,128)(2,1)S(1)}, u32[]{:S(2)}, u32[]{:S(2)}) collective-permute-start(bf16[80,640]{1,0:T(8,128)(2,1)S(1)} %maximum_select_fusion.1), channel_id=1, source_target_pairs={{0,152},{8,0},{16,8},{24,16},{128,24},{136,128},{144,136},{152,144... | collective-permute-start | bytes 307208 | tf_op jit(solution)/shard_map/ppermute | solution.py:210
  16.0 6.9 %collective-permute-start.10 = (bf16[80,640]{1,0:T(8,128)(2,1)S(1)}, bf16[80,640]{1,0:T(8,128)(2,1)S(1)}, u32[]{:S(2)}, u32[]{:S(2)}) collective-permute-start(bf16[80,640]{1,0:T(8,128)(2,1)S(1)} %maximum_select_fusion.1), channel_id=1, source_target_pairs={{0,16},{8,24},{16,128},{24,136},{128,144},{136,152},{144,0},{152,8... | collective-permute-start | bytes 307208 | tf_op jit(solution)/shard_map/ppermute | solution.py:210
  24.6 14.6 %collective-permute-start = (bf16[128,1280]{1,0:T(8,128)(2,1)}, bf16[128,1280]{1,0:T(8,128)(2,1)}, u32[]{:S(2)}, u32[]{:S(2)}) collective-permute-start(bf16[128,1280]{1,0:T(8,128)(2,1)} %bitcast.8), channel_id=1, source_target_pairs={{0,32},{32,64},{64,96},{96,0},{1,33},{33,65},{65,97},{97,1},{2,34}... | collective-permute-start | bytes 983048 | tf_op jit(solution)/shard_map/ppermute | solution.py:228
  26.6 15.0 %collective-permute-start.1 = (bf16[128,1280]{1,0:T(8,128)(2,1)}, bf16[128,1280]{1,0:T(8,128)(2,1)}, u32[]{:S(2)}, u32[]{:S(2)}) collective-permute-start(bf16[128,1280]{1,0:T(8,128)(2,1)} %bitcast.11), channel_id=1, source_target_pairs={{0,96},{32,0},{64,32},{96,64},{1,97},{33,1},{65,33},{97,65},{2,98}... | collective-permute-start | bytes 983048 | tf_op jit(solution)/shard_map/ppermute | solution.py:228
  28.8 18.0 %collective-permute-start.2 = (bf16[128,1280]{1,0:T(8,128)(2,1)}, bf16[128,1280]{1,0:T(8,128)(2,1)S(1)}, u32[]{:S(2)}, u32[]{:S(2)}) collective-permute-start(bf16[128,1280]{1,0:T(8,128)(2,1)} %bitcast.14), channel_id=1, source_target_pairs={{0,64},{32,96},{64,0},{96,32},{1,65},{33,97},{65,1},{97,33},{2,66}... | collective-permute-start | bytes 983048 | tf_op jit(solution)/shard_map/ppermute | solution.py:228
  30.3 25.9 %collective-permute-start.3 = (bf16[128,1280]{1,0:T(8,128)(2,1)S(1)}, bf16[128,1280]{1,0:T(8,128)(2,1)}, u32[]{:S(2)}, u32[]{:S(2)}) collective-permute-start(bf16[128,1280]{1,0:T(8,128)(2,1)S(1)} %bitcast.78), channel_id=1, source_target_pairs={{0,128},{8,136},{16,144},{24,152},{128,0},{136,8},{144,16},{152,24... | collective-permute-start | bytes 983048 | tf_op jit(solution)/shard_map/ppermute | solution.py:229
  39.2 37.9 %collective-permute-start.4 = (bf16[128,1280]{1,0:T(8,128)(2,1)}, bf16[128,1280]{1,0:T(8,128)(2,1)S(1)}, u32[]{:S(2)}, u32[]{:S(2)}) collective-permute-start(bf16[128,1280]{1,0:T(8,128)(2,1)} %collective-permute-done), channel_id=1, source_target_pairs={{0,128},{8,136},{16,144},{24,152},{128,0},{136,8},{144,16},{152,24... | collective-permute-start | bytes 983048 | tf_op jit(solution)/shard_map/ppermute | solution.py:229
  41.5 43.5 %collective-permute-start.5 = (bf16[128,1280]{1,0:T(8,128)(2,1)}, bf16[128,1280]{1,0:T(8,128)(2,1)S(1)}, u32[]{:S(2)}, u32[]{:S(2)}) collective-permute-start(bf16[128,1280]{1,0:T(8,128)(2,1)} %collective-permute-done.1), channel_id=1, source_target_pairs={{0,128},{8,136},{16,144},{24,152},{128,0},{136,8},{144,16},{152,24... | collective-permute-start | bytes 983048 | tf_op jit(solution)/shard_map/ppermute | solution.py:229
  46.8 45.2 %collective-permute-start.6 = (bf16[128,1280]{1,0:T(8,128)(2,1)S(1)}, bf16[128,1280]{1,0:T(8,128)(2,1)S(1)}, u32[]{:S(2)}, u32[]{:S(2)}) collective-permute-start(bf16[128,1280]{1,0:T(8,128)(2,1)S(1)} %collective-permute-done.2), channel_id=1, source_target_pairs={{0,128},{8,136},{16,144},{24,152},{128,0},{136,8},{144,16},{152,24... | collective-permute-start | bytes 983048 | tf_op jit(solution)/shard_map/ppermute | solution.py:229
  108.7 12.4 %collective-permute-start.11 = (bf16[128,640]{1,0:T(8,128)(2,1)S(1)}, bf16[128,640]{1,0:T(8,128)(2,1)S(1)}, u32[]{:S(2)}, u32[]{:S(2)}) collective-permute-start(bf16[128,640]{1,0:T(8,128)(2,1)S(1)} %bitcast.88), channel_id=1, source_target_pairs={{0,96},{32,0},{64,32},{96,64},{1,97},{33,1},{65,33},{97,65},{2,98}... | collective-permute-start | bytes 491528 | tf_op jit(solution)/shard_map/ppermute | solution.py:243
  109.6 11.5 %collective-permute-start.12 = (bf16[128,640]{1,0:T(8,128)(2,1)S(1)}, bf16[128,640]{1,0:T(8,128)(2,1)S(1)}, u32[]{:S(2)}, u32[]{:S(2)}) collective-permute-start(bf16[128,640]{1,0:T(8,128)(2,1)S(1)} %bitcast.86), channel_id=1, source_target_pairs={{0,32},{32,64},{64,96},{96,0},{1,33},{33,65},{65,97},{97,1},{2,34}... | collective-permute-start | bytes 491528 | tf_op jit(solution)/shard_map/ppermute | solution.py:243
  110.3 10.9 %collective-permute-start.13 = (bf16[128,640]{1,0:T(8,128)(2,1)S(1)}, bf16[128,640]{1,0:T(8,128)(2,1)S(1)}, u32[]{:S(2)}, u32[]{:S(2)}) collective-permute-start(bf16[128,640]{1,0:T(8,128)(2,1)S(1)} %bitcast.84), channel_id=1, source_target_pairs={{0,64},{32,96},{64,0},{96,32},{1,65},{33,97},{65,1},{97,33},{2,66}... | collective-permute-start | bytes 491528 | tf_op jit(solution)/shard_map/ppermute | solution.py:243
  121.0 3.7 %copy-start = (f32[4,4,4,8,1280]{4,3,0,2,1:T(8,128)S(1)}, f32[4,4,4,8,1280]{4,3,0,2,1:T(8,128)}, u32[]{:S(2)}) copy-start(f32[4,4,4,8,1280]{4,3,0,2,1:T(8,128)} %copy.13) | copy-start | bytes 7864324
  121.3 4.8 %collective-permute-start.14 = (bf16[128,640]{1,0:T(8,128)(2,1)S(1)}, bf16[128,640]{1,0:T(8,128)(2,1)S(1)}, u32[]{:S(2)}, u32[]{:S(2)}) collective-permute-start(bf16[128,640]{1,0:T(8,128)(2,1)S(1)} %bitcast.89), channel_id=1, source_target_pairs={{0,96},{32,0},{64,32},{96,64},{1,97},{33,1},{65,33},{97,65},{2,98}... | collective-permute-start | bytes 491528 | tf_op jit(solution)/shard_map/ppermute | solution.py:243
  122.7 7.2 %collective-permute-start.15 = (bf16[128,640]{1,0:T(8,128)(2,1)S(1)}, bf16[128,640]{1,0:T(8,128)(2,1)S(1)}, u32[]{:S(2)}, u32[]{:S(2)}) collective-permute-start(bf16[128,640]{1,0:T(8,128)(2,1)S(1)} %bitcast.87), channel_id=1, source_target_pairs={{0,32},{32,64},{64,96},{96,0},{1,33},{33,65},{65,97},{97,1},{2,34}... | collective-permute-start | bytes 491528 | tf_op jit(solution)/shard_map/ppermute | solution.py:243
  123.2 7.6 %collective-permute-start.16 = (bf16[128,640]{1,0:T(8,128)(2,1)S(1)}, bf16[128,640]{1,0:T(8,128)(2,1)S(1)}, u32[]{:S(2)}, u32[]{:S(2)}) collective-permute-start(bf16[128,640]{1,0:T(8,128)(2,1)S(1)} %bitcast.85), channel_id=1, source_target_pairs={{0,64},{32,96},{64,0},{96,32},{1,65},{33,97},{65,1},{97,33},{2,66}... | collective-permute-start | bytes 491528 | tf_op jit(solution)/shard_map/ppermute | solution.py:243
  132.0 10.0 %copy-start.3 = (f32[3,3,1280]{2,1,0:T(4,128)S(1)}, f32[3,3,1280]{2,1,0:T(4,128)}, u32[]{:S(2)}) copy-start(f32[3,3,1280]{2,1,0:T(4,128)} %param.8) | copy-start | bytes 138244
  132.3 15.3 %collective-permute-start.17 = (bf16[4,1,64,1280]{3,2,1,0:T(8,128)(2,1)S(1)}, bf16[4,1,64,1280]{3,2,1,0:T(8,128)(2,1)S(1)}, u32[]{:S(2)}, u32[]{:S(2)}) collective-permute-start(bf16[4,1,64,1280]{3,2,1,0:T(8,128)(2,1)S(1)} %get-tuple-element.26), channel_id=1, source_target_pairs={{0,1},{1,2},{2,3},{3,4},{4,5},{5,6},{6,7},{7,8},{8,9},{9,10},{10,1... | collective-permute-start | bytes 1966088 | tf_op jit(solution)/shard_map/ppermute | solution.py:256
  140.1 14.0 %collective-permute-start.18 = (bf16[4,1,64,1280]{3,2,1,0:T(8,128)(2,1)S(1)}, bf16[4,1,64,1280]{3,2,1,0:T(8,128)(2,1)S(1)}, u32[]{:S(2)}, u32[]{:S(2)}) collective-permute-start(bf16[4,1,64,1280]{3,2,1,0:T(8,128)(2,1)S(1)} %get-tuple-element.27), channel_id=1, source_target_pairs={{1,0},{2,1},{3,2},{4,3},{5,4},{6,5},{7,6},{8,7},{9,8},{10,9},{11,1... | collective-permute-start | bytes 1966088 | tf_op jit(solution)/shard_map/ppermute | solution.py:257
  142.2 12.3 %copy-start.4 = (f32[1280]{0:T(1024)S(1)}, f32[1280]{0:T(1024)}, u32[]{:S(2)}) copy-start(f32[1280]{0:T(1024)} %param.9) | copy-start | bytes 15364
  (1 other events, 0.8 us)
Sparse Core Ops, SparseCore 0:
  23.8 72.7 all-gather.1

commit v5 on v4

--- a/solution.py
+++ b/solution.py
@@ -28,7 +28,6 @@
         == lax.broadcasted_iota(jnp.int32, (GROUP, cols), 1) % GROUP
     )
     others = jnp.where(same, 0.0, -jnp.inf)[None]
-    ones = jnp.ones((cols, 128), BF16)
     tiles = [None] * (width // 128)
     head, heads = 0, width // head_size
     while head < heads:
@@ -56,8 +55,9 @@
         )
         scores = (scores.reshape(-1, GROUP, cols) + others).reshape(-1, cols)
         top = jnp.max(scores, axis=1, keepdims=True)
-        weights = jnp.exp2((scores - top) * scale).astype(BF16)
-        total = 1.0 / dot(weights, ones)
+        weights = jnp.exp2((scores - top) * scale)
+        total = 1.0 / jnp.sum(weights, axis=1, keepdims=True)
+        weights = weights.astype(BF16)
         out = dot(weights, values[:, base : base + 256])
         for i, h in enumerate(range(head, head + count)):
             part = slice(i * rows, (i + 1) * rows)
@@ -109,7 +109,7 @@
         out[:, pl.ds(group, 1)] = got.reshape(4, 1, -1, half)
         return _
 
-    lax.fori_loop(0, 4, attend, 0)
+    lax.fori_loop(0, 4, attend, 0, unroll=4)
 
 
 def first_kernel(head_size, x_ref, w_hbm, out, w_next, w_home, w_vm, q_vm, k_vm, v_vm, *sems):
@@ -126,10 +126,12 @@
                     home_sem.at[core, row],
                 )
             )
-    for copy in now + later:
+    for copy in now:
         copy.start()
     for copy in now:
         copy.wait()
+    for copy in later:
+        copy.start()
     attend_half(head_size, x_ref, w_vm, out, q_vm, k_vm, v_vm)
     for copy in later:
         copy.wait()
@@ -197,9 +199,10 @@
     rows, width = w_out.shape
     half = width // 2
     x, zl, core = lax.axis_index("x"), lax.axis_index("zl"), lax.axis_index("c")
-    joined = jnp.concatenate([w_qkv, w_out], axis=1)
-    keep = lax.dynamic_slice_in_dim(joined, x * width + core * half, half, 1)
-    give = lax.dynamic_slice_in_dim(joined, x * width + (1 - core) * half, half, 1)
+    parts = [w_qkv[:, i * width : (i + 1) * width] for i in range(3)] + [w_out]
+    mine = lax.select_n(x, *parts)
+    keep = jnp.where(core == 0, mine[:, :half], mine[:, half:])
+    give = jnp.where(core == 0, mine[:, half:], mine[:, :half])
     other = lax.ppermute(give, "c", ring(2, 1))
     piece = jnp.where(
         core == 0, jnp.concatenate([keep, other]), jnp.concatenate([other, keep])

time: 166 us -> 161 us (0.970)
  Pallas kernels: 21.4 us -> 17.9 us
  local copies, waits for them, and re-layouts: 12.5 us -> 10.5 us
    pallas_call x1, Pallas kernels: 9.38 us -> 7.61 us  [run_halves(): pl.pallas_call(functools.partial(second_kernel, head_size), out_shape=att...]
    pallas_call x1, Pallas kernels: 12.1 us -> 10.3 us  [run_halves(): pl.pallas_call(functools.partial(first_kernel, head_size), out_shape=(att...]
    unnamed x18 -> x17, local copies, waits for them, and re-layouts: 4.99 us -> 3.9 us
  transfers between devices with their start and end apart: 20 -> 20, of which waited for: 13 -> 12; matrix products, arithmetic and copies ran while one was open for 6% -> 7% of each run, Pallas kernels for 6% -> 5%
where the time goes in v5:
time: 161 us
  waiting for transfers between devices  70.6 us (44%)
  starting transfers between devices  40.1 us (25%)
  Pallas kernels  17.9 us (11%)
  between operations  13.8 us (9%)
  local copies, waits for them, and re-layouts  10.5 us (7%)
  other arithmetic  5.45 us (3%)
  matrix products  2.42 us (2%)
    ppermute x4, waiting for transfers between devices, shards(): partner = [lax.ppermute(block, ('zh', 'zl'), ring(8, 4)) for block in own]  41.7 us
    ppermute x4, starting transfers between devices, shards(): partner = [lax.ppermute(block, ('zh', 'zl'), ring(8, 4)) for block in own]  13.6 us
    pallas_call x1, Pallas kernels, run_halves(): pl.pallas_call(functools.partial(first_kernel, head_size), out_shape=(att...  10.3 us
    ppermute x1, starting transfers between devices, shards(): lax.ppermute(band[:, -1:], axes, [(i, i + 1) for i in range(bands - 1)])  7.81 us
    pallas_call x1, Pallas kernels, run_halves(): pl.pallas_call(functools.partial(second_kernel, head_size), out_shape=att...  7.61 us
    ppermute x3, waiting for transfers between devices, gather_weights(): got = lax.ppermute(piece, ('zh', 'zl'), ring(8, shift))  6.76 us
    ppermute x1, waiting for transfers between devices, shards(): lax.ppermute(band[:, :1], axes, [(i + 1, i) for i in range(bands - 1)])  6.51 us
    ppermute x6, starting transfers between devices, shards(): back = lax.ppermute(back, 'x', ring(4, 4 - s))  6.06 us
  transfers between devices with their start and end apart: 20, of which 12 were waited for; matrix products, arithmetic and copies ran while one was open for 7% of the time, Pallas kernels for 5%

profile of v5, /device:TPU:25, one launch (start us, length us, event | category | flops | bytes accessed | tf_op | source)
XLA Modules:
  0.0 160.8 jit_solution(11030090433760380688)
XLA Ops:
  9.4 1.7 %collective-permute-start.8 = (bf16[80,640]{1,0:T(8,128)(2,1)S(1)}, bf16[80,640]{1,0:T(8,128)(2,1)S(1)}, u32[]{:S(2)}, u32[]{:S(2)}) collective-permute-start(bf16[80,640]{1,0:T(8,128)(2,1)S(1)} %maximum_select_fusion.1), channel_id=1, source_target_pairs={{0,8},{8,16},{16,24},{24,128},{128,136},{136,144},{144,152},{152,0... | collective-permute-start | bytes 307208 | tf_op jit(solution)/shard_map/ppermute | solution.py:213
  11.1 4.0 %collective-permute-start.9 = (bf16[80,640]{1,0:T(8,128)(2,1)S(1)}, bf16[80,640]{1,0:T(8,128)(2,1)S(1)}, u32[]{:S(2)}, u32[]{:S(2)}) collective-permute-start(bf16[80,640]{1,0:T(8,128)(2,1)S(1)} %maximum_select_fusion.1), channel_id=1, source_target_pairs={{0,152},{8,0},{16,8},{24,16},{128,24},{136,128},{144,136},{152,144... | collective-permute-start | bytes 307208 | tf_op jit(solution)/shard_map/ppermute | solution.py:213
  15.2 2.8 %collective-permute-done.8 = bf16[80,640]{1,0:T(8,128)(2,1)S(1)} collective-permute-done((bf16[80,640]{1,0:T(8,128)(2,1)S(1)}, bf16[80,640]{1,0:T(8,128)(2,1)S(1)}, u32[]{:S(2)}, u32[]{:S(2)}) %collective-permute-start.8) | collective-permute-done | bytes 102432 | tf_op jit(solution)/shard_map/ppermute | solution.py:213
  18.0 3.9 %collective-permute-done.10 = bf16[80,640]{1,0:T(8,128)(2,1)S(1)} collective-permute-done((bf16[80,640]{1,0:T(8,128)(2,1)S(1)}, bf16[80,640]{1,0:T(8,128)(2,1)S(1)}, u32[]{:S(2)}, u32[]{:S(2)}) %collective-permute-start.10) | collective-permute-done | bytes 102432 | tf_op jit(solution)/shard_map/ppermute | solution.py:213
  25.7 1.5 collective-permute-start.1
  27.9 1.5 collective-permute-start.2
  29.5 5.8 %collective-permute-start.3 = (bf16[128,1280]{1,0:T(8,128)(2,1)S(1)}, bf16[128,1280]{1,0:T(8,128)(2,1)}, u32[]{:S(2)}, u32[]{:S(2)}) collective-permute-start(bf16[128,1280]{1,0:T(8,128)(2,1)S(1)} %bitcast.78), channel_id=1, source_target_pairs={{0,128},{8,136},{16,144},{24,152},{128,0},{136,8},{144,16},{152,24... | collective-permute-start | bytes 983048 | tf_op jit(solution)/shard_map/ppermute | solution.py:232
  35.3 3.1 %copy.13 = f32[4,4,4,8,1280]{4,3,0,2,1:T(8,128)} copy(bf16[4,4,4,8,1280]{4,3,2,1,0:T(8,128)(2,1)} %bitcast.75) | data formatting | bytes 3932160 | tf_op jit(solution)/shard_map/convert_element_type | solution.py:239
  40.7 4.2 %collective-permute-start.5 = (bf16[128,1280]{1,0:T(8,128)(2,1)}, bf16[128,1280]{1,0:T(8,128)(2,1)S(1)}, u32[]{:S(2)}, u32[]{:S(2)}) collective-permute-start(bf16[128,1280]{1,0:T(8,128)(2,1)} %collective-permute-done.1), channel_id=1, source_target_pairs={{0,128},{8,136},{16,144},{24,152},{128,0},{136,8},{144,16},{152,24... | collective-permute-start | bytes 983048 | tf_op jit(solution)/shard_map/ppermute | solution.py:232
  45.9 2.4 %collective-permute-start.6 = (bf16[128,1280]{1,0:T(8,128)(2,1)S(1)}, bf16[128,1280]{1,0:T(8,128)(2,1)S(1)}, u32[]{:S(2)}, u32[]{:S(2)}) collective-permute-start(bf16[128,1280]{1,0:T(8,128)(2,1)S(1)} %collective-permute-done.2), channel_id=1, source_target_pairs={{0,128},{8,136},{16,144},{24,152},{128,0},{136,8},{144,16},{152,24... | collective-permute-start | bytes 983048 | tf_op jit(solution)/shard_map/ppermute | solution.py:232
  48.4 7.0 %collective-permute-done.3 = bf16[128,1280]{1,0:T(8,128)(2,1)} collective-permute-done((bf16[128,1280]{1,0:T(8,128)(2,1)S(1)}, bf16[128,1280]{1,0:T(8,128)(2,1)}, u32[]{:S(2)}, u32[]{:S(2)}) %collective-permute-start.3) | collective-permute-done | bytes 327712 | tf_op jit(solution)/shard_map/ppermute | solution.py:232
  56.4 19.9 %collective-permute-done.4 = bf16[128,1280]{1,0:T(8,128)(2,1)S(1)} collective-permute-done((bf16[128,1280]{1,0:T(8,128)(2,1)}, bf16[128,1280]{1,0:T(8,128)(2,1)S(1)}, u32[]{:S(2)}, u32[]{:S(2)}) %collective-permute-start.4) | collective-permute-done | bytes 327712 | tf_op jit(solution)/shard_map/ppermute | solution.py:232
  76.3 7.9 %collective-permute-done.5 = bf16[128,1280]{1,0:T(8,128)(2,1)S(1)} collective-permute-done((bf16[128,1280]{1,0:T(8,128)(2,1)}, bf16[128,1280]{1,0:T(8,128)(2,1)S(1)}, u32[]{:S(2)}, u32[]{:S(2)}) %collective-permute-start.5) | collective-permute-done | bytes 327712 | tf_op jit(solution)/shard_map/ppermute | solution.py:232
  84.2 6.9 %collective-permute-done.6 = bf16[128,1280]{1,0:T(8,128)(2,1)S(1)} collective-permute-done((bf16[128,1280]{1,0:T(8,128)(2,1)S(1)}, bf16[128,1280]{1,0:T(8,128)(2,1)S(1)}, u32[]{:S(2)}, u32[]{:S(2)}) %collective-permute-start.6) | collective-permute-done | bytes 327712 | tf_op jit(solution)/shard_map/ppermute | solution.py:232
  91.1 4.6 %all-gather.2.cloned.1.call-done = bf16[32,4,80,640]{3,2,1,0:T(8,128)(2,1)} async-done(((bf16[1,4,80,640]{3,2,1,0:T(8,128)(2,1)}), bf16[32,4,80,640]{3,2,1,0:T(8,128)(2,1)}) %all-gather.2.cloned.1.call-update) | async-done | bytes 13107216 | tf_op jit(solution)/shard_map/all_gather | solution.py:215
  95.7 10.3 %shard_map.55 = (bf16[4,4,32,640]{3,2,1,0:T(8,128)(2,1)S(1)}, bf16[4,4,80,1920]{3,2,1,0:T(8,128)(2,1)S(1)}, bf16[4,4,80,1280]{3,2,1,0:T(8,128)(2,1)S(1)}) custom-call(bf16[1024,1280]{1,0:T(8,128)(2,1)S(1)} %constant_dynamic-update-slice_fusion.x_ref, bf16[4,4,2,4,80,640]{5,4,3,2,1,0:T(8,128)(2,1)} %bitcast.70), custom_call_target="tpu_custom_call" | custom-call | flops 4194304000 | bytes 6553600 | tf_op jit(solution)/shard_map/pallas_call | solution.py:159
  109.0 7.6 %shard_map.56 = bf16[4,4,32,640]{3,2,1,0:T(8,128)(2,1)S(1)} custom-call(bf16[1024,1280]{1,0:T(8,128)(2,1)S(1)} %constant_dynamic-update-slice_fusion.x_ref, bf16[4,4,80,1920]{3,2,1,0:T(8,128)(2,1)S(1)} %get-tuple-element.11.w_ref), custom_call_target="tpu_custom_call" | custom-call | flops 1048576 | bytes 4096 | tf_op jit(solution)/shard_map/pallas_call | solution.py:178
  118.6 1.7 %collective-permute-start.16 = (bf16[128,640]{1,0:T(8,128)(2,1)S(1)}, bf16[128,640]{1,0:T(8,128)(2,1)S(1)}, u32[]{:S(2)}, u32[]{:S(2)}) collective-permute-start(bf16[128,640]{1,0:T(8,128)(2,1)S(1)} %bitcast.85), channel_id=1, source_target_pairs={{0,64},{32,96},{64,0},{96,32},{1,65},{33,97},{65,1},{97,33},{2,66}... | collective-permute-start | bytes 491528 | tf_op jit(solution)/shard_map/ppermute | solution.py:246
  121.7 3.8 %collective-permute-done.15 = bf16[128,640]{1,0:T(8,128)(2,1)S(1)} collective-permute-done((bf16[128,640]{1,0:T(8,128)(2,1)S(1)}, bf16[128,640]{1,0:T(8,128)(2,1)S(1)}, u32[]{:S(2)}, u32[]{:S(2)}) %collective-permute-start.15) | collective-permute-done | bytes 163872 | tf_op jit(solution)/shard_map/ppermute | solution.py:246
  127.9 7.8 %collective-permute-start.17 = (bf16[4,1,64,1280]{3,2,1,0:T(8,128)(2,1)S(1)}, bf16[4,1,64,1280]{3,2,1,0:T(8,128)(2,1)S(1)}, u32[]{:S(2)}, u32[]{:S(2)}) collective-permute-start(bf16[4,1,64,1280]{3,2,1,0:T(8,128)(2,1)S(1)} %get-tuple-element.26), channel_id=1, source_target_pairs={{0,1},{1,2},{2,3},{3,4},{4,5},{5,6},{6,7},{7,8},{8,9},{9,10},{10,1... | collective-permute-start | bytes 1966088 | tf_op jit(solution)/shard_map/ppermute | solution.py:259
  135.7 1.9 %collective-permute-start.18 = (bf16[4,1,64,1280]{3,2,1,0:T(8,128)(2,1)S(1)}, bf16[4,1,64,1280]{3,2,1,0:T(8,128)(2,1)S(1)}, u32[]{:S(2)}, u32[]{:S(2)}) collective-permute-start(bf16[4,1,64,1280]{3,2,1,0:T(8,128)(2,1)S(1)} %get-tuple-element.27), channel_id=1, source_target_pairs={{1,0},{2,1},{3,2},{4,3},{5,4},{6,5},{7,6},{8,7},{9,8},{10,9},{11,1... | collective-permute-start | bytes 1966088 | tf_op jit(solution)/shard_map/ppermute | solution.py:260
  137.8 5.4 %collective-permute-done.17 = bf16[4,1,64,1280]{3,2,1,0:T(8,128)(2,1)S(1)} collective-permute-done((bf16[4,1,64,1280]{3,2,1,0:T(8,128)(2,1)S(1)}, bf16[4,1,64,1280]{3,2,1,0:T(8,128)(2,1)S(1)}, u32[]{:S(2)}, u32[]{:S(2)}) %collective-permute-start.17) | collective-permute-done | bytes 655392 | tf_op jit(solution)/shard_map/ppermute | solution.py:259
  143.2 6.5 %collective-permute-done.18 = bf16[4,1,64,1280]{3,2,1,0:T(8,128)(2,1)S(1)} collective-permute-done((bf16[4,1,64,1280]{3,2,1,0:T(8,128)(2,1)S(1)}, bf16[4,1,64,1280]{3,2,1,0:T(8,128)(2,1)S(1)}, u32[]{:S(2)}, u32[]{:S(2)}) %collective-permute-start.18) | collective-permute-done | bytes 655392 | tf_op jit(solution)/shard_map/ppermute | solution.py:260
  150.1 3.9 %fusion.16 = bf16[4,2,64,1280]{3,2,1,0:T(8,128)(2,1)} fusion(f32[4,4,64,1280]{3,2,1,0:T(8,128)S(1)} %maximum_convert_fusion, bf16[4,2,64,1280]{3,2,1,0:T(8,128)(2,1)S(1)} %bitcast.69, f32[1280]{0:T(1024)S(1)} %get-tuple-element.22, f32[1280]{0:T(1024)S(1)} %get-tuple-element.23, f32[1280]{0:T(1024)S(1)} %get-tuple-element.16, ...), kind=kLoop, calls=%fused_computation.28 | loop fusion | flops 13762560 | bytes 15810560 | tf_op jit(solution)/shard_map/convert_element_type | solution.py:271
  (71 shorter events, 20.8 us)
Async XLA Ops:
  6.5 16.3 %copy-start.1 = (bf16[4,128,1280]{2,1,0:T(8,128)(2,1)S(1)}, bf16[4,128,1280]{2,1,0:T(8,128)(2,1)}, u32[]{:S(2)}) copy-start(bf16[4,128,1280]{2,1,0:T(8,128)(2,1)} %param.5) | copy-start | bytes 3932164
  6.5 89.2 %all-gather.2.cloned.1.call-start = ((), (), s32[]{:S(2)}) async-start(), calls=%async_computation | async-start | bytes 13516800 | tf_op jit(solution)/shard_map/all_gather | solution.py:215
  7.7 1.6 %collective-permute-start.7 = (bf16[40,640]{1,0:T(8,128)(2,1)S(1)}, bf16[40,640]{1,0:T(8,128)(2,1)S(1)}, u32[]{:S(2)}, u32[]{:S(2)}) collective-permute-start(bf16[40,640]{1,0:T(8,128)(2,1)S(1)} %get-tuple-element.41), channel_id=1, source_target_pairs={{0,1},{1,0},{2,3},{3,2},{4,5},{5,4},{6,7},{7,6},{8,9},{9,8},{10,11... | collective-permute-start | bytes 153608 | tf_op jit(solution)/shard_map/ppermute | solution.py:206
  9.4 8.6 %collective-permute-start.8 = (bf16[80,640]{1,0:T(8,128)(2,1)S(1)}, bf16[80,640]{1,0:T(8,128)(2,1)S(1)}, u32[]{:S(2)}, u32[]{:S(2)}) collective-permute-start(bf16[80,640]{1,0:T(8,128)(2,1)S(1)} %maximum_select_fusion.1), channel_id=1, source_target_pairs={{0,8},{8,16},{16,24},{24,128},{128,136},{136,144},{144,152},{152,0... | collective-permute-start | bytes 307208 | tf_op jit(solution)/shard_map/ppermute | solution.py:213
  11.1 6.9 %collective-permute-start.9 = (bf16[80,640]{1,0:T(8,128)(2,1)S(1)}, bf16[80,640]{1,0:T(8,128)(2,1)S(1)}, u32[]{:S(2)}, u32[]{:S(2)}) collective-permute-start(bf16[80,640]{1,0:T(8,128)(2,1)S(1)} %maximum_select_fusion.1), channel_id=1, source_target_pairs={{0,152},{8,0},{16,8},{24,16},{128,24},{136,128},{144,136},{152,144... | collective-permute-start | bytes 307208 | tf_op jit(solution)/shard_map/ppermute | solution.py:213
  15.1 6.9 %collective-permute-start.10 = (bf16[80,640]{1,0:T(8,128)(2,1)S(1)}, bf16[80,640]{1,0:T(8,128)(2,1)S(1)}, u32[]{:S(2)}, u32[]{:S(2)}) collective-permute-start(bf16[80,640]{1,0:T(8,128)(2,1)S(1)} %maximum_select_fusion.1), channel_id=1, source_target_pairs={{0,16},{8,24},{16,128},{24,136},{128,144},{136,152},{144,0},{152,8... | collective-permute-start | bytes 307208 | tf_op jit(solution)/shard_map/ppermute | solution.py:213
  23.7 14.6 %collective-permute-start = (bf16[128,1280]{1,0:T(8,128)(2,1)}, bf16[128,1280]{1,0:T(8,128)(2,1)}, u32[]{:S(2)}, u32[]{:S(2)}) collective-permute-start(bf16[128,1280]{1,0:T(8,128)(2,1)} %bitcast.8), channel_id=1, source_target_pairs={{0,32},{32,64},{64,96},{96,0},{1,33},{33,65},{65,97},{97,1},{2,34}... | collective-permute-start | bytes 983048 | tf_op jit(solution)/shard_map/ppermute | solution.py:231
  25.7 15.0 %collective-permute-start.1 = (bf16[128,1280]{1,0:T(8,128)(2,1)}, bf16[128,1280]{1,0:T(8,128)(2,1)}, u32[]{:S(2)}, u32[]{:S(2)}) collective-permute-start(bf16[128,1280]{1,0:T(8,128)(2,1)} %bitcast.11), channel_id=1, source_target_pairs={{0,96},{32,0},{64,32},{96,64},{1,97},{33,1},{65,33},{97,65},{2,98}... | collective-permute-start | bytes 983048 | tf_op jit(solution)/shard_map/ppermute | solution.py:231
  27.9 18.0 %collective-permute-start.2 = (bf16[128,1280]{1,0:T(8,128)(2,1)}, bf16[128,1280]{1,0:T(8,128)(2,1)S(1)}, u32[]{:S(2)}, u32[]{:S(2)}) collective-permute-start(bf16[128,1280]{1,0:T(8,128)(2,1)} %bitcast.14), channel_id=1, source_target_pairs={{0,64},{32,96},{64,0},{96,32},{1,65},{33,97},{65,1},{97,33},{2,66}... | collective-permute-start | bytes 983048 | tf_op jit(solution)/shard_map/ppermute | solution.py:231
  29.5 25.9 %collective-permute-start.3 = (bf16[128,1280]{1,0:T(8,128)(2,1)S(1)}, bf16[128,1280]{1,0:T(8,128)(2,1)}, u32[]{:S(2)}, u32[]{:S(2)}) collective-permute-start(bf16[128,1280]{1,0:T(8,128)(2,1)S(1)} %bitcast.78), channel_id=1, source_target_pairs={{0,128},{8,136},{16,144},{24,152},{128,0},{136,8},{144,16},{152,24... | collective-permute-start | bytes 983048 | tf_op jit(solution)/shard_map/ppermute | solution.py:232
  38.4 37.9 %collective-permute-start.4 = (bf16[128,1280]{1,0:T(8,128)(2,1)}, bf16[128,1280]{1,0:T(8,128)(2,1)S(1)}, u32[]{:S(2)}, u32[]{:S(2)}) collective-permute-start(bf16[128,1280]{1,0:T(8,128)(2,1)} %collective-permute-done), channel_id=1, source_target_pairs={{0,128},{8,136},{16,144},{24,152},{128,0},{136,8},{144,16},{152,24... | collective-permute-start | bytes 983048 | tf_op jit(solution)/shard_map/ppermute | solution.py:232
  40.7 43.5 %collective-permute-start.5 = (bf16[128,1280]{1,0:T(8,128)(2,1)}, bf16[128,1280]{1,0:T(8,128)(2,1)S(1)}, u32[]{:S(2)}, u32[]{:S(2)}) collective-permute-start(bf16[128,1280]{1,0:T(8,128)(2,1)} %collective-permute-done.1), channel_id=1, source_target_pairs={{0,128},{8,136},{16,144},{24,152},{128,0},{136,8},{144,16},{152,24... | collective-permute-start | bytes 983048 | tf_op jit(solution)/shard_map/ppermute | solution.py:232
  45.9 45.2 %collective-permute-start.6 = (bf16[128,1280]{1,0:T(8,128)(2,1)S(1)}, bf16[128,1280]{1,0:T(8,128)(2,1)S(1)}, u32[]{:S(2)}, u32[]{:S(2)}) collective-permute-start(bf16[128,1280]{1,0:T(8,128)(2,1)S(1)} %collective-permute-done.2), channel_id=1, source_target_pairs={{0,128},{8,136},{16,144},{24,152},{128,0},{136,8},{144,16},{152,24... | collective-permute-start | bytes 983048 | tf_op jit(solution)/shard_map/ppermute | solution.py:232
  106.1 10.6 %collective-permute-start.11 = (bf16[128,640]{1,0:T(8,128)(2,1)S(1)}, bf16[128,640]{1,0:T(8,128)(2,1)S(1)}, u32[]{:S(2)}, u32[]{:S(2)}) collective-permute-start(bf16[128,640]{1,0:T(8,128)(2,1)S(1)} %bitcast.88), channel_id=1, source_target_pairs={{0,96},{32,0},{64,32},{96,64},{1,97},{33,1},{65,33},{97,65},{2,98}... | collective-permute-start | bytes 491528 | tf_op jit(solution)/shard_map/ppermute | solution.py:246
  107.0 9.7 %collective-permute-start.12 = (bf16[128,640]{1,0:T(8,128)(2,1)S(1)}, bf16[128,640]{1,0:T(8,128)(2,1)S(1)}, u32[]{:S(2)}, u32[]{:S(2)}) collective-permute-start(bf16[128,640]{1,0:T(8,128)(2,1)S(1)} %bitcast.86), channel_id=1, source_target_pairs={{0,32},{32,64},{64,96},{96,0},{1,33},{33,65},{65,97},{97,1},{2,34}... | collective-permute-start | bytes 491528 | tf_op jit(solution)/shard_map/ppermute | solution.py:246
  107.6 9.2 %collective-permute-start.13 = (bf16[128,640]{1,0:T(8,128)(2,1)S(1)}, bf16[128,640]{1,0:T(8,128)(2,1)S(1)}, u32[]{:S(2)}, u32[]{:S(2)}) collective-permute-start(bf16[128,640]{1,0:T(8,128)(2,1)S(1)} %bitcast.84), channel_id=1, source_target_pairs={{0,64},{32,96},{64,0},{96,32},{1,65},{33,97},{65,1},{97,33},{2,66}... | collective-permute-start | bytes 491528 | tf_op jit(solution)/shard_map/ppermute | solution.py:246
  116.6 3.7 %copy-start = (f32[4,4,4,8,1280]{4,3,0,2,1:T(8,128)S(1)}, f32[4,4,4,8,1280]{4,3,0,2,1:T(8,128)}, u32[]{:S(2)}) copy-start(f32[4,4,4,8,1280]{4,3,0,2,1:T(8,128)} %copy.13) | copy-start | bytes 7864324
  116.9 4.7 %collective-permute-start.14 = (bf16[128,640]{1,0:T(8,128)(2,1)S(1)}, bf16[128,640]{1,0:T(8,128)(2,1)S(1)}, u32[]{:S(2)}, u32[]{:S(2)}) collective-permute-start(bf16[128,640]{1,0:T(8,128)(2,1)S(1)} %bitcast.89), channel_id=1, source_target_pairs={{0,96},{32,0},{64,32},{96,64},{1,97},{33,1},{65,33},{97,65},{2,98}... | collective-permute-start | bytes 491528 | tf_op jit(solution)/shard_map/ppermute | solution.py:246
  118.3 7.2 %collective-permute-start.15 = (bf16[128,640]{1,0:T(8,128)(2,1)S(1)}, bf16[128,640]{1,0:T(8,128)(2,1)S(1)}, u32[]{:S(2)}, u32[]{:S(2)}) collective-permute-start(bf16[128,640]{1,0:T(8,128)(2,1)S(1)} %bitcast.87), channel_id=1, source_target_pairs={{0,32},{32,64},{64,96},{96,0},{1,33},{33,65},{65,97},{97,1},{2,34}... | collective-permute-start | bytes 491528 | tf_op jit(solution)/shard_map/ppermute | solution.py:246
  118.6 7.8 %collective-permute-start.16 = (bf16[128,640]{1,0:T(8,128)(2,1)S(1)}, bf16[128,640]{1,0:T(8,128)(2,1)S(1)}, u32[]{:S(2)}, u32[]{:S(2)}) collective-permute-start(bf16[128,640]{1,0:T(8,128)(2,1)S(1)} %bitcast.85), channel_id=1, source_target_pairs={{0,64},{32,96},{64,0},{96,32},{1,65},{33,97},{65,1},{97,33},{2,66}... | collective-permute-start | bytes 491528 | tf_op jit(solution)/shard_map/ppermute | solution.py:246
  127.6 10.0 %copy-start.3 = (f32[3,3,1280]{2,1,0:T(4,128)S(1)}, f32[3,3,1280]{2,1,0:T(4,128)}, u32[]{:S(2)}) copy-start(f32[3,3,1280]{2,1,0:T(4,128)} %param.8) | copy-start | bytes 138244
  127.9 15.3 %collective-permute-start.17 = (bf16[4,1,64,1280]{3,2,1,0:T(8,128)(2,1)S(1)}, bf16[4,1,64,1280]{3,2,1,0:T(8,128)(2,1)S(1)}, u32[]{:S(2)}, u32[]{:S(2)}) collective-permute-start(bf16[4,1,64,1280]{3,2,1,0:T(8,128)(2,1)S(1)} %get-tuple-element.26), channel_id=1, source_target_pairs={{0,1},{1,2},{2,3},{3,4},{4,5},{5,6},{6,7},{7,8},{8,9},{9,10},{10,1... | collective-permute-start | bytes 1966088 | tf_op jit(solution)/shard_map/ppermute | solution.py:259
  135.7 14.0 %collective-permute-start.18 = (bf16[4,1,64,1280]{3,2,1,0:T(8,128)(2,1)S(1)}, bf16[4,1,64,1280]{3,2,1,0:T(8,128)(2,1)S(1)}, u32[]{:S(2)}, u32[]{:S(2)}) collective-permute-start(bf16[4,1,64,1280]{3,2,1,0:T(8,128)(2,1)S(1)} %get-tuple-element.27), channel_id=1, source_target_pairs={{1,0},{2,1},{3,2},{4,3},{5,4},{6,5},{7,6},{8,7},{9,8},{10,9},{11,1... | collective-permute-start | bytes 1966088 | tf_op jit(solution)/shard_map/ppermute | solution.py:260
  137.8 12.3 %copy-start.4 = (f32[1280]{0:T(1024)S(1)}, f32[1280]{0:T(1024)}, u32[]{:S(2)}) copy-start(f32[1280]{0:T(1024)} %param.9) | copy-start | bytes 15364
  (1 other events, 0.8 us)
Sparse Core Ops, SparseCore 0:
  22.9 72.7 all-gather.1

commit v6 on v5

--- a/solution.py
+++ b/solution.py
@@ -191,6 +191,10 @@
     return [(i, (i + shift) % count) for i in range(count)]
 
 
+def pairs(count, mask):
+    return [(i, i ^ mask) for i in range(count)]
+
+
 def tied(*values):
     return lax.optimization_barrier(values)
 
@@ -209,9 +213,14 @@
     )
     planes = jnp.zeros((4, 2 * rows, half), BF16)
     planes = lax.dynamic_update_index_in_dim(planes, piece, zl, 0)
-    for shift in (1, 7, 2):
-        got = lax.ppermute(piece, ("zh", "zl"), ring(8, shift))
-        planes = lax.dynamic_update_index_in_dim(planes, got, (zl + 8 - shift) % 4, 0)
+    below = [(z, (z + 7) % 8 if z % 2 == 0 else (z + 1) % 8) for z in range(8)]
+    for moves, source in (
+        (pairs(8, 1), zl ^ 1),
+        (below, jnp.where(zl % 2 == 0, zl + 3, zl + 1) % 4),
+        (pairs(8, 2), zl ^ 2),
+    ):
+        got = lax.ppermute(piece, ("zh", "zl"), moves)
+        planes = lax.dynamic_update_index_in_dim(planes, got, source, 0)
     gathered = lax.all_gather(planes, ("x", "y", "c"), axis=0, tiled=False)
     return gathered.reshape(4, 4, 2, 4, 2 * rows, half)
 
@@ -222,13 +231,13 @@
     x = lax.axis_index("x")
     part = patch_dev // 4
 
-    def cut(shift):
-        block = lax.dynamic_slice_in_dim(stack, ((x + shift) % 4) * part, part, axis=1)
+    def cut(mask):
+        block = lax.dynamic_slice_in_dim(stack, (x ^ mask) * part, part, axis=1)
         block = block.reshape(date_dev, part // GROUP, GROUP, width).transpose(1, 0, 2, 3)
         return block.reshape(date_dev * part, width)
 
-    shifts = (0, 1, 3, 2)
-    own = [cut(0)] + [lax.ppermute(cut(s), "x", ring(4, s)) for s in shifts[1:]]
+    masks = (0, 1, 3, 2)
+    own = [cut(0)] + [lax.ppermute(cut(m), "x", pairs(4, m)) for m in masks[1:]]
     partner = [lax.ppermute(block, ("zh", "zl"), ring(8, 4)) for block in own]
     w_all = gather_weights(w_qkv, w_out)
     tokens = jnp.concatenate(own + partner)
@@ -240,11 +249,11 @@
     for core in range(2):
         attended = halves[core]
         home = jnp.zeros((4, date_dev * part, width // 2), BF16)
-        for slot, s in enumerate(shifts):
+        for slot, m in enumerate(masks):
             back = attended[slot].reshape(date_dev * part, width // 2)
-            if s:
-                back = lax.ppermute(back, "x", ring(4, 4 - s))
-            home = lax.dynamic_update_index_in_dim(home, back, (x + s) % 4, 0)
+            if m:
+                back = lax.ppermute(back, "x", pairs(4, m))
+            home = lax.dynamic_update_index_in_dim(home, back, x ^ m, 0)
         if core == 0:
             home, halves[1] = tied(home, halves[1])
         columns = slice(core * width // 2, (core + 1) * width // 2)
@@ -254,10 +263,13 @@
     band_rows = 2
     grid_cols = patch_dev // band_rows
     band = mixed.reshape(date_dev, band_rows, grid_cols, width)
-    bands = 32
     axes = ("zl", "y", "c")
-    above = lax.ppermute(band[:, -1:], axes, [(i, i + 1) for i in range(bands - 1)])
-    below = lax.ppermute(band[:, :1], axes, [(i + 1, i) for i in range(bands - 1)])
+    core = lax.axis_index("c")
+    first, last = band[:, :1], band[:, -1:]
+    near = lax.ppermute(jnp.where(core == 0, last, first), "c", pairs(2, 1))
+    across = [(i, i + 1 if i % 2 else i - 1) for i in range(1, 31)]
+    far = lax.ppermute(jnp.where(core == 0, first, last), axes, across)
+    above, below = jnp.where(core == 0, far, near), jnp.where(core == 0, near, far)
     widened = jnp.concatenate([above, band, below], axis=1)
     padded = jnp.pad(widened.astype(F32), ((0, 0), (0, 0), (1, 1), (0, 0)))
     result = band.astype(F32) + conv_bias

time: 161 us -> 155 us (0.963); the launches traced: 161 us -> 153 us
  starting transfers between devices: 40.1 us -> 33.4 us
    ppermute x4, starting transfers between devices: 13.6 us -> 8.86 us  [shards(): partner = [lax.ppermute(block, ('zh', 'zl'), ring(8, 4)) for block in own]]
    all_gather x1, waiting for transfers between devices: 4.62 us -> 1.36 us  [gather_weights(): gathered = lax.all_gather(planes, ('x', 'y', 'c'), axis=0, tiled=False)]
    ppermute x14, starting transfers between devices: 25.7 us -> 23.8 us  [the longest x1 6.9 us: shards(): far = lax.ppermute(jnp.where(core == 0, first, last), axes, across)]
  transfers between devices with their start and end apart: 20 -> 20, of which waited for: 12 -> 13; matrix products, arithmetic and copies ran while one was open for 7% -> 7% of each run, Pallas kernels for 5% -> 5%
where the time goes in v6:
time: 155 us; the launch traced here: 153 us
  waiting for transfers between devices  69.2 us (45%)
  starting transfers between devices  33.4 us (22%)
  Pallas kernels  17.9 us (12%)
  between operations  13.8 us (9%)
  local copies, waits for them, and re-layouts  10.7 us (7%)
  other arithmetic  5.6 us (4%)
  matrix products  2.42 us (2%)
    ppermute x4, waiting for transfers between devices, shards(): partner = [lax.ppermute(block, ('zh', 'zl'), ring(8, 4)) for block in own]  42.9 us
    pallas_call x1, Pallas kernels, run_halves(): pl.pallas_call(functools.partial(first_kernel, head_size), out_shape=(att...  10.3 us
    ppermute x4, starting transfers between devices, shards(): partner = [lax.ppermute(block, ('zh', 'zl'), ring(8, 4)) for block in own]  8.86 us
    ppermute x1, waiting for transfers between devices, shards(): far = lax.ppermute(jnp.where(core == 0, first, last), axes, across)  8.01 us
    pallas_call x1, Pallas kernels, run_halves(): pl.pallas_call(functools.partial(second_kernel, head_size), out_shape=att...  7.61 us
    ppermute x3, waiting for transfers between devices, gather_weights(): got = lax.ppermute(piece, ('zh', 'zl'), moves)  7.03 us
    ppermute x1, starting transfers between devices, shards(): far = lax.ppermute(jnp.where(core == 0, first, last), axes, across)  6.9 us
    ppermute x6, starting transfers between devices, shards(): back = lax.ppermute(back, 'x', pairs(4, m))  6.67 us
  transfers between devices with their start and end apart: 20, of which 13 were waited for; matrix products, arithmetic and copies ran while one was open for 7% of the time, Pallas kernels for 5%

profile of v6, /device:TPU:25, one launch (start us, length us, event | category | flops | bytes accessed | tf_op | source)
XLA Modules:
  0.0 152.9 jit_solution(12784541278899075790)
XLA Ops:
  9.4 1.7 %collective-permute-start.8 = (bf16[80,640]{1,0:T(8,128)(2,1)S(1)}, bf16[80,640]{1,0:T(8,128)(2,1)S(1)}, u32[]{:S(2)}, u32[]{:S(2)}) collective-permute-start(bf16[80,640]{1,0:T(8,128)(2,1)S(1)} %maximum_select_fusion.1), channel_id=1, source_target_pairs={{0,8},{8,0},{16,24},{24,16},{128,136},{136,128},{144,152},{152,144... | collective-permute-start | bytes 307208 | tf_op jit(solution)/shard_map/ppermute | solution.py:222
  11.1 4.7 %collective-permute-start.9 = (bf16[80,640]{1,0:T(8,128)(2,1)S(1)}, bf16[80,640]{1,0:T(8,128)(2,1)S(1)}, u32[]{:S(2)}, u32[]{:S(2)}) collective-permute-start(bf16[80,640]{1,0:T(8,128)(2,1)S(1)} %maximum_select_fusion.1), channel_id=1, source_target_pairs={{0,152},{8,16},{16,8},{24,128},{128,24},{136,144},{144,136},{152,0... | collective-permute-start | bytes 307208 | tf_op jit(solution)/shard_map/ppermute | solution.py:222
  15.9 2.5 %collective-permute-done.9 = bf16[80,640]{1,0:T(8,128)(2,1)S(1)} collective-permute-done((bf16[80,640]{1,0:T(8,128)(2,1)S(1)}, bf16[80,640]{1,0:T(8,128)(2,1)S(1)}, u32[]{:S(2)}, u32[]{:S(2)}) %collective-permute-start.9) | collective-permute-done | bytes 102432 | tf_op jit(solution)/shard_map/ppermute | solution.py:222
  18.4 4.5 %collective-permute-done.10 = bf16[80,640]{1,0:T(8,128)(2,1)S(1)} collective-permute-done((bf16[80,640]{1,0:T(8,128)(2,1)S(1)}, bf16[80,640]{1,0:T(8,128)(2,1)S(1)}, u32[]{:S(2)}, u32[]{:S(2)}) %collective-permute-start.10) | collective-permute-done | bytes 102432 | tf_op jit(solution)/shard_map/ppermute | solution.py:222
  26.6 1.8 %collective-permute-start.1 = (bf16[128,1280]{1,0:T(8,128)(2,1)}, bf16[128,1280]{1,0:T(8,128)(2,1)}, u32[]{:S(2)}, u32[]{:S(2)}) collective-permute-start(bf16[128,1280]{1,0:T(8,128)(2,1)} %bitcast.11), channel_id=1, source_target_pairs={{0,96},{32,64},{64,32},{96,0},{1,97},{33,65},{65,33},{97,1},{2,98}... | collective-permute-start | bytes 983048 | tf_op jit(solution)/shard_map/ppermute | solution.py:240
  29.9 2.6 %collective-permute-start.3 = (bf16[128,1280]{1,0:T(8,128)(2,1)S(1)}, bf16[128,1280]{1,0:T(8,128)(2,1)}, u32[]{:S(2)}, u32[]{:S(2)}) collective-permute-start(bf16[128,1280]{1,0:T(8,128)(2,1)S(1)} %bitcast.78), channel_id=1, source_target_pairs={{0,128},{8,136},{16,144},{24,152},{128,0},{136,8},{144,16},{152,24... | collective-permute-start | bytes 983048 | tf_op jit(solution)/shard_map/ppermute | solution.py:241
  32.5 3.1 %copy.13 = f32[4,4,4,8,1280]{4,3,0,2,1:T(8,128)} copy(bf16[4,4,4,8,1280]{4,3,2,1,0:T(8,128)(2,1)} %bitcast.75) | data formatting | bytes 3932160 | tf_op jit(solution)/shard_map/convert_element_type | solution.py:248
  35.6 2.9 %collective-permute-start.4 = (bf16[128,1280]{1,0:T(8,128)(2,1)}, bf16[128,1280]{1,0:T(8,128)(2,1)S(1)}, u32[]{:S(2)}, u32[]{:S(2)}) collective-permute-start(bf16[128,1280]{1,0:T(8,128)(2,1)} %collective-permute-done), channel_id=1, source_target_pairs={{0,128},{8,136},{16,144},{24,152},{128,0},{136,8},{144,16},{152,24... | collective-permute-start | bytes 983048 | tf_op jit(solution)/shard_map/ppermute | solution.py:241
  39.5 2.2 %collective-permute-done.1 = bf16[128,1280]{1,0:T(8,128)(2,1)} collective-permute-done((bf16[128,1280]{1,0:T(8,128)(2,1)}, bf16[128,1280]{1,0:T(8,128)(2,1)}, u32[]{:S(2)}, u32[]{:S(2)}) %collective-permute-start.1) | collective-permute-done | bytes 327712 | tf_op jit(solution)/shard_map/ppermute | solution.py:240
  43.1 2.3 %collective-permute-done.2 = bf16[128,1280]{1,0:T(8,128)(2,1)S(1)} collective-permute-done((bf16[128,1280]{1,0:T(8,128)(2,1)}, bf16[128,1280]{1,0:T(8,128)(2,1)S(1)}, u32[]{:S(2)}, u32[]{:S(2)}) %collective-permute-start.2) | collective-permute-done | bytes 327712 | tf_op jit(solution)/shard_map/ppermute | solution.py:240
  45.4 3.0 %collective-permute-start.6 = (bf16[128,1280]{1,0:T(8,128)(2,1)S(1)}, bf16[128,1280]{1,0:T(8,128)(2,1)S(1)}, u32[]{:S(2)}, u32[]{:S(2)}) collective-permute-start(bf16[128,1280]{1,0:T(8,128)(2,1)S(1)} %collective-permute-done.2), channel_id=1, source_target_pairs={{0,128},{8,136},{16,144},{24,152},{128,0},{136,8},{144,16},{152,24... | collective-permute-start | bytes 983048 | tf_op jit(solution)/shard_map/ppermute | solution.py:241
  48.4 23.0 %collective-permute-done.3 = bf16[128,1280]{1,0:T(8,128)(2,1)} collective-permute-done((bf16[128,1280]{1,0:T(8,128)(2,1)S(1)}, bf16[128,1280]{1,0:T(8,128)(2,1)}, u32[]{:S(2)}, u32[]{:S(2)}) %collective-permute-start.3) | collective-permute-done | bytes 327712 | tf_op jit(solution)/shard_map/ppermute | solution.py:241
  72.4 5.9 %collective-permute-done.4 = bf16[128,1280]{1,0:T(8,128)(2,1)S(1)} collective-permute-done((bf16[128,1280]{1,0:T(8,128)(2,1)}, bf16[128,1280]{1,0:T(8,128)(2,1)S(1)}, u32[]{:S(2)}, u32[]{:S(2)}) %collective-permute-start.4) | collective-permute-done | bytes 327712 | tf_op jit(solution)/shard_map/ppermute | solution.py:241
  78.3 7.0 %collective-permute-done.5 = bf16[128,1280]{1,0:T(8,128)(2,1)S(1)} collective-permute-done((bf16[128,1280]{1,0:T(8,128)(2,1)}, bf16[128,1280]{1,0:T(8,128)(2,1)S(1)}, u32[]{:S(2)}, u32[]{:S(2)}) %collective-permute-start.5) | collective-permute-done | bytes 327712 | tf_op jit(solution)/shard_map/ppermute | solution.py:241
  85.4 7.0 %collective-permute-done.6 = bf16[128,1280]{1,0:T(8,128)(2,1)S(1)} collective-permute-done((bf16[128,1280]{1,0:T(8,128)(2,1)S(1)}, bf16[128,1280]{1,0:T(8,128)(2,1)S(1)}, u32[]{:S(2)}, u32[]{:S(2)}) %collective-permute-start.6) | collective-permute-done | bytes 327712 | tf_op jit(solution)/shard_map/ppermute | solution.py:241
  93.7 10.3 %shard_map.55 = (bf16[4,4,32,640]{3,2,1,0:T(8,128)(2,1)S(1)}, bf16[4,4,80,1920]{3,2,1,0:T(8,128)(2,1)S(1)}, bf16[4,4,80,1280]{3,2,1,0:T(8,128)(2,1)S(1)}) custom-call(bf16[1024,1280]{1,0:T(8,128)(2,1)S(1)} %constant_dynamic-update-slice_fusion.x_ref, bf16[4,4,2,4,80,640]{5,4,3,2,1,0:T(8,128)(2,1)} %bitcast.70), custom_call_target="tpu_custom_call" | custom-call | flops 4194304000 | bytes 6553600 | tf_op jit(solution)/shard_map/pallas_call | solution.py:159
  105.6 1.9 %collective-permute-start.13 = (bf16[128,640]{1,0:T(8,128)(2,1)S(1)}, bf16[128,640]{1,0:T(8,128)(2,1)S(1)}, u32[]{:S(2)}, u32[]{:S(2)}) collective-permute-start(bf16[128,640]{1,0:T(8,128)(2,1)S(1)} %bitcast.84), channel_id=1, source_target_pairs={{0,64},{32,96},{64,0},{96,32},{1,65},{33,97},{65,1},{97,33},{2,66}... | collective-permute-start | bytes 491528 | tf_op jit(solution)/shard_map/ppermute | solution.py:255
  107.7 7.6 %shard_map.56 = bf16[4,4,32,640]{3,2,1,0:T(8,128)(2,1)S(1)} custom-call(bf16[1024,1280]{1,0:T(8,128)(2,1)S(1)} %constant_dynamic-update-slice_fusion.x_ref, bf16[4,4,80,1920]{3,2,1,0:T(8,128)(2,1)S(1)} %get-tuple-element.11.w_ref), custom_call_target="tpu_custom_call" | custom-call | flops 1048576 | bytes 4096 | tf_op jit(solution)/shard_map/pallas_call | solution.py:178
  117.1 1.9 %collective-permute-start.16 = (bf16[128,640]{1,0:T(8,128)(2,1)S(1)}, bf16[128,640]{1,0:T(8,128)(2,1)S(1)}, u32[]{:S(2)}, u32[]{:S(2)}) collective-permute-start(bf16[128,640]{1,0:T(8,128)(2,1)S(1)} %bitcast.85), channel_id=1, source_target_pairs={{0,64},{32,96},{64,0},{96,32},{1,65},{33,97},{65,1},{97,33},{2,66}... | collective-permute-start | bytes 491528 | tf_op jit(solution)/shard_map/ppermute | solution.py:255
  120.3 1.6 %collective-permute-done.15 = bf16[128,640]{1,0:T(8,128)(2,1)S(1)} collective-permute-done((bf16[128,640]{1,0:T(8,128)(2,1)S(1)}, bf16[128,640]{1,0:T(8,128)(2,1)S(1)}, u32[]{:S(2)}, u32[]{:S(2)}) %collective-permute-start.15) | collective-permute-done | bytes 163872 | tf_op jit(solution)/shard_map/ppermute | solution.py:255
  121.9 2.8 %collective-permute-done.16 = bf16[128,640]{1,0:T(8,128)(2,1)S(1)} collective-permute-done((bf16[128,640]{1,0:T(8,128)(2,1)S(1)}, bf16[128,640]{1,0:T(8,128)(2,1)S(1)}, u32[]{:S(2)}, u32[]{:S(2)}) %collective-permute-start.16) | collective-permute-done | bytes 163872 | tf_op jit(solution)/shard_map/ppermute | solution.py:255
  126.3 6.9 %collective-permute-start.17 = (bf16[4,1,64,1280]{3,2,1,0:T(8,128)(2,1)S(1)}, bf16[4,1,64,1280]{3,2,1,0:T(8,128)(2,1)S(1)}, u32[]{:S(2)}, u32[]{:S(2)}) collective-permute-start(bf16[4,1,64,1280]{3,2,1,0:T(8,128)(2,1)S(1)} %get-tuple-element.28), channel_id=1, source_target_pairs={{1,2},{2,1},{3,4},{4,3},{5,6},{6,5},{7,8},{8,7},{9,10},{10,9},{11,... | collective-permute-start | bytes 1966088 | tf_op jit(solution)/shard_map/ppermute | solution.py:271
  133.4 8.0 %collective-permute-done.17 = bf16[4,1,64,1280]{3,2,1,0:T(8,128)(2,1)S(1)} collective-permute-done((bf16[4,1,64,1280]{3,2,1,0:T(8,128)(2,1)S(1)}, bf16[4,1,64,1280]{3,2,1,0:T(8,128)(2,1)S(1)}, u32[]{:S(2)}, u32[]{:S(2)}) %collective-permute-start.17) | collective-permute-done | bytes 655392 | tf_op jit(solution)/shard_map/ppermute | solution.py:271
  142.2 3.8 %fusion.16 = bf16[4,2,64,1280]{3,2,1,0:T(8,128)(2,1)} fusion(f32[4,4,64,1280]{3,2,1,0:T(8,128)S(1)} %maximum_convert_fusion, bf16[4,2,64,1280]{3,2,1,0:T(8,128)(2,1)S(1)} %bitcast.69, f32[1280]{0:T(1024)S(1)} %get-tuple-element.22, f32[1280]{0:T(1024)S(1)} %get-tuple-element.23, f32[1280]{0:T(1024)S(1)} %get-tuple-element.16, ...), kind=kLoop, calls=%fused_computation.28 | loop fusion | flops 13762560 | bytes 15810560 | tf_op jit(solution)/shard_map/convert_element_type | solution.py:283
  (72 shorter events, 20.2 us)
Async XLA Ops:
  6.5 17.2 %copy-start.1 = (bf16[4,128,1280]{2,1,0:T(8,128)(2,1)S(1)}, bf16[4,128,1280]{2,1,0:T(8,128)(2,1)}, u32[]{:S(2)}) copy-start(bf16[4,128,1280]{2,1,0:T(8,128)(2,1)} %param.5) | copy-start | bytes 3932164
  6.5 87.2 %all-gather.2.cloned.1.call-start = ((), (), s32[]{:S(2)}) async-start(), calls=%async_computation | async-start | bytes 13516800 | tf_op jit(solution)/shard_map/all_gather | solution.py:224
  7.7 1.6 %collective-permute-start.7 = (bf16[40,640]{1,0:T(8,128)(2,1)S(1)}, bf16[40,640]{1,0:T(8,128)(2,1)S(1)}, u32[]{:S(2)}, u32[]{:S(2)}) collective-permute-start(bf16[40,640]{1,0:T(8,128)(2,1)S(1)} %get-tuple-element.43), channel_id=1, source_target_pairs={{0,1},{1,0},{2,3},{3,2},{4,5},{5,4},{6,7},{7,6},{8,9},{9,8},{10,11... | collective-permute-start | bytes 153608 | tf_op jit(solution)/shard_map/ppermute | solution.py:210
  9.4 6.5 %collective-permute-start.8 = (bf16[80,640]{1,0:T(8,128)(2,1)S(1)}, bf16[80,640]{1,0:T(8,128)(2,1)S(1)}, u32[]{:S(2)}, u32[]{:S(2)}) collective-permute-start(bf16[80,640]{1,0:T(8,128)(2,1)S(1)} %maximum_select_fusion.1), channel_id=1, source_target_pairs={{0,8},{8,0},{16,24},{24,16},{128,136},{136,128},{144,152},{152,144... | collective-permute-start | bytes 307208 | tf_op jit(solution)/shard_map/ppermute | solution.py:222
  11.1 7.3 %collective-permute-start.9 = (bf16[80,640]{1,0:T(8,128)(2,1)S(1)}, bf16[80,640]{1,0:T(8,128)(2,1)S(1)}, u32[]{:S(2)}, u32[]{:S(2)}) collective-permute-start(bf16[80,640]{1,0:T(8,128)(2,1)S(1)} %maximum_select_fusion.1), channel_id=1, source_target_pairs={{0,152},{8,16},{16,8},{24,128},{128,24},{136,144},{144,136},{152,0... | collective-permute-start | bytes 307208 | tf_op jit(solution)/shard_map/ppermute | solution.py:222
  15.7 7.2 %collective-permute-start.10 = (bf16[80,640]{1,0:T(8,128)(2,1)S(1)}, bf16[80,640]{1,0:T(8,128)(2,1)S(1)}, u32[]{:S(2)}, u32[]{:S(2)}) collective-permute-start(bf16[80,640]{1,0:T(8,128)(2,1)S(1)} %maximum_select_fusion.1), channel_id=1, source_target_pairs={{0,16},{8,24},{16,0},{24,8},{128,144},{136,152},{144,128},{152,136... | collective-permute-start | bytes 307208 | tf_op jit(solution)/shard_map/ppermute | solution.py:222
  22.9 0.8 copy-start.2
  24.6 11.0 %collective-permute-start = (bf16[128,1280]{1,0:T(8,128)(2,1)}, bf16[128,1280]{1,0:T(8,128)(2,1)}, u32[]{:S(2)}, u32[]{:S(2)}) collective-permute-start(bf16[128,1280]{1,0:T(8,128)(2,1)} %bitcast.8), channel_id=1, source_target_pairs={{0,32},{32,0},{64,96},{96,64},{1,33},{33,1},{65,97},{97,65},{2,34}... | collective-permute-start | bytes 983048 | tf_op jit(solution)/shard_map/ppermute | solution.py:240
  26.6 15.1 %collective-permute-start.1 = (bf16[128,1280]{1,0:T(8,128)(2,1)}, bf16[128,1280]{1,0:T(8,128)(2,1)}, u32[]{:S(2)}, u32[]{:S(2)}) collective-permute-start(bf16[128,1280]{1,0:T(8,128)(2,1)} %bitcast.11), channel_id=1, source_target_pairs={{0,96},{32,64},{64,32},{96,0},{1,97},{33,65},{65,33},{97,1},{2,98}... | collective-permute-start | bytes 983048 | tf_op jit(solution)/shard_map/ppermute | solution.py:240
  29.1 16.2 %collective-permute-start.2 = (bf16[128,1280]{1,0:T(8,128)(2,1)}, bf16[128,1280]{1,0:T(8,128)(2,1)S(1)}, u32[]{:S(2)}, u32[]{:S(2)}) collective-permute-start(bf16[128,1280]{1,0:T(8,128)(2,1)} %bitcast.14), channel_id=1, source_target_pairs={{0,64},{32,96},{64,0},{96,32},{1,65},{33,97},{65,1},{97,33},{2,66}... | collective-permute-start | bytes 983048 | tf_op jit(solution)/shard_map/ppermute | solution.py:240
  29.9 41.5 %collective-permute-start.3 = (bf16[128,1280]{1,0:T(8,128)(2,1)S(1)}, bf16[128,1280]{1,0:T(8,128)(2,1)}, u32[]{:S(2)}, u32[]{:S(2)}) collective-permute-start(bf16[128,1280]{1,0:T(8,128)(2,1)S(1)} %bitcast.78), channel_id=1, source_target_pairs={{0,128},{8,136},{16,144},{24,152},{128,0},{136,8},{144,16},{152,24... | collective-permute-start | bytes 983048 | tf_op jit(solution)/shard_map/ppermute | solution.py:241
  35.6 42.7 %collective-permute-start.4 = (bf16[128,1280]{1,0:T(8,128)(2,1)}, bf16[128,1280]{1,0:T(8,128)(2,1)S(1)}, u32[]{:S(2)}, u32[]{:S(2)}) collective-permute-start(bf16[128,1280]{1,0:T(8,128)(2,1)} %collective-permute-done), channel_id=1, source_target_pairs={{0,128},{8,136},{16,144},{24,152},{128,0},{136,8},{144,16},{152,24... | collective-permute-start | bytes 983048 | tf_op jit(solution)/shard_map/ppermute | solution.py:241
  41.7 43.7 %collective-permute-start.5 = (bf16[128,1280]{1,0:T(8,128)(2,1)}, bf16[128,1280]{1,0:T(8,128)(2,1)S(1)}, u32[]{:S(2)}, u32[]{:S(2)}) collective-permute-start(bf16[128,1280]{1,0:T(8,128)(2,1)} %collective-permute-done.1), channel_id=1, source_target_pairs={{0,128},{8,136},{16,144},{24,152},{128,0},{136,8},{144,16},{152,24... | collective-permute-start | bytes 983048 | tf_op jit(solution)/shard_map/ppermute | solution.py:241
  45.4 47.0 %collective-permute-start.6 = (bf16[128,1280]{1,0:T(8,128)(2,1)S(1)}, bf16[128,1280]{1,0:T(8,128)(2,1)S(1)}, u32[]{:S(2)}, u32[]{:S(2)}) collective-permute-start(bf16[128,1280]{1,0:T(8,128)(2,1)S(1)} %collective-permute-done.2), channel_id=1, source_target_pairs={{0,128},{8,136},{16,144},{24,152},{128,0},{136,8},{144,16},{152,24... | collective-permute-start | bytes 983048 | tf_op jit(solution)/shard_map/ppermute | solution.py:241
  104.1 11.3 %collective-permute-start.11 = (bf16[128,640]{1,0:T(8,128)(2,1)S(1)}, bf16[128,640]{1,0:T(8,128)(2,1)S(1)}, u32[]{:S(2)}, u32[]{:S(2)}) collective-permute-start(bf16[128,640]{1,0:T(8,128)(2,1)S(1)} %bitcast.88), channel_id=1, source_target_pairs={{0,32},{32,0},{64,96},{96,64},{1,33},{33,1},{65,97},{97,65},{2,34}... | collective-permute-start | bytes 491528 | tf_op jit(solution)/shard_map/ppermute | solution.py:255
  104.2 11.2 %collective-permute-start.12 = (bf16[128,640]{1,0:T(8,128)(2,1)S(1)}, bf16[128,640]{1,0:T(8,128)(2,1)S(1)}, u32[]{:S(2)}, u32[]{:S(2)}) collective-permute-start(bf16[128,640]{1,0:T(8,128)(2,1)S(1)} %bitcast.86), channel_id=1, source_target_pairs={{0,96},{32,64},{64,32},{96,0},{1,97},{33,65},{65,33},{97,1},{2,98}... | collective-permute-start | bytes 491528 | tf_op jit(solution)/shard_map/ppermute | solution.py:255
  105.6 9.9 %collective-permute-start.13 = (bf16[128,640]{1,0:T(8,128)(2,1)S(1)}, bf16[128,640]{1,0:T(8,128)(2,1)S(1)}, u32[]{:S(2)}, u32[]{:S(2)}) collective-permute-start(bf16[128,640]{1,0:T(8,128)(2,1)S(1)} %bitcast.84), channel_id=1, source_target_pairs={{0,64},{32,96},{64,0},{96,32},{1,65},{33,97},{65,1},{97,33},{2,66}... | collective-permute-start | bytes 491528 | tf_op jit(solution)/shard_map/ppermute | solution.py:255
  115.3 3.7 %copy-start = (f32[4,4,4,8,1280]{4,3,0,2,1:T(8,128)S(1)}, f32[4,4,4,8,1280]{4,3,0,2,1:T(8,128)}, u32[]{:S(2)}) copy-start(f32[4,4,4,8,1280]{4,3,0,2,1:T(8,128)} %copy.13) | copy-start | bytes 7864324
  115.6 4.7 %collective-permute-start.14 = (bf16[128,640]{1,0:T(8,128)(2,1)S(1)}, bf16[128,640]{1,0:T(8,128)(2,1)S(1)}, u32[]{:S(2)}, u32[]{:S(2)}) collective-permute-start(bf16[128,640]{1,0:T(8,128)(2,1)S(1)} %bitcast.89), channel_id=1, source_target_pairs={{0,32},{32,0},{64,96},{96,64},{1,33},{33,1},{65,97},{97,65},{2,34}... | collective-permute-start | bytes 491528 | tf_op jit(solution)/shard_map/ppermute | solution.py:255
  115.8 6.1 %collective-permute-start.15 = (bf16[128,640]{1,0:T(8,128)(2,1)S(1)}, bf16[128,640]{1,0:T(8,128)(2,1)S(1)}, u32[]{:S(2)}, u32[]{:S(2)}) collective-permute-start(bf16[128,640]{1,0:T(8,128)(2,1)S(1)} %bitcast.87), channel_id=1, source_target_pairs={{0,96},{32,64},{64,32},{96,0},{1,97},{33,65},{65,33},{97,1},{2,98}... | collective-permute-start | bytes 491528 | tf_op jit(solution)/shard_map/ppermute | solution.py:255
  117.1 7.7 %collective-permute-start.16 = (bf16[128,640]{1,0:T(8,128)(2,1)S(1)}, bf16[128,640]{1,0:T(8,128)(2,1)S(1)}, u32[]{:S(2)}, u32[]{:S(2)}) collective-permute-start(bf16[128,640]{1,0:T(8,128)(2,1)S(1)} %bitcast.85), channel_id=1, source_target_pairs={{0,64},{32,96},{64,0},{96,32},{1,65},{33,97},{65,1},{97,33},{2,66}... | collective-permute-start | bytes 491528 | tf_op jit(solution)/shard_map/ppermute | solution.py:255
  126.0 7.3 %copy-start.3 = (f32[3,3,1280]{2,1,0:T(4,128)S(1)}, f32[3,3,1280]{2,1,0:T(4,128)}, u32[]{:S(2)}) copy-start(f32[3,3,1280]{2,1,0:T(4,128)} %param.8) | copy-start | bytes 138244
  126.3 15.2 %collective-permute-start.17 = (bf16[4,1,64,1280]{3,2,1,0:T(8,128)(2,1)S(1)}, bf16[4,1,64,1280]{3,2,1,0:T(8,128)(2,1)S(1)}, u32[]{:S(2)}, u32[]{:S(2)}) collective-permute-start(bf16[4,1,64,1280]{3,2,1,0:T(8,128)(2,1)S(1)} %get-tuple-element.28), channel_id=1, source_target_pairs={{1,2},{2,1},{3,4},{4,3},{5,6},{6,5},{7,8},{8,7},{9,10},{10,9},{11,... | collective-permute-start | bytes 1966088 | tf_op jit(solution)/shard_map/ppermute | solution.py:271
  133.2 8.3 %collective-permute-start.18 = (bf16[4,1,64,1280]{3,2,1,0:T(8,128)(2,1)S(1)}, bf16[4,1,64,1280]{3,2,1,0:T(8,128)(2,1)S(1)}, u32[]{:S(2)}, u32[]{:S(2)}) collective-permute-start(bf16[4,1,64,1280]{3,2,1,0:T(8,128)(2,1)S(1)} %get-tuple-element.29), channel_id=1, source_target_pairs={{0,1},{1,0},{2,3},{3,2},{4,5},{5,4},{6,7},{7,6},{8,9},{9,8},{10,11... | collective-permute-start | bytes 1966088 | tf_op jit(solution)/shard_map/ppermute | solution.py:269
  (1 other events, 0.7 us)
Sparse Core Ops, SparseCore 0:
  23.8 69.8 all-gather.1

commit v7 on v6

--- a/solution.py
+++ b/solution.py
@@ -86,18 +86,19 @@
     ]
 
 
-def attend_half(head_size, x_ref, w_ref, out, q_vm, k_vm, v_vm):
+def attend_half(head_size, x_ref, w_ref, out, q_vm, k_vm, v_vm, ready=lambda mat: None):
     width = x_ref.shape[1]
     half = width // 2
     own = x_ref.shape[0] // 2
-    w = w_ref[...].reshape(width, 3 * half)
-    got = dot(x_ref[:own], w).astype(BF16)
-    q_vm[...] = got[:, :half].reshape(q_vm.shape)
-    k_vm[:4] = got[:, half:width].reshape(q_vm.shape)
-    v_vm[:4] = got[:, width:].reshape(q_vm.shape)
-    got = dot(x_ref[own:], w[:, half:]).astype(BF16)
-    k_vm[4:] = got[:, :half].reshape(q_vm.shape)
-    v_vm[4:] = got[:, half:].reshape(q_vm.shape)
+    ready(0)
+    q_vm[...] = dot(x_ref[:own], w_ref[..., :half].reshape(width, half)).astype(BF16).reshape(
+        q_vm.shape
+    )
+    ready(1)
+    ready(2)
+    got = dot(x_ref[...], w_ref[..., half:].reshape(width, width)).astype(BF16)
+    k_vm[...] = got[:, :half].reshape(k_vm.shape)
+    v_vm[...] = got[:, half:].reshape(v_vm.shape)
 
     def attend(group, _):
         got = attend_rows(
@@ -128,11 +129,15 @@
             )
     for copy in now:
         copy.start()
-    for copy in now:
-        copy.wait()
-    for copy in later:
-        copy.start()
-    attend_half(head_size, x_ref, w_vm, out, q_vm, k_vm, v_vm)
+
+    def ready(mat):
+        for copy in now[4 * mat : 4 * mat + 4]:
+            copy.wait()
+        if mat == 2:
+            for copy in later:
+                copy.start()
+
+    attend_half(head_size, x_ref, w_vm, out, q_vm, k_vm, v_vm, ready)
     for copy in later:
         copy.wait()
 
@@ -270,16 +275,17 @@
     across = [(i, i + 1 if i % 2 else i - 1) for i in range(1, 31)]
     far = lax.ppermute(jnp.where(core == 0, first, last), axes, across)
     above, below = jnp.where(core == 0, far, near), jnp.where(core == 0, near, far)
-    widened = jnp.concatenate([above, band, below], axis=1)
-    padded = jnp.pad(widened.astype(F32), ((0, 0), (0, 0), (1, 1), (0, 0)))
+    halo = jnp.concatenate([above, below], axis=1)
+
+    def taps(rows, weights):
+        padded = jnp.pad(rows.astype(F32), ((0, 0), (0, 0), (1, 1), (0, 0)))
+        return sum(weights[:, i, None] * padded[:, :, i : i + grid_cols] for i in range(3))
+
     result = band.astype(F32) + conv_bias
-    for row_off in range(3):
-        for col_off in range(3):
-            result = (
-                result
-                + conv_weight[row_off, col_off]
-                * padded[:, row_off : row_off + band_rows, col_off : col_off + grid_cols]
-            )
+    result += taps(band, conv_weight[1:2])
+    result += taps(band[:, ::-1], jnp.stack([conv_weight[2], conv_weight[0]]))
+    result, halo = tied(result, halo)
+    result += taps(halo, jnp.stack([conv_weight[0], conv_weight[2]]))
     return result.astype(BF16).reshape(date_dev, patch_dev, width)
 
 

time: 155 us -> 153 us (0.987)
  local copies, waits for them, and re-layouts: 10.7 us -> 9.02 us
    ppermute x1, waiting for transfers between devices: 8.01 us -> 5.98 us  [shards(): far = lax.ppermute(jnp.where(core == 0, first, last), axes, across)]
    add x0 -> x1, other arithmetic: none -> 1.9 us  [shards(): result += taps(band[:, ::-1], jnp.stack([conv_weight[2], conv_weight[0]]))]
    convert_element_type x1, other arithmetic: 3.85 us -> 1.98 us  [shards(): return result.astype(BF16).reshape(date_dev, patch_dev, width)]
    unnamed x17 -> x21, local copies, waits for them, and re-layouts: 4.2 us -> 3.95 us
where the time goes in v7:
time: 153 us; the launch traced here: 151 us
  waiting for transfers between devices  68.5 us (45%)
  starting transfers between devices  33.4 us (22%)
  Pallas kernels  17.8 us (12%)
  between operations  13.8 us (9%)
  local copies, waits for them, and re-layouts  9.02 us (6%)
  other arithmetic  6.09 us (4%)
  matrix products  2.42 us (2%)
    ppermute x4, waiting for transfers between devices, shards(): partner = [lax.ppermute(block, ('zh', 'zl'), ring(8, 4)) for block in own]  42.9 us
    pallas_call x1, Pallas kernels, run_halves(): pl.pallas_call(functools.partial(first_kernel, head_size), out_shape=(att...  10.1 us
    ppermute x4, starting transfers between devices, shards(): partner = [lax.ppermute(block, ('zh', 'zl'), ring(8, 4)) for block in own]  8.56 us
    pallas_call x1, Pallas kernels, run_halves(): pl.pallas_call(functools.partial(second_kernel, head_size), out_shape=att...  7.63 us
    ppermute x3, waiting for transfers between devices, gather_weights(): got = lax.ppermute(piece, ('zh', 'zl'), moves)  7.03 us
    ppermute x1, starting transfers between devices, shards(): far = lax.ppermute(jnp.where(core == 0, first, last), axes, across)  6.9 us
    ppermute x6, starting transfers between devices, shards(): back = lax.ppermute(back, 'x', pairs(4, m))  6.67 us
    ppermute x3, starting transfers between devices, gather_weights(): got = lax.ppermute(piece, ('zh', 'zl'), moves)  6.39 us
  transfers between devices with their start and end apart: 20, of which 13 were waited for; matrix products, arithmetic and copies ran while one was open for 7% of the time, Pallas kernels for 5%

profile of v7, /device:TPU:25, one launch (start us, length us, event | category | flops | bytes accessed | tf_op | source)
XLA Modules:
  0.0 151.0 jit_solution(3110464948277608520)
XLA Ops:
  9.4 1.7 %collective-permute-start.8 = (bf16[80,640]{1,0:T(8,128)(2,1)S(1)}, bf16[80,640]{1,0:T(8,128)(2,1)S(1)}, u32[]{:S(2)}, u32[]{:S(2)}) collective-permute-start(bf16[80,640]{1,0:T(8,128)(2,1)S(1)} %maximum_select_fusion.1), channel_id=1, source_target_pairs={{0,8},{8,0},{16,24},{24,16},{128,136},{136,128},{144,152},{152,144... | collective-permute-start | bytes 307208 | tf_op jit(solution)/shard_map/ppermute | solution.py:227
  11.1 4.7 %collective-permute-start.9 = (bf16[80,640]{1,0:T(8,128)(2,1)S(1)}, bf16[80,640]{1,0:T(8,128)(2,1)S(1)}, u32[]{:S(2)}, u32[]{:S(2)}) collective-permute-start(bf16[80,640]{1,0:T(8,128)(2,1)S(1)} %maximum_select_fusion.1), channel_id=1, source_target_pairs={{0,152},{8,16},{16,8},{24,128},{128,24},{136,144},{144,136},{152,0... | collective-permute-start | bytes 307208 | tf_op jit(solution)/shard_map/ppermute | solution.py:227
  15.9 2.5 %collective-permute-done.9 = bf16[80,640]{1,0:T(8,128)(2,1)S(1)} collective-permute-done((bf16[80,640]{1,0:T(8,128)(2,1)S(1)}, bf16[80,640]{1,0:T(8,128)(2,1)S(1)}, u32[]{:S(2)}, u32[]{:S(2)}) %collective-permute-start.9) | collective-permute-done | bytes 102432 | tf_op jit(solution)/shard_map/ppermute | solution.py:227
  18.4 4.5 %collective-permute-done.10 = bf16[80,640]{1,0:T(8,128)(2,1)S(1)} collective-permute-done((bf16[80,640]{1,0:T(8,128)(2,1)S(1)}, bf16[80,640]{1,0:T(8,128)(2,1)S(1)}, u32[]{:S(2)}, u32[]{:S(2)}) %collective-permute-start.10) | collective-permute-done | bytes 102432 | tf_op jit(solution)/shard_map/ppermute | solution.py:227
  26.6 1.8 %collective-permute-start.1 = (bf16[128,1280]{1,0:T(8,128)(2,1)}, bf16[128,1280]{1,0:T(8,128)(2,1)}, u32[]{:S(2)}, u32[]{:S(2)}) collective-permute-start(bf16[128,1280]{1,0:T(8,128)(2,1)} %bitcast.11), channel_id=1, source_target_pairs={{0,96},{32,64},{64,32},{96,0},{1,97},{33,65},{65,33},{97,1},{2,98}... | collective-permute-start | bytes 983048 | tf_op jit(solution)/shard_map/ppermute | solution.py:245
  29.8 2.6 %collective-permute-start.3 = (bf16[128,1280]{1,0:T(8,128)(2,1)S(1)}, bf16[128,1280]{1,0:T(8,128)(2,1)}, u32[]{:S(2)}, u32[]{:S(2)}) collective-permute-start(bf16[128,1280]{1,0:T(8,128)(2,1)S(1)} %bitcast.92), channel_id=1, source_target_pairs={{0,128},{8,136},{16,144},{24,152},{128,0},{136,8},{144,16},{152,24... | collective-permute-start | bytes 983048 | tf_op jit(solution)/shard_map/ppermute | solution.py:246
  32.4 1.8 %copy.13 = f32[4,4,4,8,1280]{4,3,0,2,1:T(8,128)} copy(bf16[4,4,4,8,1280]{4,3,2,1,0:T(8,128)(2,1)S(1)} %bitcast.89) | data formatting | bytes 3932160 | tf_op jit(solution)/shard_map/convert_element_type | solution.py:253
  34.4 2.9 %collective-permute-start.4 = (bf16[128,1280]{1,0:T(8,128)(2,1)}, bf16[128,1280]{1,0:T(8,128)(2,1)S(1)}, u32[]{:S(2)}, u32[]{:S(2)}) collective-permute-start(bf16[128,1280]{1,0:T(8,128)(2,1)} %collective-permute-done), channel_id=1, source_target_pairs={{0,128},{8,136},{16,144},{24,152},{128,0},{136,8},{144,16},{152,24... | collective-permute-start | bytes 983048 | tf_op jit(solution)/shard_map/ppermute | solution.py:246
  38.4 3.2 %collective-permute-done.1 = bf16[128,1280]{1,0:T(8,128)(2,1)} collective-permute-done((bf16[128,1280]{1,0:T(8,128)(2,1)}, bf16[128,1280]{1,0:T(8,128)(2,1)}, u32[]{:S(2)}, u32[]{:S(2)}) %collective-permute-start.1) | collective-permute-done | bytes 327712 | tf_op jit(solution)/shard_map/ppermute | solution.py:245
  42.7 2.6 %collective-permute-done.2 = bf16[128,1280]{1,0:T(8,128)(2,1)S(1)} collective-permute-done((bf16[128,1280]{1,0:T(8,128)(2,1)}, bf16[128,1280]{1,0:T(8,128)(2,1)S(1)}, u32[]{:S(2)}, u32[]{:S(2)}) %collective-permute-start.2) | collective-permute-done | bytes 327712 | tf_op jit(solution)/shard_map/ppermute | solution.py:245
  45.3 3.0 %collective-permute-start.6 = (bf16[128,1280]{1,0:T(8,128)(2,1)S(1)}, bf16[128,1280]{1,0:T(8,128)(2,1)S(1)}, u32[]{:S(2)}, u32[]{:S(2)}) collective-permute-start(bf16[128,1280]{1,0:T(8,128)(2,1)S(1)} %collective-permute-done.2), channel_id=1, source_target_pairs={{0,128},{8,136},{16,144},{24,152},{128,0},{136,8},{144,16},{152,24... | collective-permute-start | bytes 983048 | tf_op jit(solution)/shard_map/ppermute | solution.py:246
  48.4 23.0 %collective-permute-done.3 = bf16[128,1280]{1,0:T(8,128)(2,1)} collective-permute-done((bf16[128,1280]{1,0:T(8,128)(2,1)S(1)}, bf16[128,1280]{1,0:T(8,128)(2,1)}, u32[]{:S(2)}, u32[]{:S(2)}) %collective-permute-start.3) | collective-permute-done | bytes 327712 | tf_op jit(solution)/shard_map/ppermute | solution.py:246
  72.4 5.9 %collective-permute-done.4 = bf16[128,1280]{1,0:T(8,128)(2,1)S(1)} collective-permute-done((bf16[128,1280]{1,0:T(8,128)(2,1)}, bf16[128,1280]{1,0:T(8,128)(2,1)S(1)}, u32[]{:S(2)}, u32[]{:S(2)}) %collective-permute-start.4) | collective-permute-done | bytes 327712 | tf_op jit(solution)/shard_map/ppermute | solution.py:246
  78.3 7.0 %collective-permute-done.5 = bf16[128,1280]{1,0:T(8,128)(2,1)S(1)} collective-permute-done((bf16[128,1280]{1,0:T(8,128)(2,1)}, bf16[128,1280]{1,0:T(8,128)(2,1)S(1)}, u32[]{:S(2)}, u32[]{:S(2)}) %collective-permute-start.5) | collective-permute-done | bytes 327712 | tf_op jit(solution)/shard_map/ppermute | solution.py:246
  85.3 7.0 %collective-permute-done.6 = bf16[128,1280]{1,0:T(8,128)(2,1)S(1)} collective-permute-done((bf16[128,1280]{1,0:T(8,128)(2,1)S(1)}, bf16[128,1280]{1,0:T(8,128)(2,1)S(1)}, u32[]{:S(2)}, u32[]{:S(2)}) %collective-permute-start.6) | collective-permute-done | bytes 327712 | tf_op jit(solution)/shard_map/ppermute | solution.py:246
  93.7 10.1 %shard_map.55 = (bf16[4,4,32,640]{3,2,1,0:T(8,128)(2,1)S(1)}, bf16[4,4,80,1920]{3,2,1,0:T(8,128)(2,1)S(1)}, bf16[4,4,80,1280]{3,2,1,0:T(8,128)(2,1)S(1)}) custom-call(bf16[1024,1280]{1,0:T(8,128)(2,1)S(1)} %constant_dynamic-update-slice_fusion.x_ref, bf16[4,4,2,4,80,640]{5,4,3,2,1,0:T(8,128)(2,1)} %bitcast.84), custom_call_target="tpu_custom_call" | custom-call | flops 4194304000 | bytes 6553600 | tf_op jit(solution)/shard_map/pallas_call | solution.py:164
  105.4 1.9 %collective-permute-start.13 = (bf16[128,640]{1,0:T(8,128)(2,1)S(1)}, bf16[128,640]{1,0:T(8,128)(2,1)S(1)}, u32[]{:S(2)}, u32[]{:S(2)}) collective-permute-start(bf16[128,640]{1,0:T(8,128)(2,1)S(1)} %bitcast.98), channel_id=1, source_target_pairs={{0,64},{32,96},{64,0},{96,32},{1,65},{33,97},{65,1},{97,33},{2,66}... | collective-permute-start | bytes 491528 | tf_op jit(solution)/shard_map/ppermute | solution.py:260
  107.5 7.6 %shard_map.56 = bf16[4,4,32,640]{3,2,1,0:T(8,128)(2,1)S(1)} custom-call(bf16[1024,1280]{1,0:T(8,128)(2,1)S(1)} %constant_dynamic-update-slice_fusion.x_ref, bf16[4,4,80,1920]{3,2,1,0:T(8,128)(2,1)S(1)} %get-tuple-element.13.w_ref), custom_call_target="tpu_custom_call" | custom-call | flops 1048576 | bytes 4096 | tf_op jit(solution)/shard_map/pallas_call | solution.py:183
  116.9 1.9 %collective-permute-start.16 = (bf16[128,640]{1,0:T(8,128)(2,1)S(1)}, bf16[128,640]{1,0:T(8,128)(2,1)S(1)}, u32[]{:S(2)}, u32[]{:S(2)}) collective-permute-start(bf16[128,640]{1,0:T(8,128)(2,1)S(1)} %bitcast.99), channel_id=1, source_target_pairs={{0,64},{32,96},{64,0},{96,32},{1,65},{33,97},{65,1},{97,33},{2,66}... | collective-permute-start | bytes 491528 | tf_op jit(solution)/shard_map/ppermute | solution.py:260
  121.8 2.8 %collective-permute-done.16 = bf16[128,640]{1,0:T(8,128)(2,1)S(1)} collective-permute-done((bf16[128,640]{1,0:T(8,128)(2,1)S(1)}, bf16[128,640]{1,0:T(8,128)(2,1)S(1)}, u32[]{:S(2)}, u32[]{:S(2)}) %collective-permute-start.16) | collective-permute-done | bytes 163872 | tf_op jit(solution)/shard_map/ppermute | solution.py:260
  126.6 6.9 %collective-permute-start.17 = (bf16[4,1,64,1280]{3,2,1,0:T(8,128)(2,1)S(1)}, bf16[4,1,64,1280]{3,2,1,0:T(8,128)(2,1)S(1)}, u32[]{:S(2)}, u32[]{:S(2)}) collective-permute-start(bf16[4,1,64,1280]{3,2,1,0:T(8,128)(2,1)S(1)} %get-tuple-element.26), channel_id=1, source_target_pairs={{1,2},{2,1},{3,4},{4,3},{5,6},{6,5},{7,8},{8,7},{9,10},{10,9},{11,... | collective-permute-start | bytes 1966088 | tf_op jit(solution)/shard_map/ppermute | solution.py:276
  133.9 1.9 %fusion.5 = f32[4,2,64,1280]{3,2,1,0:T(8,128)S(1)} fusion(f32[4,2,64,1280]{3,2,1,0:T(8,128)S(1)} %convert_element_type.37, f32[4,2,64,1280]{3,2,1,0:T(8,128)S(1)} %reverse_convert_fusion, f32[2,1280]{1,0:T(2,128)S(1)} %get-tuple-element.52, f32[2,1280]{1,0:T(2,128)S(1)} %get-tuple-element.53, f32[2,1280]{1,0:T(2,128)S(1)} %bitcast.105, ...), kind=kLoop, calls=%fused_computation.13 | loop fusion | flops 8519680 | bytes 7915520 | tf_op jit(solution)/shard_map/add | solution.py:286
  135.8 6.0 %collective-permute-done.17 = bf16[4,1,64,1280]{3,2,1,0:T(8,128)(2,1)S(1)} collective-permute-done((bf16[4,1,64,1280]{3,2,1,0:T(8,128)(2,1)S(1)}, bf16[4,1,64,1280]{3,2,1,0:T(8,128)(2,1)S(1)}, u32[]{:S(2)}, u32[]{:S(2)}) %collective-permute-start.17) | collective-permute-done | bytes 655392 | tf_op jit(solution)/shard_map/ppermute | solution.py:276
  142.2 2.0 %fusion.15 = bf16[4,2,64,1280]{3,2,1,0:T(8,128)(2,1)} fusion(f32[4,2,64,1280]{3,2,1,0:T(8,128)S(1)} %fusion.5, f32[4,2,64,1280]{3,2,1,0:T(8,128)S(1)} %convert_element_type.39, f32[2,1280]{1,0:T(2,128)S(1)} %get-tuple-element.50, f32[2,1280]{1,0:T(2,128)S(1)} %get-tuple-element.51, f32[2,1280]{1,0:T(2,128)S(1)} %bitcast.104), kind=kLoop, calls=%fused_computation.23 | loop fusion | flops 4587520 | bytes 6584320 | tf_op jit(solution)/shard_map/convert_element_type | solution.py:289
  (82 shorter events, 21.8 us)
Async XLA Ops:
  6.5 17.2 %copy-start.1 = (bf16[4,128,1280]{2,1,0:T(8,128)(2,1)S(1)}, bf16[4,128,1280]{2,1,0:T(8,128)(2,1)}, u32[]{:S(2)}) copy-start(bf16[4,128,1280]{2,1,0:T(8,128)(2,1)} %param.5) | copy-start | bytes 3932164
  6.5 87.2 %all-gather.2.cloned.1.call-start = ((), (), s32[]{:S(2)}) async-start(), calls=%async_computation | async-start | bytes 13516800 | tf_op jit(solution)/shard_map/all_gather | solution.py:229
  7.7 1.6 %collective-permute-start.7 = (bf16[40,640]{1,0:T(8,128)(2,1)S(1)}, bf16[40,640]{1,0:T(8,128)(2,1)S(1)}, u32[]{:S(2)}, u32[]{:S(2)}) collective-permute-start(bf16[40,640]{1,0:T(8,128)(2,1)S(1)} %get-tuple-element.41), channel_id=1, source_target_pairs={{0,1},{1,0},{2,3},{3,2},{4,5},{5,4},{6,7},{7,6},{8,9},{9,8},{10,11... | collective-permute-start | bytes 153608 | tf_op jit(solution)/shard_map/ppermute | solution.py:215
  9.4 6.5 %collective-permute-start.8 = (bf16[80,640]{1,0:T(8,128)(2,1)S(1)}, bf16[80,640]{1,0:T(8,128)(2,1)S(1)}, u32[]{:S(2)}, u32[]{:S(2)}) collective-permute-start(bf16[80,640]{1,0:T(8,128)(2,1)S(1)} %maximum_select_fusion.1), channel_id=1, source_target_pairs={{0,8},{8,0},{16,24},{24,16},{128,136},{136,128},{144,152},{152,144... | collective-permute-start | bytes 307208 | tf_op jit(solution)/shard_map/ppermute | solution.py:227
  11.1 7.3 %collective-permute-start.9 = (bf16[80,640]{1,0:T(8,128)(2,1)S(1)}, bf16[80,640]{1,0:T(8,128)(2,1)S(1)}, u32[]{:S(2)}, u32[]{:S(2)}) collective-permute-start(bf16[80,640]{1,0:T(8,128)(2,1)S(1)} %maximum_select_fusion.1), channel_id=1, source_target_pairs={{0,152},{8,16},{16,8},{24,128},{128,24},{136,144},{144,136},{152,0... | collective-permute-start | bytes 307208 | tf_op jit(solution)/shard_map/ppermute | solution.py:227
  15.7 7.2 %collective-permute-start.10 = (bf16[80,640]{1,0:T(8,128)(2,1)S(1)}, bf16[80,640]{1,0:T(8,128)(2,1)S(1)}, u32[]{:S(2)}, u32[]{:S(2)}) collective-permute-start(bf16[80,640]{1,0:T(8,128)(2,1)S(1)} %maximum_select_fusion.1), channel_id=1, source_target_pairs={{0,16},{8,24},{16,0},{24,8},{128,144},{136,152},{144,128},{152,136... | collective-permute-start | bytes 307208 | tf_op jit(solution)/shard_map/ppermute | solution.py:227
  24.6 9.8 %collective-permute-start = (bf16[128,1280]{1,0:T(8,128)(2,1)}, bf16[128,1280]{1,0:T(8,128)(2,1)}, u32[]{:S(2)}, u32[]{:S(2)}) collective-permute-start(bf16[128,1280]{1,0:T(8,128)(2,1)} %bitcast.8), channel_id=1, source_target_pairs={{0,32},{32,0},{64,96},{96,64},{1,33},{33,1},{65,97},{97,65},{2,34}... | collective-permute-start | bytes 983048 | tf_op jit(solution)/shard_map/ppermute | solution.py:245
  26.6 15.1 %collective-permute-start.1 = (bf16[128,1280]{1,0:T(8,128)(2,1)}, bf16[128,1280]{1,0:T(8,128)(2,1)}, u32[]{:S(2)}, u32[]{:S(2)}) collective-permute-start(bf16[128,1280]{1,0:T(8,128)(2,1)} %bitcast.11), channel_id=1, source_target_pairs={{0,96},{32,64},{64,32},{96,0},{1,97},{33,65},{65,33},{97,1},{2,98}... | collective-permute-start | bytes 983048 | tf_op jit(solution)/shard_map/ppermute | solution.py:245
  28.4 5.8 %copy-start.3 = (f32[3,3,1280]{2,1,0:T(4,128)S(1)}, f32[3,3,1280]{2,1,0:T(4,128)}, u32[]{:S(2)}) copy-start(f32[3,3,1280]{2,1,0:T(4,128)} %param.8) | copy-start | bytes 138244
  29.1 16.2 %collective-permute-start.2 = (bf16[128,1280]{1,0:T(8,128)(2,1)}, bf16[128,1280]{1,0:T(8,128)(2,1)S(1)}, u32[]{:S(2)}, u32[]{:S(2)}) collective-permute-start(bf16[128,1280]{1,0:T(8,128)(2,1)} %bitcast.14), channel_id=1, source_target_pairs={{0,64},{32,96},{64,0},{96,32},{1,65},{33,97},{65,1},{97,33},{2,66}... | collective-permute-start | bytes 983048 | tf_op jit(solution)/shard_map/ppermute | solution.py:245
  29.8 41.5 %collective-permute-start.3 = (bf16[128,1280]{1,0:T(8,128)(2,1)S(1)}, bf16[128,1280]{1,0:T(8,128)(2,1)}, u32[]{:S(2)}, u32[]{:S(2)}) collective-permute-start(bf16[128,1280]{1,0:T(8,128)(2,1)S(1)} %bitcast.92), channel_id=1, source_target_pairs={{0,128},{8,136},{16,144},{24,152},{128,0},{136,8},{144,16},{152,24... | collective-permute-start | bytes 983048 | tf_op jit(solution)/shard_map/ppermute | solution.py:246
  34.4 43.8 %collective-permute-start.4 = (bf16[128,1280]{1,0:T(8,128)(2,1)}, bf16[128,1280]{1,0:T(8,128)(2,1)S(1)}, u32[]{:S(2)}, u32[]{:S(2)}) collective-permute-start(bf16[128,1280]{1,0:T(8,128)(2,1)} %collective-permute-done), channel_id=1, source_target_pairs={{0,128},{8,136},{16,144},{24,152},{128,0},{136,8},{144,16},{152,24... | collective-permute-start | bytes 983048 | tf_op jit(solution)/shard_map/ppermute | solution.py:246
  41.7 43.6 %collective-permute-start.5 = (bf16[128,1280]{1,0:T(8,128)(2,1)}, bf16[128,1280]{1,0:T(8,128)(2,1)S(1)}, u32[]{:S(2)}, u32[]{:S(2)}) collective-permute-start(bf16[128,1280]{1,0:T(8,128)(2,1)} %collective-permute-done.1), channel_id=1, source_target_pairs={{0,128},{8,136},{16,144},{24,152},{128,0},{136,8},{144,16},{152,24... | collective-permute-start | bytes 983048 | tf_op jit(solution)/shard_map/ppermute | solution.py:246
  45.3 47.0 %collective-permute-start.6 = (bf16[128,1280]{1,0:T(8,128)(2,1)S(1)}, bf16[128,1280]{1,0:T(8,128)(2,1)S(1)}, u32[]{:S(2)}, u32[]{:S(2)}) collective-permute-start(bf16[128,1280]{1,0:T(8,128)(2,1)S(1)} %collective-permute-done.2), channel_id=1, source_target_pairs={{0,128},{8,136},{16,144},{24,152},{128,0},{136,8},{144,16},{152,24... | collective-permute-start | bytes 983048 | tf_op jit(solution)/shard_map/ppermute | solution.py:246
  103.9 11.3 %collective-permute-start.11 = (bf16[128,640]{1,0:T(8,128)(2,1)S(1)}, bf16[128,640]{1,0:T(8,128)(2,1)S(1)}, u32[]{:S(2)}, u32[]{:S(2)}) collective-permute-start(bf16[128,640]{1,0:T(8,128)(2,1)S(1)} %bitcast.102), channel_id=1, source_target_pairs={{0,32},{32,0},{64,96},{96,64},{1,33},{33,1},{65,97},{97,65},{2,34}... | collective-permute-start | bytes 491528 | tf_op jit(solution)/shard_map/ppermute | solution.py:260
  104.0 11.2 %collective-permute-start.12 = (bf16[128,640]{1,0:T(8,128)(2,1)S(1)}, bf16[128,640]{1,0:T(8,128)(2,1)S(1)}, u32[]{:S(2)}, u32[]{:S(2)}) collective-permute-start(bf16[128,640]{1,0:T(8,128)(2,1)S(1)} %bitcast.100), channel_id=1, source_target_pairs={{0,96},{32,64},{64,32},{96,0},{1,97},{33,65},{65,33},{97,1},{2,98}... | collective-permute-start | bytes 491528 | tf_op jit(solution)/shard_map/ppermute | solution.py:260
  105.4 9.9 %collective-permute-start.13 = (bf16[128,640]{1,0:T(8,128)(2,1)S(1)}, bf16[128,640]{1,0:T(8,128)(2,1)S(1)}, u32[]{:S(2)}, u32[]{:S(2)}) collective-permute-start(bf16[128,640]{1,0:T(8,128)(2,1)S(1)} %bitcast.98), channel_id=1, source_target_pairs={{0,64},{32,96},{64,0},{96,32},{1,65},{33,97},{65,1},{97,33},{2,66}... | collective-permute-start | bytes 491528 | tf_op jit(solution)/shard_map/ppermute | solution.py:260
  115.1 3.7 %copy-start = (f32[4,4,4,8,1280]{4,3,0,2,1:T(8,128)S(1)}, f32[4,4,4,8,1280]{4,3,0,2,1:T(8,128)}, u32[]{:S(2)}) copy-start(f32[4,4,4,8,1280]{4,3,0,2,1:T(8,128)} %copy.13) | copy-start | bytes 7864324
  115.5 4.7 %collective-permute-start.14 = (bf16[128,640]{1,0:T(8,128)(2,1)S(1)}, bf16[128,640]{1,0:T(8,128)(2,1)S(1)}, u32[]{:S(2)}, u32[]{:S(2)}) collective-permute-start(bf16[128,640]{1,0:T(8,128)(2,1)S(1)} %bitcast.103), channel_id=1, source_target_pairs={{0,32},{32,0},{64,96},{96,64},{1,33},{33,1},{65,97},{97,65},{2,34}... | collective-permute-start | bytes 491528 | tf_op jit(solution)/shard_map/ppermute | solution.py:260
  115.6 6.1 %collective-permute-start.15 = (bf16[128,640]{1,0:T(8,128)(2,1)S(1)}, bf16[128,640]{1,0:T(8,128)(2,1)S(1)}, u32[]{:S(2)}, u32[]{:S(2)}) collective-permute-start(bf16[128,640]{1,0:T(8,128)(2,1)S(1)} %bitcast.101), channel_id=1, source_target_pairs={{0,96},{32,64},{64,32},{96,0},{1,97},{33,65},{65,33},{97,1},{2,98}... | collective-permute-start | bytes 491528 | tf_op jit(solution)/shard_map/ppermute | solution.py:260
  116.9 7.7 %collective-permute-start.16 = (bf16[128,640]{1,0:T(8,128)(2,1)S(1)}, bf16[128,640]{1,0:T(8,128)(2,1)S(1)}, u32[]{:S(2)}, u32[]{:S(2)}) collective-permute-start(bf16[128,640]{1,0:T(8,128)(2,1)S(1)} %bitcast.99), channel_id=1, source_target_pairs={{0,64},{32,96},{64,0},{96,32},{1,65},{33,97},{65,1},{97,33},{2,66}... | collective-permute-start | bytes 491528 | tf_op jit(solution)/shard_map/ppermute | solution.py:260
  126.3 7.5 %copy-start.4 = (f32[1280]{0:T(1024)S(1)}, f32[1280]{0:T(1024)}, u32[]{:S(2)}) copy-start(f32[1280]{0:T(1024)} %param.9) | copy-start | bytes 15364
  126.6 15.2 %collective-permute-start.17 = (bf16[4,1,64,1280]{3,2,1,0:T(8,128)(2,1)S(1)}, bf16[4,1,64,1280]{3,2,1,0:T(8,128)(2,1)S(1)}, u32[]{:S(2)}, u32[]{:S(2)}) collective-permute-start(bf16[4,1,64,1280]{3,2,1,0:T(8,128)(2,1)S(1)} %get-tuple-element.26), channel_id=1, source_target_pairs={{1,2},{2,1},{3,4},{4,3},{5,6},{6,5},{7,8},{8,7},{9,10},{10,9},{11,... | collective-permute-start | bytes 1966088 | tf_op jit(solution)/shard_map/ppermute | solution.py:276
  133.5 8.3 %collective-permute-start.18 = (bf16[4,1,64,1280]{3,2,1,0:T(8,128)(2,1)S(1)}, bf16[4,1,64,1280]{3,2,1,0:T(8,128)(2,1)S(1)}, u32[]{:S(2)}, u32[]{:S(2)}) collective-permute-start(bf16[4,1,64,1280]{3,2,1,0:T(8,128)(2,1)S(1)} %get-tuple-element.27), channel_id=1, source_target_pairs={{0,1},{1,0},{2,3},{3,2},{4,5},{5,4},{6,7},{7,6},{8,9},{9,8},{10,11... | collective-permute-start | bytes 1966088 | tf_op jit(solution)/shard_map/ppermute | solution.py:274
  (1 other events, 0.8 us)
Sparse Core Ops, SparseCore 0:
  23.8 69.8 all-gather.1

commit v8 on v7

--- a/solution.py
+++ b/solution.py
@@ -28,13 +28,13 @@
         == lax.broadcasted_iota(jnp.int32, (GROUP, cols), 1) % GROUP
     )
     others = jnp.where(same, 0.0, -jnp.inf)[None]
-    tiles = [None] * (width // 128)
-    head, heads = 0, width // head_size
+    windows, head, heads = [], 0, width // head_size
     while head < heads:
-        base = head * head_size // 128 * 128
-        count = max(1, min((base + 256) // head_size, heads) - head)
-        if base + 256 > width:
-            base = width - 256
+        count = max(1, min((head * head_size // 128 * 128 + 256) // head_size, heads) - head)
+        windows.append((min(head * head_size // 128 * 128, width - 256), range(head, head + count)))
+        head += count
+
+    def score(base, members):
         lane = lax.broadcasted_iota(jnp.int32, (rows, 256), 1) + base
         query = queries[:, base : base + 256]
         stacked = jnp.concatenate(
@@ -44,7 +44,7 @@
                     query,
                     jnp.zeros((), BF16),
                 )
-                for h in range(head, head + count)
+                for h in members
             ]
         )
         scores = lax.dot_general(
@@ -53,13 +53,16 @@
             (((1,), (1,)), ((), ())),
             preferred_element_type=F32,
         )
-        scores = (scores.reshape(-1, GROUP, cols) + others).reshape(-1, cols)
+        return (scores.reshape(-1, GROUP, cols) + others).reshape(-1, cols)
+
+    tiles = [None] * (width // 128)
+
+    def gather(base, members, scores):
         top = jnp.max(scores, axis=1, keepdims=True)
         weights = jnp.exp2((scores - top) * scale)
         total = 1.0 / jnp.sum(weights, axis=1, keepdims=True)
-        weights = weights.astype(BF16)
-        out = dot(weights, values[:, base : base + 256])
-        for i, h in enumerate(range(head, head + count)):
+        out = dot(weights.astype(BF16), values[:, base : base + 256])
+        for i, h in enumerate(members):
             part = slice(i * rows, (i + 1) * rows)
             for tile in range(h * head_size // 128, -(-(h + 1) * head_size // 128)):
                 at = tile * 128 - base
@@ -69,7 +72,10 @@
                 else:
                     lanes = lax.broadcasted_iota(jnp.int32, (rows, 128), 1) + tile * 128
                     tiles[tile] = jnp.where(lanes < h * head_size, tiles[tile], got)
-        head += count
+
+    all_scores = [score(*window) for window in windows]
+    for window, scores in zip(windows, all_scores):
+        gather(*window, scores)
     return jnp.concatenate(tiles, axis=1).astype(BF16)
 
 
@@ -86,34 +92,38 @@
     ]
 
 
-def attend_half(head_size, x_ref, w_ref, out, q_vm, k_vm, v_vm, ready=lambda mat: None):
+def attend_half(head_size, x_ref, w_ref, out, ready=lambda mat: None):
     width = x_ref.shape[1]
     half = width // 2
-    own = x_ref.shape[0] // 2
+    part = out.shape[2]
+    turns = 4
+    take = 4 // turns
+
+    def project(turn):
+        x = x_ref[...].reshape(8, 4, part, width)[:, turn * take : (turn + 1) * take]
+        x = x.reshape(8 * take * part, width)
+        q = dot(x[: 4 * take * part], w_ref[..., :half].reshape(width, half)).astype(BF16)
+        if turn == 0:
+            ready(1)
+            ready(2)
+        kv = dot(x, w_ref[..., half:].reshape(width, width)).astype(BF16)
+        shape = (8, take, part, half)
+        return q.reshape(4, *shape[1:]), kv[:, :half].reshape(shape), kv[:, half:].reshape(shape)
+
+    def attend(turn, q, k, v):
+        for i in range(take):
+            got = attend_rows(*(m[:, i].reshape(-1, half) for m in (q, k, v)), head_size)
+            out[:, turn * take + i] = got.reshape(4, -1, half)
+
     ready(0)
-    q_vm[...] = dot(x_ref[:own], w_ref[..., :half].reshape(width, half)).astype(BF16).reshape(
-        q_vm.shape
-    )
-    ready(1)
-    ready(2)
-    got = dot(x_ref[...], w_ref[..., half:].reshape(width, width)).astype(BF16)
-    k_vm[...] = got[:, :half].reshape(k_vm.shape)
-    v_vm[...] = got[:, half:].reshape(v_vm.shape)
-
-    def attend(group, _):
-        got = attend_rows(
-            q_vm[:, pl.ds(group, 1)].reshape(-1, half),
-            k_vm[:, pl.ds(group, 1)].reshape(-1, half),
-            v_vm[:, pl.ds(group, 1)].reshape(-1, half),
-            head_size,
-        )
-        out[:, pl.ds(group, 1)] = got.reshape(4, 1, -1, half)
-        return _
-
-    lax.fori_loop(0, 4, attend, 0, unroll=4)
-
-
-def first_kernel(head_size, x_ref, w_hbm, out, w_next, w_home, w_vm, q_vm, k_vm, v_vm, *sems):
+    held = project(0)
+    for turn in range(turns):
+        after = project(turn + 1) if turn + 1 < turns else None
+        attend(turn, *held)
+        held = after
+
+
+def first_kernel(head_size, x_ref, w_hbm, out, w_next, w_home, w_vm, *sems):
     sem, next_sem, home_sem = sems
     half = w_hbm.shape[-1]
     now = weight_copies(w_hbm, 0, w_vm, sem)
@@ -137,13 +147,13 @@
             for copy in later:
                 copy.start()
 
-    attend_half(head_size, x_ref, w_vm, out, q_vm, k_vm, v_vm, ready)
+    attend_half(head_size, x_ref, w_vm, out, ready)
     for copy in later:
         copy.wait()
 
 
-def second_kernel(head_size, x_ref, w_ref, out, q_vm, k_vm, v_vm):
-    attend_half(head_size, x_ref, w_ref, out, q_vm, k_vm, v_vm)
+def second_kernel(head_size, x_ref, w_ref, out):
+    attend_half(head_size, x_ref, w_ref, out)
 
 
 def run_halves(x, w_all, head_size):
@@ -152,11 +162,6 @@
     vmem = pl.BlockSpec(memory_space=pltpu.VMEM)
     attended = jax.ShapeDtypeStruct((4, 4, part, half), BF16)
     columns = (4, 4, width // 16, 3 * half)
-    scratch = [
-        pltpu.VMEM((4, 4, part, half), BF16),
-        pltpu.VMEM((8, 4, part, half), BF16),
-        pltpu.VMEM((8, 4, part, half), BF16),
-    ]
     params = pltpu.CompilerParams(vmem_limit_bytes=36 * 1024 * 1024)
     cost = pl.CostEstimate(
         flops=5 * rows * width * half, bytes_accessed=8 * width * half, transcendentals=0
@@ -172,7 +177,6 @@
         out_specs=(vmem, vmem, vmem),
         scratch_shapes=[
             pltpu.VMEM(columns, BF16),
-            *scratch,
             pltpu.SemaphoreType.DMA((3, 4)),
             pltpu.SemaphoreType.DMA((3, 4)),
             pltpu.SemaphoreType.DMA((2, 4)),
@@ -185,7 +189,6 @@
         out_shape=attended,
         in_specs=[vmem, vmem],
         out_specs=vmem,
-        scratch_shapes=scratch,
         compiler_params=params,
         cost_estimate=pl.CostEstimate(flops=1 << 20, bytes_accessed=1 << 12, transcendentals=0),
     )(x, w_next)

time: 153 us -> 151 us (0.987)
  Pallas kernels: 17.8 us -> 14.6 us
    pallas_call x1, Pallas kernels: 10.1 us -> 8.51 us  [run_halves(): pl.pallas_call(functools.partial(first_kernel, head_size), out_shape=(att...]
  transfers between devices with their start and end apart: 20 -> 20, of which waited for: 13 -> 13; matrix products, arithmetic and copies ran while one was open for 7% -> 7% of each run, Pallas kernels for 5% -> 4%
where the time goes in v8:
time: 151 us; the launch traced here: 148 us
  waiting for transfers between devices  69 us (46%)
  starting transfers between devices  33.4 us (22%)
  Pallas kernels  14.6 us (10%)
  between operations  13.9 us (9%)
  local copies, waits for them, and re-layouts  9.03 us (6%)
  other arithmetic  6.09 us (4%)
  matrix products  2.42 us (2%)
    ppermute x4, waiting for transfers between devices, shards(): partner = [lax.ppermute(block, ('zh', 'zl'), ring(8, 4)) for block in own]  42.9 us
    ppermute x4, starting transfers between devices, shards(): partner = [lax.ppermute(block, ('zh', 'zl'), ring(8, 4)) for block in own]  8.56 us
    pallas_call x1, Pallas kernels, run_halves(): pl.pallas_call(functools.partial(first_kernel, head_size), out_shape=(att...  8.51 us
    ppermute x3, waiting for transfers between devices, gather_weights(): got = lax.ppermute(piece, ('zh', 'zl'), moves)  7.03 us
    ppermute x1, starting transfers between devices, shards(): far = lax.ppermute(jnp.where(core == 0, first, last), axes, across)  6.91 us
    ppermute x6, starting transfers between devices, shards(): back = lax.ppermute(back, 'x', pairs(4, m))  6.67 us
    ppermute x3, starting transfers between devices, gather_weights(): got = lax.ppermute(piece, ('zh', 'zl'), moves)  6.39 us
    pallas_call x1, Pallas kernels, run_halves(): pl.pallas_call(functools.partial(second_kernel, head_size), out_shape=att...  6.1 us
  transfers between devices with their start and end apart: 20, of which 13 were waited for; matrix products, arithmetic and copies ran while one was open for 7% of the time, Pallas kernels for 4%

profile of v8, /device:TPU:25, one launch (start us, length us, event | category | flops | bytes accessed | tf_op | source)
XLA Modules:
  0.0 148.3 jit_solution(15047646741148626740)
XLA Ops:
  9.4 1.7 %collective-permute-start.8 = (bf16[80,640]{1,0:T(8,128)(2,1)S(1)}, bf16[80,640]{1,0:T(8,128)(2,1)S(1)}, u32[]{:S(2)}, u32[]{:S(2)}) collective-permute-start(bf16[80,640]{1,0:T(8,128)(2,1)S(1)} %maximum_select_fusion.1), channel_id=1, source_target_pairs={{0,8},{8,0},{16,24},{24,16},{128,136},{136,128},{144,152},{152,144... | collective-permute-start | bytes 307208 | tf_op jit(solution)/shard_map/ppermute | solution.py:230
  11.1 4.7 %collective-permute-start.9 = (bf16[80,640]{1,0:T(8,128)(2,1)S(1)}, bf16[80,640]{1,0:T(8,128)(2,1)S(1)}, u32[]{:S(2)}, u32[]{:S(2)}) collective-permute-start(bf16[80,640]{1,0:T(8,128)(2,1)S(1)} %maximum_select_fusion.1), channel_id=1, source_target_pairs={{0,152},{8,16},{16,8},{24,128},{128,24},{136,144},{144,136},{152,0... | collective-permute-start | bytes 307208 | tf_op jit(solution)/shard_map/ppermute | solution.py:230
  15.9 2.5 %collective-permute-done.9 = bf16[80,640]{1,0:T(8,128)(2,1)S(1)} collective-permute-done((bf16[80,640]{1,0:T(8,128)(2,1)S(1)}, bf16[80,640]{1,0:T(8,128)(2,1)S(1)}, u32[]{:S(2)}, u32[]{:S(2)}) %collective-permute-start.9) | collective-permute-done | bytes 102432 | tf_op jit(solution)/shard_map/ppermute | solution.py:230
  18.4 4.5 %collective-permute-done.10 = bf16[80,640]{1,0:T(8,128)(2,1)S(1)} collective-permute-done((bf16[80,640]{1,0:T(8,128)(2,1)S(1)}, bf16[80,640]{1,0:T(8,128)(2,1)S(1)}, u32[]{:S(2)}, u32[]{:S(2)}) %collective-permute-start.10) | collective-permute-done | bytes 102432 | tf_op jit(solution)/shard_map/ppermute | solution.py:230
  26.6 1.8 %collective-permute-start.1 = (bf16[128,1280]{1,0:T(8,128)(2,1)}, bf16[128,1280]{1,0:T(8,128)(2,1)}, u32[]{:S(2)}, u32[]{:S(2)}) collective-permute-start(bf16[128,1280]{1,0:T(8,128)(2,1)} %bitcast.11), channel_id=1, source_target_pairs={{0,96},{32,64},{64,32},{96,0},{1,97},{33,65},{65,33},{97,1},{2,98}... | collective-permute-start | bytes 983048 | tf_op jit(solution)/shard_map/ppermute | solution.py:248
  29.8 2.6 %collective-permute-start.3 = (bf16[128,1280]{1,0:T(8,128)(2,1)S(1)}, bf16[128,1280]{1,0:T(8,128)(2,1)}, u32[]{:S(2)}, u32[]{:S(2)}) collective-permute-start(bf16[128,1280]{1,0:T(8,128)(2,1)S(1)} %bitcast.92), channel_id=1, source_target_pairs={{0,128},{8,136},{16,144},{24,152},{128,0},{136,8},{144,16},{152,24... | collective-permute-start | bytes 983048 | tf_op jit(solution)/shard_map/ppermute | solution.py:249
  32.4 1.8 %copy.13 = f32[4,4,4,8,1280]{4,3,0,2,1:T(8,128)} copy(bf16[4,4,4,8,1280]{4,3,2,1,0:T(8,128)(2,1)S(1)} %bitcast.89) | data formatting | bytes 3932160 | tf_op jit(solution)/shard_map/convert_element_type | solution.py:256
  34.4 2.9 %collective-permute-start.4 = (bf16[128,1280]{1,0:T(8,128)(2,1)}, bf16[128,1280]{1,0:T(8,128)(2,1)S(1)}, u32[]{:S(2)}, u32[]{:S(2)}) collective-permute-start(bf16[128,1280]{1,0:T(8,128)(2,1)} %collective-permute-done), channel_id=1, source_target_pairs={{0,128},{8,136},{16,144},{24,152},{128,0},{136,8},{144,16},{152,24... | collective-permute-start | bytes 983048 | tf_op jit(solution)/shard_map/ppermute | solution.py:249
  38.4 3.2 %collective-permute-done.1 = bf16[128,1280]{1,0:T(8,128)(2,1)} collective-permute-done((bf16[128,1280]{1,0:T(8,128)(2,1)}, bf16[128,1280]{1,0:T(8,128)(2,1)}, u32[]{:S(2)}, u32[]{:S(2)}) %collective-permute-start.1) | collective-permute-done | bytes 327712 | tf_op jit(solution)/shard_map/ppermute | solution.py:248
  42.7 2.6 %collective-permute-done.2 = bf16[128,1280]{1,0:T(8,128)(2,1)S(1)} collective-permute-done((bf16[128,1280]{1,0:T(8,128)(2,1)}, bf16[128,1280]{1,0:T(8,128)(2,1)S(1)}, u32[]{:S(2)}, u32[]{:S(2)}) %collective-permute-start.2) | collective-permute-done | bytes 327712 | tf_op jit(solution)/shard_map/ppermute | solution.py:248
  45.3 3.0 %collective-permute-start.6 = (bf16[128,1280]{1,0:T(8,128)(2,1)S(1)}, bf16[128,1280]{1,0:T(8,128)(2,1)S(1)}, u32[]{:S(2)}, u32[]{:S(2)}) collective-permute-start(bf16[128,1280]{1,0:T(8,128)(2,1)S(1)} %collective-permute-done.2), channel_id=1, source_target_pairs={{0,128},{8,136},{16,144},{24,152},{128,0},{136,8},{144,16},{152,24... | collective-permute-start | bytes 983048 | tf_op jit(solution)/shard_map/ppermute | solution.py:249
  48.4 23.0 %collective-permute-done.3 = bf16[128,1280]{1,0:T(8,128)(2,1)} collective-permute-done((bf16[128,1280]{1,0:T(8,128)(2,1)S(1)}, bf16[128,1280]{1,0:T(8,128)(2,1)}, u32[]{:S(2)}, u32[]{:S(2)}) %collective-permute-start.3) | collective-permute-done | bytes 327712 | tf_op jit(solution)/shard_map/ppermute | solution.py:249
  72.4 5.9 %collective-permute-done.4 = bf16[128,1280]{1,0:T(8,128)(2,1)S(1)} collective-permute-done((bf16[128,1280]{1,0:T(8,128)(2,1)}, bf16[128,1280]{1,0:T(8,128)(2,1)S(1)}, u32[]{:S(2)}, u32[]{:S(2)}) %collective-permute-start.4) | collective-permute-done | bytes 327712 | tf_op jit(solution)/shard_map/ppermute | solution.py:249
  78.3 7.0 %collective-permute-done.5 = bf16[128,1280]{1,0:T(8,128)(2,1)S(1)} collective-permute-done((bf16[128,1280]{1,0:T(8,128)(2,1)}, bf16[128,1280]{1,0:T(8,128)(2,1)S(1)}, u32[]{:S(2)}, u32[]{:S(2)}) %collective-permute-start.5) | collective-permute-done | bytes 327712 | tf_op jit(solution)/shard_map/ppermute | solution.py:249
  85.3 7.0 %collective-permute-done.6 = bf16[128,1280]{1,0:T(8,128)(2,1)S(1)} collective-permute-done((bf16[128,1280]{1,0:T(8,128)(2,1)S(1)}, bf16[128,1280]{1,0:T(8,128)(2,1)S(1)}, u32[]{:S(2)}, u32[]{:S(2)}) %collective-permute-start.6) | collective-permute-done | bytes 327712 | tf_op jit(solution)/shard_map/ppermute | solution.py:249
  93.7 8.5 %shard_map.55 = (bf16[4,4,32,640]{3,2,1,0:T(8,128)(2,1)S(1)}, bf16[4,4,80,1920]{3,2,1,0:T(8,128)(2,1)S(1)}, bf16[4,4,80,1280]{3,2,1,0:T(8,128)(2,1)S(1)}) custom-call(bf16[1024,1280]{1,0:T(8,128)(2,1)S(1)} %constant_dynamic-update-slice_fusion.x_ref, bf16[4,4,2,4,80,640]{5,4,3,2,1,0:T(8,128)(2,1)} %bitcast.84), custom_call_target="tpu_custom_call" | custom-call | flops 4194304000 | bytes 6553600 | tf_op jit(solution)/shard_map/pallas_call | solution.py:169
  103.8 1.9 %collective-permute-start.13 = (bf16[128,640]{1,0:T(8,128)(2,1)S(1)}, bf16[128,640]{1,0:T(8,128)(2,1)S(1)}, u32[]{:S(2)}, u32[]{:S(2)}) collective-permute-start(bf16[128,640]{1,0:T(8,128)(2,1)S(1)} %bitcast.98), channel_id=1, source_target_pairs={{0,64},{32,96},{64,0},{96,32},{1,65},{33,97},{65,1},{97,33},{2,66}... | collective-permute-start | bytes 491528 | tf_op jit(solution)/shard_map/ppermute | solution.py:263
  105.9 6.1 %shard_map.56 = bf16[4,4,32,640]{3,2,1,0:T(8,128)(2,1)S(1)} custom-call(bf16[1024,1280]{1,0:T(8,128)(2,1)S(1)} %constant_dynamic-update-slice_fusion.x_ref, bf16[4,4,80,1920]{3,2,1,0:T(8,128)(2,1)S(1)} %get-tuple-element.13.w_ref), custom_call_target="tpu_custom_call" | custom-call | flops 1048576 | bytes 4096 | tf_op jit(solution)/shard_map/pallas_call | solution.py:187
  112.5 1.7 %collective-permute-start.15 = (bf16[128,640]{1,0:T(8,128)(2,1)S(1)}, bf16[128,640]{1,0:T(8,128)(2,1)S(1)}, u32[]{:S(2)}, u32[]{:S(2)}) collective-permute-start(bf16[128,640]{1,0:T(8,128)(2,1)S(1)} %bitcast.101), channel_id=1, source_target_pairs={{0,96},{32,64},{64,32},{96,0},{1,97},{33,65},{65,33},{97,1},{2,98}... | collective-permute-start | bytes 491528 | tf_op jit(solution)/shard_map/ppermute | solution.py:263
  117.9 4.0 %collective-permute-done.16 = bf16[128,640]{1,0:T(8,128)(2,1)S(1)} collective-permute-done((bf16[128,640]{1,0:T(8,128)(2,1)S(1)}, bf16[128,640]{1,0:T(8,128)(2,1)S(1)}, u32[]{:S(2)}, u32[]{:S(2)}) %collective-permute-start.16) | collective-permute-done | bytes 163872 | tf_op jit(solution)/shard_map/ppermute | solution.py:263
  123.9 6.9 %collective-permute-start.17 = (bf16[4,1,64,1280]{3,2,1,0:T(8,128)(2,1)S(1)}, bf16[4,1,64,1280]{3,2,1,0:T(8,128)(2,1)S(1)}, u32[]{:S(2)}, u32[]{:S(2)}) collective-permute-start(bf16[4,1,64,1280]{3,2,1,0:T(8,128)(2,1)S(1)} %get-tuple-element.26), channel_id=1, source_target_pairs={{1,2},{2,1},{3,4},{4,3},{5,6},{6,5},{7,8},{8,7},{9,10},{10,9},{11,... | collective-permute-start | bytes 1966088 | tf_op jit(solution)/shard_map/ppermute | solution.py:279
  131.2 1.9 %fusion.5 = f32[4,2,64,1280]{3,2,1,0:T(8,128)S(1)} fusion(f32[4,2,64,1280]{3,2,1,0:T(8,128)S(1)} %convert_element_type.37, f32[4,2,64,1280]{3,2,1,0:T(8,128)S(1)} %reverse_convert_fusion, f32[2,1280]{1,0:T(2,128)S(1)} %get-tuple-element.52, f32[2,1280]{1,0:T(2,128)S(1)} %get-tuple-element.53, f32[2,1280]{1,0:T(2,128)S(1)} %bitcast.105, ...), kind=kLoop, calls=%fused_computation.13 | loop fusion | flops 8519680 | bytes 7915520 | tf_op jit(solution)/shard_map/add | solution.py:289
  133.1 6.0 %collective-permute-done.17 = bf16[4,1,64,1280]{3,2,1,0:T(8,128)(2,1)S(1)} collective-permute-done((bf16[4,1,64,1280]{3,2,1,0:T(8,128)(2,1)S(1)}, bf16[4,1,64,1280]{3,2,1,0:T(8,128)(2,1)S(1)}, u32[]{:S(2)}, u32[]{:S(2)}) %collective-permute-start.17) | collective-permute-done | bytes 655392 | tf_op jit(solution)/shard_map/ppermute | solution.py:279
  139.5 2.0 %fusion.15 = bf16[4,2,64,1280]{3,2,1,0:T(8,128)(2,1)} fusion(f32[4,2,64,1280]{3,2,1,0:T(8,128)S(1)} %fusion.5, f32[4,2,64,1280]{3,2,1,0:T(8,128)S(1)} %convert_element_type.39, f32[2,1280]{1,0:T(2,128)S(1)} %get-tuple-element.50, f32[2,1280]{1,0:T(2,128)S(1)} %get-tuple-element.51, f32[2,1280]{1,0:T(2,128)S(1)} %bitcast.104), kind=kLoop, calls=%fused_computation.23 | loop fusion | flops 4587520 | bytes 6584320 | tf_op jit(solution)/shard_map/convert_element_type | solution.py:292
  (82 shorter events, 21.2 us)
Async XLA Ops:
  6.5 17.2 %copy-start.1 = (bf16[4,128,1280]{2,1,0:T(8,128)(2,1)S(1)}, bf16[4,128,1280]{2,1,0:T(8,128)(2,1)}, u32[]{:S(2)}) copy-start(bf16[4,128,1280]{2,1,0:T(8,128)(2,1)} %param.5) | copy-start | bytes 3932164
  6.5 87.2 %all-gather.2.cloned.1.call-start = ((), (), s32[]{:S(2)}) async-start(), calls=%async_computation | async-start | bytes 13516800 | tf_op jit(solution)/shard_map/all_gather | solution.py:232
  7.7 1.6 %collective-permute-start.7 = (bf16[40,640]{1,0:T(8,128)(2,1)S(1)}, bf16[40,640]{1,0:T(8,128)(2,1)S(1)}, u32[]{:S(2)}, u32[]{:S(2)}) collective-permute-start(bf16[40,640]{1,0:T(8,128)(2,1)S(1)} %get-tuple-element.41), channel_id=1, source_target_pairs={{0,1},{1,0},{2,3},{3,2},{4,5},{5,4},{6,7},{7,6},{8,9},{9,8},{10,11... | collective-permute-start | bytes 153608 | tf_op jit(solution)/shard_map/ppermute | solution.py:218
  9.4 6.5 %collective-permute-start.8 = (bf16[80,640]{1,0:T(8,128)(2,1)S(1)}, bf16[80,640]{1,0:T(8,128)(2,1)S(1)}, u32[]{:S(2)}, u32[]{:S(2)}) collective-permute-start(bf16[80,640]{1,0:T(8,128)(2,1)S(1)} %maximum_select_fusion.1), channel_id=1, source_target_pairs={{0,8},{8,0},{16,24},{24,16},{128,136},{136,128},{144,152},{152,144... | collective-permute-start | bytes 307208 | tf_op jit(solution)/shard_map/ppermute | solution.py:230
  11.1 7.3 %collective-permute-start.9 = (bf16[80,640]{1,0:T(8,128)(2,1)S(1)}, bf16[80,640]{1,0:T(8,128)(2,1)S(1)}, u32[]{:S(2)}, u32[]{:S(2)}) collective-permute-start(bf16[80,640]{1,0:T(8,128)(2,1)S(1)} %maximum_select_fusion.1), channel_id=1, source_target_pairs={{0,152},{8,16},{16,8},{24,128},{128,24},{136,144},{144,136},{152,0... | collective-permute-start | bytes 307208 | tf_op jit(solution)/shard_map/ppermute | solution.py:230
  15.7 7.2 %collective-permute-start.10 = (bf16[80,640]{1,0:T(8,128)(2,1)S(1)}, bf16[80,640]{1,0:T(8,128)(2,1)S(1)}, u32[]{:S(2)}, u32[]{:S(2)}) collective-permute-start(bf16[80,640]{1,0:T(8,128)(2,1)S(1)} %maximum_select_fusion.1), channel_id=1, source_target_pairs={{0,16},{8,24},{16,0},{24,8},{128,144},{136,152},{144,128},{152,136... | collective-permute-start | bytes 307208 | tf_op jit(solution)/shard_map/ppermute | solution.py:230
  24.6 9.8 %collective-permute-start = (bf16[128,1280]{1,0:T(8,128)(2,1)}, bf16[128,1280]{1,0:T(8,128)(2,1)}, u32[]{:S(2)}, u32[]{:S(2)}) collective-permute-start(bf16[128,1280]{1,0:T(8,128)(2,1)} %bitcast.8), channel_id=1, source_target_pairs={{0,32},{32,0},{64,96},{96,64},{1,33},{33,1},{65,97},{97,65},{2,34}... | collective-permute-start | bytes 983048 | tf_op jit(solution)/shard_map/ppermute | solution.py:248
  26.6 15.1 %collective-permute-start.1 = (bf16[128,1280]{1,0:T(8,128)(2,1)}, bf16[128,1280]{1,0:T(8,128)(2,1)}, u32[]{:S(2)}, u32[]{:S(2)}) collective-permute-start(bf16[128,1280]{1,0:T(8,128)(2,1)} %bitcast.11), channel_id=1, source_target_pairs={{0,96},{32,64},{64,32},{96,0},{1,97},{33,65},{65,33},{97,1},{2,98}... | collective-permute-start | bytes 983048 | tf_op jit(solution)/shard_map/ppermute | solution.py:248
  28.4 5.8 %copy-start.3 = (f32[3,3,1280]{2,1,0:T(4,128)S(1)}, f32[3,3,1280]{2,1,0:T(4,128)}, u32[]{:S(2)}) copy-start(f32[3,3,1280]{2,1,0:T(4,128)} %param.8) | copy-start | bytes 138244
  29.1 16.2 %collective-permute-start.2 = (bf16[128,1280]{1,0:T(8,128)(2,1)}, bf16[128,1280]{1,0:T(8,128)(2,1)S(1)}, u32[]{:S(2)}, u32[]{:S(2)}) collective-permute-start(bf16[128,1280]{1,0:T(8,128)(2,1)} %bitcast.14), channel_id=1, source_target_pairs={{0,64},{32,96},{64,0},{96,32},{1,65},{33,97},{65,1},{97,33},{2,66}... | collective-permute-start | bytes 983048 | tf_op jit(solution)/shard_map/ppermute | solution.py:248
  29.8 41.5 %collective-permute-start.3 = (bf16[128,1280]{1,0:T(8,128)(2,1)S(1)}, bf16[128,1280]{1,0:T(8,128)(2,1)}, u32[]{:S(2)}, u32[]{:S(2)}) collective-permute-start(bf16[128,1280]{1,0:T(8,128)(2,1)S(1)} %bitcast.92), channel_id=1, source_target_pairs={{0,128},{8,136},{16,144},{24,152},{128,0},{136,8},{144,16},{152,24... | collective-permute-start | bytes 983048 | tf_op jit(solution)/shard_map/ppermute | solution.py:249
  34.4 43.8 %collective-permute-start.4 = (bf16[128,1280]{1,0:T(8,128)(2,1)}, bf16[128,1280]{1,0:T(8,128)(2,1)S(1)}, u32[]{:S(2)}, u32[]{:S(2)}) collective-permute-start(bf16[128,1280]{1,0:T(8,128)(2,1)} %collective-permute-done), channel_id=1, source_target_pairs={{0,128},{8,136},{16,144},{24,152},{128,0},{136,8},{144,16},{152,24... | collective-permute-start | bytes 983048 | tf_op jit(solution)/shard_map/ppermute | solution.py:249
  41.7 43.6 %collective-permute-start.5 = (bf16[128,1280]{1,0:T(8,128)(2,1)}, bf16[128,1280]{1,0:T(8,128)(2,1)S(1)}, u32[]{:S(2)}, u32[]{:S(2)}) collective-permute-start(bf16[128,1280]{1,0:T(8,128)(2,1)} %collective-permute-done.1), channel_id=1, source_target_pairs={{0,128},{8,136},{16,144},{24,152},{128,0},{136,8},{144,16},{152,24... | collective-permute-start | bytes 983048 | tf_op jit(solution)/shard_map/ppermute | solution.py:249
  45.3 47.0 %collective-permute-start.6 = (bf16[128,1280]{1,0:T(8,128)(2,1)S(1)}, bf16[128,1280]{1,0:T(8,128)(2,1)S(1)}, u32[]{:S(2)}, u32[]{:S(2)}) collective-permute-start(bf16[128,1280]{1,0:T(8,128)(2,1)S(1)} %collective-permute-done.2), channel_id=1, source_target_pairs={{0,128},{8,136},{16,144},{24,152},{128,0},{136,8},{144,16},{152,24... | collective-permute-start | bytes 983048 | tf_op jit(solution)/shard_map/ppermute | solution.py:249
  102.3 9.8 %collective-permute-start.11 = (bf16[128,640]{1,0:T(8,128)(2,1)S(1)}, bf16[128,640]{1,0:T(8,128)(2,1)S(1)}, u32[]{:S(2)}, u32[]{:S(2)}) collective-permute-start(bf16[128,640]{1,0:T(8,128)(2,1)S(1)} %bitcast.102), channel_id=1, source_target_pairs={{0,32},{32,0},{64,96},{96,64},{1,33},{33,1},{65,97},{97,65},{2,34}... | collective-permute-start | bytes 491528 | tf_op jit(solution)/shard_map/ppermute | solution.py:263
  102.4 9.7 %collective-permute-start.12 = (bf16[128,640]{1,0:T(8,128)(2,1)S(1)}, bf16[128,640]{1,0:T(8,128)(2,1)S(1)}, u32[]{:S(2)}, u32[]{:S(2)}) collective-permute-start(bf16[128,640]{1,0:T(8,128)(2,1)S(1)} %bitcast.100), channel_id=1, source_target_pairs={{0,96},{32,64},{64,32},{96,0},{1,97},{33,65},{65,33},{97,1},{2,98}... | collective-permute-start | bytes 491528 | tf_op jit(solution)/shard_map/ppermute | solution.py:263
  103.8 8.4 %collective-permute-start.13 = (bf16[128,640]{1,0:T(8,128)(2,1)S(1)}, bf16[128,640]{1,0:T(8,128)(2,1)S(1)}, u32[]{:S(2)}, u32[]{:S(2)}) collective-permute-start(bf16[128,640]{1,0:T(8,128)(2,1)S(1)} %bitcast.98), channel_id=1, source_target_pairs={{0,64},{32,96},{64,0},{96,32},{1,65},{33,97},{65,1},{97,33},{2,66}... | collective-permute-start | bytes 491528 | tf_op jit(solution)/shard_map/ppermute | solution.py:263
  112.0 3.7 %copy-start = (f32[4,4,4,8,1280]{4,3,0,2,1:T(8,128)S(1)}, f32[4,4,4,8,1280]{4,3,0,2,1:T(8,128)}, u32[]{:S(2)}) copy-start(f32[4,4,4,8,1280]{4,3,0,2,1:T(8,128)} %copy.13) | copy-start | bytes 7864324
  112.3 4.7 %collective-permute-start.14 = (bf16[128,640]{1,0:T(8,128)(2,1)S(1)}, bf16[128,640]{1,0:T(8,128)(2,1)S(1)}, u32[]{:S(2)}, u32[]{:S(2)}) collective-permute-start(bf16[128,640]{1,0:T(8,128)(2,1)S(1)} %bitcast.103), channel_id=1, source_target_pairs={{0,32},{32,0},{64,96},{96,64},{1,33},{33,1},{65,97},{97,65},{2,34}... | collective-permute-start | bytes 491528 | tf_op jit(solution)/shard_map/ppermute | solution.py:263
  112.5 5.4 %collective-permute-start.15 = (bf16[128,640]{1,0:T(8,128)(2,1)S(1)}, bf16[128,640]{1,0:T(8,128)(2,1)S(1)}, u32[]{:S(2)}, u32[]{:S(2)}) collective-permute-start(bf16[128,640]{1,0:T(8,128)(2,1)S(1)} %bitcast.101), channel_id=1, source_target_pairs={{0,96},{32,64},{64,32},{96,0},{1,97},{33,65},{65,33},{97,1},{2,98}... | collective-permute-start | bytes 491528 | tf_op jit(solution)/shard_map/ppermute | solution.py:263
  114.2 7.7 %collective-permute-start.16 = (bf16[128,640]{1,0:T(8,128)(2,1)S(1)}, bf16[128,640]{1,0:T(8,128)(2,1)S(1)}, u32[]{:S(2)}, u32[]{:S(2)}) collective-permute-start(bf16[128,640]{1,0:T(8,128)(2,1)S(1)} %bitcast.99), channel_id=1, source_target_pairs={{0,64},{32,96},{64,0},{96,32},{1,65},{33,97},{65,1},{97,33},{2,66}... | collective-permute-start | bytes 491528 | tf_op jit(solution)/shard_map/ppermute | solution.py:263
  123.6 7.5 %copy-start.4 = (f32[1280]{0:T(1024)S(1)}, f32[1280]{0:T(1024)}, u32[]{:S(2)}) copy-start(f32[1280]{0:T(1024)} %param.9) | copy-start | bytes 15364
  123.9 15.2 %collective-permute-start.17 = (bf16[4,1,64,1280]{3,2,1,0:T(8,128)(2,1)S(1)}, bf16[4,1,64,1280]{3,2,1,0:T(8,128)(2,1)S(1)}, u32[]{:S(2)}, u32[]{:S(2)}) collective-permute-start(bf16[4,1,64,1280]{3,2,1,0:T(8,128)(2,1)S(1)} %get-tuple-element.26), channel_id=1, source_target_pairs={{1,2},{2,1},{3,4},{4,3},{5,6},{6,5},{7,8},{8,7},{9,10},{10,9},{11,... | collective-permute-start | bytes 1966088 | tf_op jit(solution)/shard_map/ppermute | solution.py:279
  130.8 8.3 %collective-permute-start.18 = (bf16[4,1,64,1280]{3,2,1,0:T(8,128)(2,1)S(1)}, bf16[4,1,64,1280]{3,2,1,0:T(8,128)(2,1)S(1)}, u32[]{:S(2)}, u32[]{:S(2)}) collective-permute-start(bf16[4,1,64,1280]{3,2,1,0:T(8,128)(2,1)S(1)} %get-tuple-element.27), channel_id=1, source_target_pairs={{0,1},{1,0},{2,3},{3,2},{4,5},{5,4},{6,7},{7,6},{8,9},{9,8},{10,11... | collective-permute-start | bytes 1966088 | tf_op jit(solution)/shard_map/ppermute | solution.py:277
  (1 other events, 0.8 us)
Sparse Core Ops, SparseCore 0:
  23.8 69.8 all-gather.1

commit v9 on v8

--- a/solution.py
+++ b/solution.py
@@ -74,9 +74,10 @@
                     tiles[tile] = jnp.where(lanes < h * head_size, tiles[tile], got)
 
     all_scores = [score(*window) for window in windows]
+    yield
     for window, scores in zip(windows, all_scores):
         gather(*window, scores)
-    return jnp.concatenate(tiles, axis=1).astype(BF16)
+    yield jnp.concatenate(tiles, axis=1).astype(BF16)
 
 
 def weight_copies(w_hbm, core, target, sem):
@@ -110,17 +111,17 @@
         shape = (8, take, part, half)
         return q.reshape(4, *shape[1:]), kv[:, :half].reshape(shape), kv[:, half:].reshape(shape)
 
-    def attend(turn, q, k, v):
-        for i in range(take):
-            got = attend_rows(*(m[:, i].reshape(-1, half) for m in (q, k, v)), head_size)
-            out[:, turn * take + i] = got.reshape(4, -1, half)
+    def begin(q, k, v):
+        steps = attend_rows(*(m.reshape(-1, half) for m in (q, k, v)), head_size)
+        next(steps)
+        return steps
 
     ready(0)
-    held = project(0)
+    steps = begin(*project(0))
     for turn in range(turns):
-        after = project(turn + 1) if turn + 1 < turns else None
-        attend(turn, *held)
-        held = after
+        after = begin(*project(turn + 1)) if turn + 1 < turns else None
+        out[:, turn] = next(steps).reshape(4, -1, half)
+        steps = after
 
 
 def first_kernel(head_size, x_ref, w_hbm, out, w_next, w_home, w_vm, *sems):
@@ -211,10 +212,11 @@
     rows, width = w_out.shape
     half = width // 2
     x, zl, core = lax.axis_index("x"), lax.axis_index("zl"), lax.axis_index("c")
-    parts = [w_qkv[:, i * width : (i + 1) * width] for i in range(3)] + [w_out]
-    mine = lax.select_n(x, *parts)
-    keep = jnp.where(core == 0, mine[:, :half], mine[:, half:])
-    give = jnp.where(core == 0, mine[:, half:], mine[:, :half])
+    def columns(at):
+        inner = lax.dynamic_slice_in_dim(w_qkv, jnp.minimum(x, 2) * width + at * half, half, 1)
+        return jnp.where(x == 3, lax.dynamic_slice_in_dim(w_out, at * half, half, 1), inner)
+
+    keep, give = columns(core), columns(1 - core)
     other = lax.ppermute(give, "c", ring(2, 1))
     piece = jnp.where(
         core == 0, jnp.concatenate([keep, other]), jnp.concatenate([other, keep])

time: 151 us -> 150 us (level)
  no operation moved by 1% of the time
where the time goes in v9:
time: 150 us; the launch traced here: 148 us
  waiting for transfers between devices  69.1 us (46%)
  starting transfers between devices  33.4 us (22%)
  Pallas kernels  14.4 us (10%)
  between operations  13.8 us (9%)
  local copies, waits for them, and re-layouts  9.03 us (6%)
  other arithmetic  5.97 us (4%)
  matrix products  2.42 us (2%)
    ppermute x4, waiting for transfers between devices, shards(): partner = [lax.ppermute(block, ('zh', 'zl'), ring(8, 4)) for block in own]  42.9 us
    ppermute x4, starting transfers between devices, shards(): partner = [lax.ppermute(block, ('zh', 'zl'), ring(8, 4)) for block in own]  8.65 us
    pallas_call x1, Pallas kernels, run_halves(): pl.pallas_call(functools.partial(first_kernel, head_size), out_shape=(att...  8.39 us
    ppermute x3, waiting for transfers between devices, gather_weights(): got = lax.ppermute(piece, ('zh', 'zl'), moves)  7.03 us
    ppermute x1, starting transfers between devices, shards(): far = lax.ppermute(jnp.where(core == 0, first, last), axes, across)  6.91 us
    ppermute x6, starting transfers between devices, shards(): back = lax.ppermute(back, 'x', pairs(4, m))  6.67 us
    ppermute x3, starting transfers between devices, gather_weights(): got = lax.ppermute(piece, ('zh', 'zl'), moves)  6.39 us
    ppermute x1, waiting for transfers between devices, shards(): far = lax.ppermute(jnp.where(core == 0, first, last), axes, across)  5.98 us
  transfers between devices with their start and end apart: 20, of which 13 were waited for; matrix products, arithmetic and copies ran while one was open for 7% of the time, Pallas kernels for 4%

profile of v9, /device:TPU:25, one launch (start us, length us, event | category | flops | bytes accessed | tf_op | source)
XLA Modules:
  0.0 148.1 jit_solution(12923231319272072336)
XLA Ops:
  9.2 1.7 %collective-permute-start.8 = (bf16[80,640]{1,0:T(8,128)(2,1)S(1)}, bf16[80,640]{1,0:T(8,128)(2,1)S(1)}, u32[]{:S(2)}, u32[]{:S(2)}) collective-permute-start(bf16[80,640]{1,0:T(8,128)(2,1)S(1)} %maximum_select_fusion.1), channel_id=1, source_target_pairs={{0,8},{8,0},{16,24},{24,16},{128,136},{136,128},{144,152},{152,144... | collective-permute-start | bytes 307208 | tf_op jit(solution)/shard_map/ppermute | solution.py:232
  10.9 4.7 %collective-permute-start.9 = (bf16[80,640]{1,0:T(8,128)(2,1)S(1)}, bf16[80,640]{1,0:T(8,128)(2,1)S(1)}, u32[]{:S(2)}, u32[]{:S(2)}) collective-permute-start(bf16[80,640]{1,0:T(8,128)(2,1)S(1)} %maximum_select_fusion.1), channel_id=1, source_target_pairs={{0,152},{8,16},{16,8},{24,128},{128,24},{136,144},{144,136},{152,0... | collective-permute-start | bytes 307208 | tf_op jit(solution)/shard_map/ppermute | solution.py:232
  15.7 2.5 %collective-permute-done.9 = bf16[80,640]{1,0:T(8,128)(2,1)S(1)} collective-permute-done((bf16[80,640]{1,0:T(8,128)(2,1)S(1)}, bf16[80,640]{1,0:T(8,128)(2,1)S(1)}, u32[]{:S(2)}, u32[]{:S(2)}) %collective-permute-start.9) | collective-permute-done | bytes 102432 | tf_op jit(solution)/shard_map/ppermute | solution.py:232
  18.3 4.5 %collective-permute-done.10 = bf16[80,640]{1,0:T(8,128)(2,1)S(1)} collective-permute-done((bf16[80,640]{1,0:T(8,128)(2,1)S(1)}, bf16[80,640]{1,0:T(8,128)(2,1)S(1)}, u32[]{:S(2)}, u32[]{:S(2)}) %collective-permute-start.10) | collective-permute-done | bytes 102432 | tf_op jit(solution)/shard_map/ppermute | solution.py:232
  26.4 1.8 %collective-permute-start.1 = (bf16[128,1280]{1,0:T(8,128)(2,1)}, bf16[128,1280]{1,0:T(8,128)(2,1)}, u32[]{:S(2)}, u32[]{:S(2)}) collective-permute-start(bf16[128,1280]{1,0:T(8,128)(2,1)} %bitcast.11), channel_id=1, source_target_pairs={{0,96},{32,64},{64,32},{96,0},{1,97},{33,65},{65,33},{97,1},{2,98}... | collective-permute-start | bytes 983048 | tf_op jit(solution)/shard_map/ppermute | solution.py:250
  29.7 2.6 %collective-permute-start.3 = (bf16[128,1280]{1,0:T(8,128)(2,1)S(1)}, bf16[128,1280]{1,0:T(8,128)(2,1)}, u32[]{:S(2)}, u32[]{:S(2)}) collective-permute-start(bf16[128,1280]{1,0:T(8,128)(2,1)S(1)} %bitcast.92), channel_id=1, source_target_pairs={{0,128},{8,136},{16,144},{24,152},{128,0},{136,8},{144,16},{152,24... | collective-permute-start | bytes 983048 | tf_op jit(solution)/shard_map/ppermute | solution.py:251
  32.3 1.8 %copy.13 = f32[4,4,4,8,1280]{4,3,0,2,1:T(8,128)} copy(bf16[4,4,4,8,1280]{4,3,2,1,0:T(8,128)(2,1)S(1)} %bitcast.89) | data formatting | bytes 3932160 | tf_op jit(solution)/shard_map/convert_element_type | solution.py:258
  34.3 2.9 %collective-permute-start.4 = (bf16[128,1280]{1,0:T(8,128)(2,1)}, bf16[128,1280]{1,0:T(8,128)(2,1)S(1)}, u32[]{:S(2)}, u32[]{:S(2)}) collective-permute-start(bf16[128,1280]{1,0:T(8,128)(2,1)} %collective-permute-done), channel_id=1, source_target_pairs={{0,128},{8,136},{16,144},{24,152},{128,0},{136,8},{144,16},{152,24... | collective-permute-start | bytes 983048 | tf_op jit(solution)/shard_map/ppermute | solution.py:251
  38.2 3.3 %collective-permute-done.1 = bf16[128,1280]{1,0:T(8,128)(2,1)} collective-permute-done((bf16[128,1280]{1,0:T(8,128)(2,1)}, bf16[128,1280]{1,0:T(8,128)(2,1)}, u32[]{:S(2)}, u32[]{:S(2)}) %collective-permute-start.1) | collective-permute-done | bytes 327712 | tf_op jit(solution)/shard_map/ppermute | solution.py:250
  42.6 2.5 %collective-permute-done.2 = bf16[128,1280]{1,0:T(8,128)(2,1)S(1)} collective-permute-done((bf16[128,1280]{1,0:T(8,128)(2,1)}, bf16[128,1280]{1,0:T(8,128)(2,1)S(1)}, u32[]{:S(2)}, u32[]{:S(2)}) %collective-permute-start.2) | collective-permute-done | bytes 327712 | tf_op jit(solution)/shard_map/ppermute | solution.py:250
  45.1 3.1 %collective-permute-start.6 = (bf16[128,1280]{1,0:T(8,128)(2,1)S(1)}, bf16[128,1280]{1,0:T(8,128)(2,1)S(1)}, u32[]{:S(2)}, u32[]{:S(2)}) collective-permute-start(bf16[128,1280]{1,0:T(8,128)(2,1)S(1)} %collective-permute-done.2), channel_id=1, source_target_pairs={{0,128},{8,136},{16,144},{24,152},{128,0},{136,8},{144,16},{152,24... | collective-permute-start | bytes 983048 | tf_op jit(solution)/shard_map/ppermute | solution.py:251
  48.2 23.0 %collective-permute-done.3 = bf16[128,1280]{1,0:T(8,128)(2,1)} collective-permute-done((bf16[128,1280]{1,0:T(8,128)(2,1)S(1)}, bf16[128,1280]{1,0:T(8,128)(2,1)}, u32[]{:S(2)}, u32[]{:S(2)}) %collective-permute-start.3) | collective-permute-done | bytes 327712 | tf_op jit(solution)/shard_map/ppermute | solution.py:251
  72.2 5.9 %collective-permute-done.4 = bf16[128,1280]{1,0:T(8,128)(2,1)S(1)} collective-permute-done((bf16[128,1280]{1,0:T(8,128)(2,1)}, bf16[128,1280]{1,0:T(8,128)(2,1)S(1)}, u32[]{:S(2)}, u32[]{:S(2)}) %collective-permute-start.4) | collective-permute-done | bytes 327712 | tf_op jit(solution)/shard_map/ppermute | solution.py:251
  78.1 7.0 %collective-permute-done.5 = bf16[128,1280]{1,0:T(8,128)(2,1)S(1)} collective-permute-done((bf16[128,1280]{1,0:T(8,128)(2,1)}, bf16[128,1280]{1,0:T(8,128)(2,1)S(1)}, u32[]{:S(2)}, u32[]{:S(2)}) %collective-permute-start.5) | collective-permute-done | bytes 327712 | tf_op jit(solution)/shard_map/ppermute | solution.py:251
  85.2 7.0 %collective-permute-done.6 = bf16[128,1280]{1,0:T(8,128)(2,1)S(1)} collective-permute-done((bf16[128,1280]{1,0:T(8,128)(2,1)S(1)}, bf16[128,1280]{1,0:T(8,128)(2,1)S(1)}, u32[]{:S(2)}, u32[]{:S(2)}) %collective-permute-start.6) | collective-permute-done | bytes 327712 | tf_op jit(solution)/shard_map/ppermute | solution.py:251
  93.6 8.4 %shard_map.55 = (bf16[4,4,32,640]{3,2,1,0:T(8,128)(2,1)S(1)}, bf16[4,4,80,1920]{3,2,1,0:T(8,128)(2,1)S(1)}, bf16[4,4,80,1280]{3,2,1,0:T(8,128)(2,1)S(1)}) custom-call(bf16[1024,1280]{1,0:T(8,128)(2,1)S(1)} %constant_dynamic-update-slice_fusion.x_ref, bf16[4,4,2,4,80,640]{5,4,3,2,1,0:T(8,128)(2,1)} %bitcast.84), custom_call_target="tpu_custom_call" | custom-call | flops 4194304000 | bytes 6553600 | tf_op jit(solution)/shard_map/pallas_call | solution.py:170
  103.6 1.8 %collective-permute-start.13 = (bf16[128,640]{1,0:T(8,128)(2,1)S(1)}, bf16[128,640]{1,0:T(8,128)(2,1)S(1)}, u32[]{:S(2)}, u32[]{:S(2)}) collective-permute-start(bf16[128,640]{1,0:T(8,128)(2,1)S(1)} %bitcast.98), channel_id=1, source_target_pairs={{0,64},{32,96},{64,0},{96,32},{1,65},{33,97},{65,1},{97,33},{2,66}... | collective-permute-start | bytes 491528 | tf_op jit(solution)/shard_map/ppermute | solution.py:265
  105.6 6.0 %shard_map.56 = bf16[4,4,32,640]{3,2,1,0:T(8,128)(2,1)S(1)} custom-call(bf16[1024,1280]{1,0:T(8,128)(2,1)S(1)} %constant_dynamic-update-slice_fusion.x_ref, bf16[4,4,80,1920]{3,2,1,0:T(8,128)(2,1)S(1)} %get-tuple-element.13.w_ref), custom_call_target="tpu_custom_call" | custom-call | flops 1048576 | bytes 4096 | tf_op jit(solution)/shard_map/pallas_call | solution.py:188
  112.1 1.8 %collective-permute-start.15 = (bf16[128,640]{1,0:T(8,128)(2,1)S(1)}, bf16[128,640]{1,0:T(8,128)(2,1)S(1)}, u32[]{:S(2)}, u32[]{:S(2)}) collective-permute-start(bf16[128,640]{1,0:T(8,128)(2,1)S(1)} %bitcast.101), channel_id=1, source_target_pairs={{0,96},{32,64},{64,32},{96,0},{1,97},{33,65},{65,33},{97,1},{2,98}... | collective-permute-start | bytes 491528 | tf_op jit(solution)/shard_map/ppermute | solution.py:265
  117.5 4.1 %collective-permute-done.16 = bf16[128,640]{1,0:T(8,128)(2,1)S(1)} collective-permute-done((bf16[128,640]{1,0:T(8,128)(2,1)S(1)}, bf16[128,640]{1,0:T(8,128)(2,1)S(1)}, u32[]{:S(2)}, u32[]{:S(2)}) %collective-permute-start.16) | collective-permute-done | bytes 163872 | tf_op jit(solution)/shard_map/ppermute | solution.py:265
  123.6 6.9 %collective-permute-start.17 = (bf16[4,1,64,1280]{3,2,1,0:T(8,128)(2,1)S(1)}, bf16[4,1,64,1280]{3,2,1,0:T(8,128)(2,1)S(1)}, u32[]{:S(2)}, u32[]{:S(2)}) collective-permute-start(bf16[4,1,64,1280]{3,2,1,0:T(8,128)(2,1)S(1)} %get-tuple-element.26), channel_id=1, source_target_pairs={{1,2},{2,1},{3,4},{4,3},{5,6},{6,5},{7,8},{8,7},{9,10},{10,9},{11,... | collective-permute-start | bytes 1966088 | tf_op jit(solution)/shard_map/ppermute | solution.py:281
  130.9 1.9 %fusion.5 = f32[4,2,64,1280]{3,2,1,0:T(8,128)S(1)} fusion(f32[4,2,64,1280]{3,2,1,0:T(8,128)S(1)} %convert_element_type.37, f32[4,2,64,1280]{3,2,1,0:T(8,128)S(1)} %reverse_convert_fusion, f32[2,1280]{1,0:T(2,128)S(1)} %get-tuple-element.52, f32[2,1280]{1,0:T(2,128)S(1)} %get-tuple-element.53, f32[2,1280]{1,0:T(2,128)S(1)} %bitcast.105, ...), kind=kLoop, calls=%fused_computation.13 | loop fusion | flops 8519680 | bytes 7915520 | tf_op jit(solution)/shard_map/add | solution.py:291
  132.8 6.0 %collective-permute-done.17 = bf16[4,1,64,1280]{3,2,1,0:T(8,128)(2,1)S(1)} collective-permute-done((bf16[4,1,64,1280]{3,2,1,0:T(8,128)(2,1)S(1)}, bf16[4,1,64,1280]{3,2,1,0:T(8,128)(2,1)S(1)}, u32[]{:S(2)}, u32[]{:S(2)}) %collective-permute-start.17) | collective-permute-done | bytes 655392 | tf_op jit(solution)/shard_map/ppermute | solution.py:281
  139.3 2.0 %fusion.15 = bf16[4,2,64,1280]{3,2,1,0:T(8,128)(2,1)} fusion(f32[4,2,64,1280]{3,2,1,0:T(8,128)S(1)} %fusion.5, f32[4,2,64,1280]{3,2,1,0:T(8,128)S(1)} %convert_element_type.39, f32[2,1280]{1,0:T(2,128)S(1)} %get-tuple-element.50, f32[2,1280]{1,0:T(2,128)S(1)} %get-tuple-element.51, f32[2,1280]{1,0:T(2,128)S(1)} %bitcast.104), kind=kLoop, calls=%fused_computation.23 | loop fusion | flops 4587520 | bytes 6584320 | tf_op jit(solution)/shard_map/convert_element_type | solution.py:294
  (81 shorter events, 21.0 us)
Async XLA Ops:
  6.5 17.1 %copy-start.1 = (bf16[4,128,1280]{2,1,0:T(8,128)(2,1)S(1)}, bf16[4,128,1280]{2,1,0:T(8,128)(2,1)}, u32[]{:S(2)}) copy-start(bf16[4,128,1280]{2,1,0:T(8,128)(2,1)} %param.5) | copy-start | bytes 3932164
  6.5 87.1 %all-gather.2.cloned.1.call-start = ((), (), s32[]{:S(2)}) async-start(), calls=%async_computation | async-start | bytes 13516800 | tf_op jit(solution)/shard_map/all_gather | solution.py:234
  7.6 1.6 %collective-permute-start.7 = (bf16[40,640]{1,0:T(8,128)(2,1)S(1)}, bf16[40,640]{1,0:T(8,128)(2,1)S(1)}, u32[]{:S(2)}, u32[]{:S(2)}) collective-permute-start(bf16[40,640]{1,0:T(8,128)(2,1)S(1)} %get-tuple-element.41), channel_id=1, source_target_pairs={{0,1},{1,0},{2,3},{3,2},{4,5},{5,4},{6,7},{7,6},{8,9},{9,8},{10,11... | collective-permute-start | bytes 153608 | tf_op jit(solution)/shard_map/ppermute | solution.py:220
  9.2 6.5 %collective-permute-start.8 = (bf16[80,640]{1,0:T(8,128)(2,1)S(1)}, bf16[80,640]{1,0:T(8,128)(2,1)S(1)}, u32[]{:S(2)}, u32[]{:S(2)}) collective-permute-start(bf16[80,640]{1,0:T(8,128)(2,1)S(1)} %maximum_select_fusion.1), channel_id=1, source_target_pairs={{0,8},{8,0},{16,24},{24,16},{128,136},{136,128},{144,152},{152,144... | collective-permute-start | bytes 307208 | tf_op jit(solution)/shard_map/ppermute | solution.py:232
  10.9 7.3 %collective-permute-start.9 = (bf16[80,640]{1,0:T(8,128)(2,1)S(1)}, bf16[80,640]{1,0:T(8,128)(2,1)S(1)}, u32[]{:S(2)}, u32[]{:S(2)}) collective-permute-start(bf16[80,640]{1,0:T(8,128)(2,1)S(1)} %maximum_select_fusion.1), channel_id=1, source_target_pairs={{0,152},{8,16},{16,8},{24,128},{128,24},{136,144},{144,136},{152,0... | collective-permute-start | bytes 307208 | tf_op jit(solution)/shard_map/ppermute | solution.py:232
  15.6 7.2 %collective-permute-start.10 = (bf16[80,640]{1,0:T(8,128)(2,1)S(1)}, bf16[80,640]{1,0:T(8,128)(2,1)S(1)}, u32[]{:S(2)}, u32[]{:S(2)}) collective-permute-start(bf16[80,640]{1,0:T(8,128)(2,1)S(1)} %maximum_select_fusion.1), channel_id=1, source_target_pairs={{0,16},{8,24},{16,0},{24,8},{128,144},{136,152},{144,128},{152,136... | collective-permute-start | bytes 307208 | tf_op jit(solution)/shard_map/ppermute | solution.py:232
  24.5 9.8 %collective-permute-start = (bf16[128,1280]{1,0:T(8,128)(2,1)}, bf16[128,1280]{1,0:T(8,128)(2,1)}, u32[]{:S(2)}, u32[]{:S(2)}) collective-permute-start(bf16[128,1280]{1,0:T(8,128)(2,1)} %bitcast.8), channel_id=1, source_target_pairs={{0,32},{32,0},{64,96},{96,64},{1,33},{33,1},{65,97},{97,65},{2,34}... | collective-permute-start | bytes 983048 | tf_op jit(solution)/shard_map/ppermute | solution.py:250
  26.4 15.1 %collective-permute-start.1 = (bf16[128,1280]{1,0:T(8,128)(2,1)}, bf16[128,1280]{1,0:T(8,128)(2,1)}, u32[]{:S(2)}, u32[]{:S(2)}) collective-permute-start(bf16[128,1280]{1,0:T(8,128)(2,1)} %bitcast.11), channel_id=1, source_target_pairs={{0,96},{32,64},{64,32},{96,0},{1,97},{33,65},{65,33},{97,1},{2,98}... | collective-permute-start | bytes 983048 | tf_op jit(solution)/shard_map/ppermute | solution.py:250
  28.2 5.8 %copy-start.3 = (f32[3,3,1280]{2,1,0:T(4,128)S(1)}, f32[3,3,1280]{2,1,0:T(4,128)}, u32[]{:S(2)}) copy-start(f32[3,3,1280]{2,1,0:T(4,128)} %param.8) | copy-start | bytes 138244
  29.0 16.1 %collective-permute-start.2 = (bf16[128,1280]{1,0:T(8,128)(2,1)}, bf16[128,1280]{1,0:T(8,128)(2,1)S(1)}, u32[]{:S(2)}, u32[]{:S(2)}) collective-permute-start(bf16[128,1280]{1,0:T(8,128)(2,1)} %bitcast.14), channel_id=1, source_target_pairs={{0,64},{32,96},{64,0},{96,32},{1,65},{33,97},{65,1},{97,33},{2,66}... | collective-permute-start | bytes 983048 | tf_op jit(solution)/shard_map/ppermute | solution.py:250
  29.7 41.5 %collective-permute-start.3 = (bf16[128,1280]{1,0:T(8,128)(2,1)S(1)}, bf16[128,1280]{1,0:T(8,128)(2,1)}, u32[]{:S(2)}, u32[]{:S(2)}) collective-permute-start(bf16[128,1280]{1,0:T(8,128)(2,1)S(1)} %bitcast.92), channel_id=1, source_target_pairs={{0,128},{8,136},{16,144},{24,152},{128,0},{136,8},{144,16},{152,24... | collective-permute-start | bytes 983048 | tf_op jit(solution)/shard_map/ppermute | solution.py:251
  34.3 43.8 %collective-permute-start.4 = (bf16[128,1280]{1,0:T(8,128)(2,1)}, bf16[128,1280]{1,0:T(8,128)(2,1)S(1)}, u32[]{:S(2)}, u32[]{:S(2)}) collective-permute-start(bf16[128,1280]{1,0:T(8,128)(2,1)} %collective-permute-done), channel_id=1, source_target_pairs={{0,128},{8,136},{16,144},{24,152},{128,0},{136,8},{144,16},{152,24... | collective-permute-start | bytes 983048 | tf_op jit(solution)/shard_map/ppermute | solution.py:251
  41.5 43.6 %collective-permute-start.5 = (bf16[128,1280]{1,0:T(8,128)(2,1)}, bf16[128,1280]{1,0:T(8,128)(2,1)S(1)}, u32[]{:S(2)}, u32[]{:S(2)}) collective-permute-start(bf16[128,1280]{1,0:T(8,128)(2,1)} %collective-permute-done.1), channel_id=1, source_target_pairs={{0,128},{8,136},{16,144},{24,152},{128,0},{136,8},{144,16},{152,24... | collective-permute-start | bytes 983048 | tf_op jit(solution)/shard_map/ppermute | solution.py:251
  45.1 47.0 %collective-permute-start.6 = (bf16[128,1280]{1,0:T(8,128)(2,1)S(1)}, bf16[128,1280]{1,0:T(8,128)(2,1)S(1)}, u32[]{:S(2)}, u32[]{:S(2)}) collective-permute-start(bf16[128,1280]{1,0:T(8,128)(2,1)S(1)} %collective-permute-done.2), channel_id=1, source_target_pairs={{0,128},{8,136},{16,144},{24,152},{128,0},{136,8},{144,16},{152,24... | collective-permute-start | bytes 983048 | tf_op jit(solution)/shard_map/ppermute | solution.py:251
  102.1 9.7 %collective-permute-start.11 = (bf16[128,640]{1,0:T(8,128)(2,1)S(1)}, bf16[128,640]{1,0:T(8,128)(2,1)S(1)}, u32[]{:S(2)}, u32[]{:S(2)}) collective-permute-start(bf16[128,640]{1,0:T(8,128)(2,1)S(1)} %bitcast.102), channel_id=1, source_target_pairs={{0,32},{32,0},{64,96},{96,64},{1,33},{33,1},{65,97},{97,65},{2,34}... | collective-permute-start | bytes 491528 | tf_op jit(solution)/shard_map/ppermute | solution.py:265
  102.2 9.6 %collective-permute-start.12 = (bf16[128,640]{1,0:T(8,128)(2,1)S(1)}, bf16[128,640]{1,0:T(8,128)(2,1)S(1)}, u32[]{:S(2)}, u32[]{:S(2)}) collective-permute-start(bf16[128,640]{1,0:T(8,128)(2,1)S(1)} %bitcast.100), channel_id=1, source_target_pairs={{0,96},{32,64},{64,32},{96,0},{1,97},{33,65},{65,33},{97,1},{2,98}... | collective-permute-start | bytes 491528 | tf_op jit(solution)/shard_map/ppermute | solution.py:265
  103.6 8.2 %collective-permute-start.13 = (bf16[128,640]{1,0:T(8,128)(2,1)S(1)}, bf16[128,640]{1,0:T(8,128)(2,1)S(1)}, u32[]{:S(2)}, u32[]{:S(2)}) collective-permute-start(bf16[128,640]{1,0:T(8,128)(2,1)S(1)} %bitcast.98), channel_id=1, source_target_pairs={{0,64},{32,96},{64,0},{96,32},{1,65},{33,97},{65,1},{97,33},{2,66}... | collective-permute-start | bytes 491528 | tf_op jit(solution)/shard_map/ppermute | solution.py:265
  111.6 3.7 %copy-start = (f32[4,4,4,8,1280]{4,3,0,2,1:T(8,128)S(1)}, f32[4,4,4,8,1280]{4,3,0,2,1:T(8,128)}, u32[]{:S(2)}) copy-start(f32[4,4,4,8,1280]{4,3,0,2,1:T(8,128)} %copy.13) | copy-start | bytes 7864324
  111.9 4.7 %collective-permute-start.14 = (bf16[128,640]{1,0:T(8,128)(2,1)S(1)}, bf16[128,640]{1,0:T(8,128)(2,1)S(1)}, u32[]{:S(2)}, u32[]{:S(2)}) collective-permute-start(bf16[128,640]{1,0:T(8,128)(2,1)S(1)} %bitcast.103), channel_id=1, source_target_pairs={{0,32},{32,0},{64,96},{96,64},{1,33},{33,1},{65,97},{97,65},{2,34}... | collective-permute-start | bytes 491528 | tf_op jit(solution)/shard_map/ppermute | solution.py:265
  112.1 5.4 %collective-permute-start.15 = (bf16[128,640]{1,0:T(8,128)(2,1)S(1)}, bf16[128,640]{1,0:T(8,128)(2,1)S(1)}, u32[]{:S(2)}, u32[]{:S(2)}) collective-permute-start(bf16[128,640]{1,0:T(8,128)(2,1)S(1)} %bitcast.101), channel_id=1, source_target_pairs={{0,96},{32,64},{64,32},{96,0},{1,97},{33,65},{65,33},{97,1},{2,98}... | collective-permute-start | bytes 491528 | tf_op jit(solution)/shard_map/ppermute | solution.py:265
  113.9 7.7 %collective-permute-start.16 = (bf16[128,640]{1,0:T(8,128)(2,1)S(1)}, bf16[128,640]{1,0:T(8,128)(2,1)S(1)}, u32[]{:S(2)}, u32[]{:S(2)}) collective-permute-start(bf16[128,640]{1,0:T(8,128)(2,1)S(1)} %bitcast.99), channel_id=1, source_target_pairs={{0,64},{32,96},{64,0},{96,32},{1,65},{33,97},{65,1},{97,33},{2,66}... | collective-permute-start | bytes 491528 | tf_op jit(solution)/shard_map/ppermute | solution.py:265
  123.4 7.5 %copy-start.4 = (f32[1280]{0:T(1024)S(1)}, f32[1280]{0:T(1024)}, u32[]{:S(2)}) copy-start(f32[1280]{0:T(1024)} %param.9) | copy-start | bytes 15364
  123.6 15.2 %collective-permute-start.17 = (bf16[4,1,64,1280]{3,2,1,0:T(8,128)(2,1)S(1)}, bf16[4,1,64,1280]{3,2,1,0:T(8,128)(2,1)S(1)}, u32[]{:S(2)}, u32[]{:S(2)}) collective-permute-start(bf16[4,1,64,1280]{3,2,1,0:T(8,128)(2,1)S(1)} %get-tuple-element.26), channel_id=1, source_target_pairs={{1,2},{2,1},{3,4},{4,3},{5,6},{6,5},{7,8},{8,7},{9,10},{10,9},{11,... | collective-permute-start | bytes 1966088 | tf_op jit(solution)/shard_map/ppermute | solution.py:281
  130.6 8.3 %collective-permute-start.18 = (bf16[4,1,64,1280]{3,2,1,0:T(8,128)(2,1)S(1)}, bf16[4,1,64,1280]{3,2,1,0:T(8,128)(2,1)S(1)}, u32[]{:S(2)}, u32[]{:S(2)}) collective-permute-start(bf16[4,1,64,1280]{3,2,1,0:T(8,128)(2,1)S(1)} %get-tuple-element.27), channel_id=1, source_target_pairs={{0,1},{1,0},{2,3},{3,2},{4,5},{5,4},{6,7},{7,6},{8,9},{9,8},{10,11... | collective-permute-start | bytes 1966088 | tf_op jit(solution)/shard_map/ppermute | solution.py:279
  (1 other events, 0.8 us)
Sparse Core Ops, SparseCore 0:
  23.7 69.8 all-gather.1

commit v10 on v9

--- a/solution.py
+++ b/solution.py
@@ -246,7 +246,7 @@
         block = block.reshape(date_dev, part // GROUP, GROUP, width).transpose(1, 0, 2, 3)
         return block.reshape(date_dev * part, width)
 
-    masks = (0, 1, 3, 2)
+    masks = (0, 2, 1, 3)
     own = [cut(0)] + [lax.ppermute(cut(m), "x", pairs(4, m)) for m in masks[1:]]
     partner = [lax.ppermute(block, ("zh", "zl"), ring(8, 4)) for block in own]
     w_all = gather_weights(w_qkv, w_out)

time: 150 us -> 150 us (level); the launches traced: 148 us -> 150 us
  waiting for transfers between devices: 69.1 us -> 72.1 us
    ppermute x4, waiting for transfers between devices: 42.9 us -> 38.9 us  [shards(): partner = [lax.ppermute(block, ('zh', 'zl'), ring(8, 4)) for block in own]]
    ppermute x6, waiting for transfers between devices: 5.03 us -> 8.01 us  [shards(): back = lax.ppermute(back, 'x', pairs(4, m))]
    ppermute x1, starting transfers between devices: 6.91 us -> 3.96 us  [shards(): far = lax.ppermute(jnp.where(core == 0, first, last), axes, across)]
    ppermute x3, waiting for transfers between devices: 5.84 us -> 8.21 us  [shards(): own = [cut(0)] + [lax.ppermute(cut(m), 'x', pairs(4, m)) for m in masks[1:]]]
    ppermute x1, waiting for transfers between devices: 5.98 us -> 7.77 us  [shards(): far = lax.ppermute(jnp.where(core == 0, first, last), axes, across)]
    ppermute x4, starting transfers between devices: 8.65 us -> 10.3 us  [shards(): partner = [lax.ppermute(block, ('zh', 'zl'), ring(8, 4)) for block in own]]
  transfers between devices with their start and end apart: 20 -> 20, of which waited for: 13 -> 15; matrix products, arithmetic and copies ran while one was open for 7% -> 7% of each run, Pallas kernels for 4% -> 4%
where the time goes in v10:
time: 150 us
  waiting for transfers between devices  72.1 us (48%)
  starting transfers between devices  32 us (21%)
  Pallas kernels  14.4 us (10%)
  between operations  13.8 us (9%)
  local copies, waits for them, and re-layouts  9.02 us (6%)
  other arithmetic  5.97 us (4%)
  matrix products  2.42 us (2%)
    ppermute x4, waiting for transfers between devices, shards(): partner = [lax.ppermute(block, ('zh', 'zl'), ring(8, 4)) for block in own]  38.9 us
    ppermute x4, starting transfers between devices, shards(): partner = [lax.ppermute(block, ('zh', 'zl'), ring(8, 4)) for block in own]  10.3 us
    pallas_call x1, Pallas kernels, run_halves(): pl.pallas_call(functools.partial(first_kernel, head_size), out_shape=(att...  8.39 us
    ppermute x3, waiting for transfers between devices, shards(): own = [cut(0)] + [lax.ppermute(cut(m), 'x', pairs(4, m)) for m in masks[1:]]  8.21 us
    ppermute x6, waiting for transfers between devices, shards(): back = lax.ppermute(back, 'x', pairs(4, m))  8.01 us
    ppermute x1, waiting for transfers between devices, shards(): far = lax.ppermute(jnp.where(core == 0, first, last), axes, across)  7.77 us
    ppermute x3, waiting for transfers between devices, gather_weights(): got = lax.ppermute(piece, ('zh', 'zl'), moves)  7.03 us
    ppermute x6, starting transfers between devices, shards(): back = lax.ppermute(back, 'x', pairs(4, m))  6.68 us
  transfers between devices with their start and end apart: 20, of which 15 were waited for; matrix products, arithmetic and copies ran while one was open for 7% of the time, Pallas kernels for 4%

profile of v10, /device:TPU:25, one launch (start us, length us, event | category | flops | bytes accessed | tf_op | source)
XLA Modules:
  0.0 149.7 jit_solution(11014080505676654791)
XLA Ops:
  9.2 1.7 %collective-permute-start.8 = (bf16[80,640]{1,0:T(8,128)(2,1)S(1)}, bf16[80,640]{1,0:T(8,128)(2,1)S(1)}, u32[]{:S(2)}, u32[]{:S(2)}) collective-permute-start(bf16[80,640]{1,0:T(8,128)(2,1)S(1)} %maximum_select_fusion.1), channel_id=1, source_target_pairs={{0,8},{8,0},{16,24},{24,16},{128,136},{136,128},{144,152},{152,144... | collective-permute-start | bytes 307208 | tf_op jit(solution)/shard_map/ppermute | solution.py:232
  10.9 4.7 %collective-permute-start.9 = (bf16[80,640]{1,0:T(8,128)(2,1)S(1)}, bf16[80,640]{1,0:T(8,128)(2,1)S(1)}, u32[]{:S(2)}, u32[]{:S(2)}) collective-permute-start(bf16[80,640]{1,0:T(8,128)(2,1)S(1)} %maximum_select_fusion.1), channel_id=1, source_target_pairs={{0,152},{8,16},{16,8},{24,128},{128,24},{136,144},{144,136},{152,0... | collective-permute-start | bytes 307208 | tf_op jit(solution)/shard_map/ppermute | solution.py:232
  15.7 2.5 %collective-permute-done.9 = bf16[80,640]{1,0:T(8,128)(2,1)S(1)} collective-permute-done((bf16[80,640]{1,0:T(8,128)(2,1)S(1)}, bf16[80,640]{1,0:T(8,128)(2,1)S(1)}, u32[]{:S(2)}, u32[]{:S(2)}) %collective-permute-start.9) | collective-permute-done | bytes 102432 | tf_op jit(solution)/shard_map/ppermute | solution.py:232
  18.3 4.5 %collective-permute-done.10 = bf16[80,640]{1,0:T(8,128)(2,1)S(1)} collective-permute-done((bf16[80,640]{1,0:T(8,128)(2,1)S(1)}, bf16[80,640]{1,0:T(8,128)(2,1)S(1)}, u32[]{:S(2)}, u32[]{:S(2)}) %collective-permute-start.10) | collective-permute-done | bytes 102432 | tf_op jit(solution)/shard_map/ppermute | solution.py:232
  24.5 2.7 %collective-permute-start = (bf16[128,1280]{1,0:T(8,128)(2,1)}, bf16[128,1280]{1,0:T(8,128)(2,1)}, u32[]{:S(2)}, u32[]{:S(2)}) collective-permute-start(bf16[128,1280]{1,0:T(8,128)(2,1)} %bitcast.8), channel_id=1, source_target_pairs={{0,64},{32,96},{64,0},{96,32},{1,65},{33,97},{65,1},{97,33},{2,66}... | collective-permute-start | bytes 983048 | tf_op jit(solution)/shard_map/ppermute | solution.py:250
  29.6 2.6 %collective-permute-start.3 = (bf16[128,1280]{1,0:T(8,128)(2,1)S(1)}, bf16[128,1280]{1,0:T(8,128)(2,1)}, u32[]{:S(2)}, u32[]{:S(2)}) collective-permute-start(bf16[128,1280]{1,0:T(8,128)(2,1)S(1)} %bitcast.92), channel_id=1, source_target_pairs={{0,128},{8,136},{16,144},{24,152},{128,0},{136,8},{144,16},{152,24... | collective-permute-start | bytes 983048 | tf_op jit(solution)/shard_map/ppermute | solution.py:251
  32.2 1.8 %copy.13 = f32[4,4,4,8,1280]{4,3,0,2,1:T(8,128)} copy(bf16[4,4,4,8,1280]{4,3,2,1,0:T(8,128)(2,1)S(1)} %bitcast.89) | data formatting | bytes 3932160 | tf_op jit(solution)/shard_map/convert_element_type | solution.py:258
  35.1 2.0 %collective-permute-start.4 = (bf16[128,1280]{1,0:T(8,128)(2,1)}, bf16[128,1280]{1,0:T(8,128)(2,1)S(1)}, u32[]{:S(2)}, u32[]{:S(2)}) collective-permute-start(bf16[128,1280]{1,0:T(8,128)(2,1)} %collective-permute-done), channel_id=1, source_target_pairs={{0,128},{8,136},{16,144},{24,152},{128,0},{136,8},{144,16},{152,24... | collective-permute-start | bytes 983048 | tf_op jit(solution)/shard_map/ppermute | solution.py:251
  38.2 7.3 %collective-permute-done.1 = bf16[128,1280]{1,0:T(8,128)(2,1)} collective-permute-done((bf16[128,1280]{1,0:T(8,128)(2,1)}, bf16[128,1280]{1,0:T(8,128)(2,1)}, u32[]{:S(2)}, u32[]{:S(2)}) %collective-permute-start.1) | collective-permute-done | bytes 327712 | tf_op jit(solution)/shard_map/ppermute | solution.py:250
  46.5 5.6 %collective-permute-start.6 = (bf16[128,1280]{1,0:T(8,128)(2,1)S(1)}, bf16[128,1280]{1,0:T(8,128)(2,1)S(1)}, u32[]{:S(2)}, u32[]{:S(2)}) collective-permute-start(bf16[128,1280]{1,0:T(8,128)(2,1)S(1)} %collective-permute-done.2), channel_id=1, source_target_pairs={{0,128},{8,136},{16,144},{24,152},{128,0},{136,8},{144,16},{152,24... | collective-permute-start | bytes 983048 | tf_op jit(solution)/shard_map/ppermute | solution.py:251
  52.2 19.0 %collective-permute-done.3 = bf16[128,1280]{1,0:T(8,128)(2,1)} collective-permute-done((bf16[128,1280]{1,0:T(8,128)(2,1)S(1)}, bf16[128,1280]{1,0:T(8,128)(2,1)}, u32[]{:S(2)}, u32[]{:S(2)}) %collective-permute-start.3) | collective-permute-done | bytes 327712 | tf_op jit(solution)/shard_map/ppermute | solution.py:251
  72.1 5.9 %collective-permute-done.4 = bf16[128,1280]{1,0:T(8,128)(2,1)S(1)} collective-permute-done((bf16[128,1280]{1,0:T(8,128)(2,1)}, bf16[128,1280]{1,0:T(8,128)(2,1)S(1)}, u32[]{:S(2)}, u32[]{:S(2)}) %collective-permute-start.4) | collective-permute-done | bytes 327712 | tf_op jit(solution)/shard_map/ppermute | solution.py:251
  78.1 7.0 %collective-permute-done.5 = bf16[128,1280]{1,0:T(8,128)(2,1)S(1)} collective-permute-done((bf16[128,1280]{1,0:T(8,128)(2,1)}, bf16[128,1280]{1,0:T(8,128)(2,1)S(1)}, u32[]{:S(2)}, u32[]{:S(2)}) %collective-permute-start.5) | collective-permute-done | bytes 327712 | tf_op jit(solution)/shard_map/ppermute | solution.py:251
  85.1 7.0 %collective-permute-done.6 = bf16[128,1280]{1,0:T(8,128)(2,1)S(1)} collective-permute-done((bf16[128,1280]{1,0:T(8,128)(2,1)S(1)}, bf16[128,1280]{1,0:T(8,128)(2,1)S(1)}, u32[]{:S(2)}, u32[]{:S(2)}) %collective-permute-start.6) | collective-permute-done | bytes 327712 | tf_op jit(solution)/shard_map/ppermute | solution.py:251
  93.4 8.4 %shard_map.55 = (bf16[4,4,32,640]{3,2,1,0:T(8,128)(2,1)S(1)}, bf16[4,4,80,1920]{3,2,1,0:T(8,128)(2,1)S(1)}, bf16[4,4,80,1280]{3,2,1,0:T(8,128)(2,1)S(1)}) custom-call(bf16[1024,1280]{1,0:T(8,128)(2,1)S(1)} %constant_dynamic-update-slice_fusion.x_ref, bf16[4,4,2,4,80,640]{5,4,3,2,1,0:T(8,128)(2,1)} %bitcast.84), custom_call_target="tpu_custom_call" | custom-call | flops 4194304000 | bytes 6553600 | tf_op jit(solution)/shard_map/pallas_call | solution.py:170
  103.4 1.8 %collective-permute-start.13 = (bf16[128,640]{1,0:T(8,128)(2,1)S(1)}, bf16[128,640]{1,0:T(8,128)(2,1)S(1)}, u32[]{:S(2)}, u32[]{:S(2)}) collective-permute-start(bf16[128,640]{1,0:T(8,128)(2,1)S(1)} %bitcast.98), channel_id=1, source_target_pairs={{0,96},{32,64},{64,32},{96,0},{1,97},{33,65},{65,33},{97,1},{2,98}... | collective-permute-start | bytes 491528 | tf_op jit(solution)/shard_map/ppermute | solution.py:265
  105.5 6.0 %shard_map.56 = bf16[4,4,32,640]{3,2,1,0:T(8,128)(2,1)S(1)} custom-call(bf16[1024,1280]{1,0:T(8,128)(2,1)S(1)} %constant_dynamic-update-slice_fusion.x_ref, bf16[4,4,80,1920]{3,2,1,0:T(8,128)(2,1)S(1)} %get-tuple-element.13.w_ref), custom_call_target="tpu_custom_call" | custom-call | flops 1048576 | bytes 4096 | tf_op jit(solution)/shard_map/pallas_call | solution.py:188
  114.5 2.1 %collective-permute-start.16 = (bf16[128,640]{1,0:T(8,128)(2,1)S(1)}, bf16[128,640]{1,0:T(8,128)(2,1)S(1)}, u32[]{:S(2)}, u32[]{:S(2)}) collective-permute-start(bf16[128,640]{1,0:T(8,128)(2,1)S(1)} %bitcast.99), channel_id=1, source_target_pairs={{0,96},{32,64},{64,32},{96,0},{1,97},{33,65},{65,33},{97,1},{2,98}... | collective-permute-start | bytes 491528 | tf_op jit(solution)/shard_map/ppermute | solution.py:265
  117.9 2.2 %collective-permute-done.14 = bf16[128,640]{1,0:T(8,128)(2,1)S(1)} collective-permute-done((bf16[128,640]{1,0:T(8,128)(2,1)S(1)}, bf16[128,640]{1,0:T(8,128)(2,1)S(1)}, u32[]{:S(2)}, u32[]{:S(2)}) %collective-permute-start.14) | collective-permute-done | bytes 163872 | tf_op jit(solution)/shard_map/ppermute | solution.py:265
  121.3 3.1 %collective-permute-done.16 = bf16[128,640]{1,0:T(8,128)(2,1)S(1)} collective-permute-done((bf16[128,640]{1,0:T(8,128)(2,1)S(1)}, bf16[128,640]{1,0:T(8,128)(2,1)S(1)}, u32[]{:S(2)}, u32[]{:S(2)}) %collective-permute-start.16) | collective-permute-done | bytes 163872 | tf_op jit(solution)/shard_map/ppermute | solution.py:265
  126.4 4.0 %collective-permute-start.17 = (bf16[4,1,64,1280]{3,2,1,0:T(8,128)(2,1)S(1)}, bf16[4,1,64,1280]{3,2,1,0:T(8,128)(2,1)S(1)}, u32[]{:S(2)}, u32[]{:S(2)}) collective-permute-start(bf16[4,1,64,1280]{3,2,1,0:T(8,128)(2,1)S(1)} %get-tuple-element.26), channel_id=1, source_target_pairs={{1,2},{2,1},{3,4},{4,3},{5,6},{6,5},{7,8},{8,7},{9,10},{10,9},{11,... | collective-permute-start | bytes 1966088 | tf_op jit(solution)/shard_map/ppermute | solution.py:281
  130.8 1.9 %fusion.5 = f32[4,2,64,1280]{3,2,1,0:T(8,128)S(1)} fusion(f32[4,2,64,1280]{3,2,1,0:T(8,128)S(1)} %convert_element_type.37, f32[4,2,64,1280]{3,2,1,0:T(8,128)S(1)} %reverse_convert_fusion, f32[2,1280]{1,0:T(2,128)S(1)} %get-tuple-element.52, f32[2,1280]{1,0:T(2,128)S(1)} %get-tuple-element.53, f32[2,1280]{1,0:T(2,128)S(1)} %bitcast.105, ...), kind=kLoop, calls=%fused_computation.13 | loop fusion | flops 8519680 | bytes 7915520 | tf_op jit(solution)/shard_map/add | solution.py:291
  132.7 7.8 %collective-permute-done.17 = bf16[4,1,64,1280]{3,2,1,0:T(8,128)(2,1)S(1)} collective-permute-done((bf16[4,1,64,1280]{3,2,1,0:T(8,128)(2,1)S(1)}, bf16[4,1,64,1280]{3,2,1,0:T(8,128)(2,1)S(1)}, u32[]{:S(2)}, u32[]{:S(2)}) %collective-permute-start.17) | collective-permute-done | bytes 655392 | tf_op jit(solution)/shard_map/ppermute | solution.py:281
  140.9 2.0 %fusion.15 = bf16[4,2,64,1280]{3,2,1,0:T(8,128)(2,1)} fusion(f32[4,2,64,1280]{3,2,1,0:T(8,128)S(1)} %fusion.5, f32[4,2,64,1280]{3,2,1,0:T(8,128)S(1)} %convert_element_type.39, f32[2,1280]{1,0:T(2,128)S(1)} %get-tuple-element.50, f32[2,1280]{1,0:T(2,128)S(1)} %get-tuple-element.51, f32[2,1280]{1,0:T(2,128)S(1)} %bitcast.104), kind=kLoop, calls=%fused_computation.23 | loop fusion | flops 4587520 | bytes 6584320 | tf_op jit(solution)/shard_map/convert_element_type | solution.py:294
  (81 shorter events, 22.3 us)
Async XLA Ops:
  6.5 17.1 %copy-start.1 = (bf16[4,128,1280]{2,1,0:T(8,128)(2,1)S(1)}, bf16[4,128,1280]{2,1,0:T(8,128)(2,1)}, u32[]{:S(2)}) copy-start(bf16[4,128,1280]{2,1,0:T(8,128)(2,1)} %param.5) | copy-start | bytes 3932164
  6.5 86.9 %all-gather.2.cloned.1.call-start = ((), (), s32[]{:S(2)}) async-start(), calls=%async_computation | async-start | bytes 13516800 | tf_op jit(solution)/shard_map/all_gather | solution.py:234
  7.6 1.6 %collective-permute-start.7 = (bf16[40,640]{1,0:T(8,128)(2,1)S(1)}, bf16[40,640]{1,0:T(8,128)(2,1)S(1)}, u32[]{:S(2)}, u32[]{:S(2)}) collective-permute-start(bf16[40,640]{1,0:T(8,128)(2,1)S(1)} %get-tuple-element.41), channel_id=1, source_target_pairs={{0,1},{1,0},{2,3},{3,2},{4,5},{5,4},{6,7},{7,6},{8,9},{9,8},{10,11... | collective-permute-start | bytes 153608 | tf_op jit(solution)/shard_map/ppermute | solution.py:220
  9.2 6.5 %collective-permute-start.8 = (bf16[80,640]{1,0:T(8,128)(2,1)S(1)}, bf16[80,640]{1,0:T(8,128)(2,1)S(1)}, u32[]{:S(2)}, u32[]{:S(2)}) collective-permute-start(bf16[80,640]{1,0:T(8,128)(2,1)S(1)} %maximum_select_fusion.1), channel_id=1, source_target_pairs={{0,8},{8,0},{16,24},{24,16},{128,136},{136,128},{144,152},{152,144... | collective-permute-start | bytes 307208 | tf_op jit(solution)/shard_map/ppermute | solution.py:232
  10.9 7.3 %collective-permute-start.9 = (bf16[80,640]{1,0:T(8,128)(2,1)S(1)}, bf16[80,640]{1,0:T(8,128)(2,1)S(1)}, u32[]{:S(2)}, u32[]{:S(2)}) collective-permute-start(bf16[80,640]{1,0:T(8,128)(2,1)S(1)} %maximum_select_fusion.1), channel_id=1, source_target_pairs={{0,152},{8,16},{16,8},{24,128},{128,24},{136,144},{144,136},{152,0... | collective-permute-start | bytes 307208 | tf_op jit(solution)/shard_map/ppermute | solution.py:232
  15.6 7.2 %collective-permute-start.10 = (bf16[80,640]{1,0:T(8,128)(2,1)S(1)}, bf16[80,640]{1,0:T(8,128)(2,1)S(1)}, u32[]{:S(2)}, u32[]{:S(2)}) collective-permute-start(bf16[80,640]{1,0:T(8,128)(2,1)S(1)} %maximum_select_fusion.1), channel_id=1, source_target_pairs={{0,16},{8,24},{16,0},{24,8},{128,144},{136,152},{144,128},{152,136... | collective-permute-start | bytes 307208 | tf_op jit(solution)/shard_map/ppermute | solution.py:232
  24.5 10.6 %collective-permute-start = (bf16[128,1280]{1,0:T(8,128)(2,1)}, bf16[128,1280]{1,0:T(8,128)(2,1)}, u32[]{:S(2)}, u32[]{:S(2)}) collective-permute-start(bf16[128,1280]{1,0:T(8,128)(2,1)} %bitcast.8), channel_id=1, source_target_pairs={{0,64},{32,96},{64,0},{96,32},{1,65},{33,97},{65,1},{97,33},{2,66}... | collective-permute-start | bytes 983048 | tf_op jit(solution)/shard_map/ppermute | solution.py:250
  28.0 17.5 %collective-permute-start.1 = (bf16[128,1280]{1,0:T(8,128)(2,1)}, bf16[128,1280]{1,0:T(8,128)(2,1)}, u32[]{:S(2)}, u32[]{:S(2)}) collective-permute-start(bf16[128,1280]{1,0:T(8,128)(2,1)} %bitcast.11), channel_id=1, source_target_pairs={{0,32},{32,0},{64,96},{96,64},{1,33},{33,1},{65,97},{97,65},{2,34}... | collective-permute-start | bytes 983048 | tf_op jit(solution)/shard_map/ppermute | solution.py:250
  28.3 5.7 %copy-start.3 = (f32[3,3,1280]{2,1,0:T(4,128)S(1)}, f32[3,3,1280]{2,1,0:T(4,128)}, u32[]{:S(2)}) copy-start(f32[3,3,1280]{2,1,0:T(4,128)} %param.8) | copy-start | bytes 138244
  29.0 17.5 %collective-permute-start.2 = (bf16[128,1280]{1,0:T(8,128)(2,1)}, bf16[128,1280]{1,0:T(8,128)(2,1)S(1)}, u32[]{:S(2)}, u32[]{:S(2)}) collective-permute-start(bf16[128,1280]{1,0:T(8,128)(2,1)} %bitcast.14), channel_id=1, source_target_pairs={{0,96},{32,64},{64,32},{96,0},{1,97},{33,65},{65,33},{97,1},{2,98}... | collective-permute-start | bytes 983048 | tf_op jit(solution)/shard_map/ppermute | solution.py:250
  29.6 41.5 %collective-permute-start.3 = (bf16[128,1280]{1,0:T(8,128)(2,1)S(1)}, bf16[128,1280]{1,0:T(8,128)(2,1)}, u32[]{:S(2)}, u32[]{:S(2)}) collective-permute-start(bf16[128,1280]{1,0:T(8,128)(2,1)S(1)} %bitcast.92), channel_id=1, source_target_pairs={{0,128},{8,136},{16,144},{24,152},{128,0},{136,8},{144,16},{152,24... | collective-permute-start | bytes 983048 | tf_op jit(solution)/shard_map/ppermute | solution.py:251
  35.1 42.9 %collective-permute-start.4 = (bf16[128,1280]{1,0:T(8,128)(2,1)}, bf16[128,1280]{1,0:T(8,128)(2,1)S(1)}, u32[]{:S(2)}, u32[]{:S(2)}) collective-permute-start(bf16[128,1280]{1,0:T(8,128)(2,1)} %collective-permute-done), channel_id=1, source_target_pairs={{0,128},{8,136},{16,144},{24,152},{128,0},{136,8},{144,16},{152,24... | collective-permute-start | bytes 983048 | tf_op jit(solution)/shard_map/ppermute | solution.py:251
  45.4 39.6 %collective-permute-start.5 = (bf16[128,1280]{1,0:T(8,128)(2,1)}, bf16[128,1280]{1,0:T(8,128)(2,1)S(1)}, u32[]{:S(2)}, u32[]{:S(2)}) collective-permute-start(bf16[128,1280]{1,0:T(8,128)(2,1)} %collective-permute-done.1), channel_id=1, source_target_pairs={{0,128},{8,136},{16,144},{24,152},{128,0},{136,8},{144,16},{152,24... | collective-permute-start | bytes 983048 | tf_op jit(solution)/shard_map/ppermute | solution.py:251
  46.5 45.6 %collective-permute-start.6 = (bf16[128,1280]{1,0:T(8,128)(2,1)S(1)}, bf16[128,1280]{1,0:T(8,128)(2,1)S(1)}, u32[]{:S(2)}, u32[]{:S(2)}) collective-permute-start(bf16[128,1280]{1,0:T(8,128)(2,1)S(1)} %collective-permute-done.2), channel_id=1, source_target_pairs={{0,128},{8,136},{16,144},{24,152},{128,0},{136,8},{144,16},{152,24... | collective-permute-start | bytes 983048 | tf_op jit(solution)/shard_map/ppermute | solution.py:251
  101.9 9.7 %collective-permute-start.11 = (bf16[128,640]{1,0:T(8,128)(2,1)S(1)}, bf16[128,640]{1,0:T(8,128)(2,1)S(1)}, u32[]{:S(2)}, u32[]{:S(2)}) collective-permute-start(bf16[128,640]{1,0:T(8,128)(2,1)S(1)} %bitcast.102), channel_id=1, source_target_pairs={{0,64},{32,96},{64,0},{96,32},{1,65},{33,97},{65,1},{97,33},{2,66}... | collective-permute-start | bytes 491528 | tf_op jit(solution)/shard_map/ppermute | solution.py:265
  103.1 8.5 %collective-permute-start.12 = (bf16[128,640]{1,0:T(8,128)(2,1)S(1)}, bf16[128,640]{1,0:T(8,128)(2,1)S(1)}, u32[]{:S(2)}, u32[]{:S(2)}) collective-permute-start(bf16[128,640]{1,0:T(8,128)(2,1)S(1)} %bitcast.100), channel_id=1, source_target_pairs={{0,32},{32,0},{64,96},{96,64},{1,33},{33,1},{65,97},{97,65},{2,34}... | collective-permute-start | bytes 491528 | tf_op jit(solution)/shard_map/ppermute | solution.py:265
  103.4 9.7 %collective-permute-start.13 = (bf16[128,640]{1,0:T(8,128)(2,1)S(1)}, bf16[128,640]{1,0:T(8,128)(2,1)S(1)}, u32[]{:S(2)}, u32[]{:S(2)}) collective-permute-start(bf16[128,640]{1,0:T(8,128)(2,1)S(1)} %bitcast.98), channel_id=1, source_target_pairs={{0,96},{32,64},{64,32},{96,0},{1,97},{33,65},{65,33},{97,1},{2,98}... | collective-permute-start | bytes 491528 | tf_op jit(solution)/shard_map/ppermute | solution.py:265
  111.5 5.1 %copy-start = (f32[4,4,4,8,1280]{4,3,0,2,1:T(8,128)S(1)}, f32[4,4,4,8,1280]{4,3,0,2,1:T(8,128)}, u32[]{:S(2)}) copy-start(f32[4,4,4,8,1280]{4,3,0,2,1:T(8,128)} %copy.13) | copy-start | bytes 7864324
  113.2 6.9 %collective-permute-start.14 = (bf16[128,640]{1,0:T(8,128)(2,1)S(1)}, bf16[128,640]{1,0:T(8,128)(2,1)S(1)}, u32[]{:S(2)}, u32[]{:S(2)}) collective-permute-start(bf16[128,640]{1,0:T(8,128)(2,1)S(1)} %bitcast.103), channel_id=1, source_target_pairs={{0,64},{32,96},{64,0},{96,32},{1,65},{33,97},{65,1},{97,33},{2,66}... | collective-permute-start | bytes 491528 | tf_op jit(solution)/shard_map/ppermute | solution.py:265
  114.5 6.9 %collective-permute-start.15 = (bf16[128,640]{1,0:T(8,128)(2,1)S(1)}, bf16[128,640]{1,0:T(8,128)(2,1)S(1)}, u32[]{:S(2)}, u32[]{:S(2)}) collective-permute-start(bf16[128,640]{1,0:T(8,128)(2,1)S(1)} %bitcast.101), channel_id=1, source_target_pairs={{0,32},{32,0},{64,96},{96,64},{1,33},{33,1},{65,97},{97,65},{2,34}... | collective-permute-start | bytes 491528 | tf_op jit(solution)/shard_map/ppermute | solution.py:265
  114.5 10.0 %collective-permute-start.16 = (bf16[128,640]{1,0:T(8,128)(2,1)S(1)}, bf16[128,640]{1,0:T(8,128)(2,1)S(1)}, u32[]{:S(2)}, u32[]{:S(2)}) collective-permute-start(bf16[128,640]{1,0:T(8,128)(2,1)S(1)} %bitcast.99), channel_id=1, source_target_pairs={{0,96},{32,64},{64,32},{96,0},{1,97},{33,65},{65,33},{97,1},{2,98}... | collective-permute-start | bytes 491528 | tf_op jit(solution)/shard_map/ppermute | solution.py:265
  126.2 4.6 %copy-start.4 = (f32[1280]{0:T(1024)S(1)}, f32[1280]{0:T(1024)}, u32[]{:S(2)}) copy-start(f32[1280]{0:T(1024)} %param.9) | copy-start | bytes 15364
  126.4 14.0 %collective-permute-start.17 = (bf16[4,1,64,1280]{3,2,1,0:T(8,128)(2,1)S(1)}, bf16[4,1,64,1280]{3,2,1,0:T(8,128)(2,1)S(1)}, u32[]{:S(2)}, u32[]{:S(2)}) collective-permute-start(bf16[4,1,64,1280]{3,2,1,0:T(8,128)(2,1)S(1)} %get-tuple-element.26), channel_id=1, source_target_pairs={{1,2},{2,1},{3,4},{4,3},{5,6},{6,5},{7,8},{8,7},{9,10},{10,9},{11,... | collective-permute-start | bytes 1966088 | tf_op jit(solution)/shard_map/ppermute | solution.py:281
  130.4 10.1 %collective-permute-start.18 = (bf16[4,1,64,1280]{3,2,1,0:T(8,128)(2,1)S(1)}, bf16[4,1,64,1280]{3,2,1,0:T(8,128)(2,1)S(1)}, u32[]{:S(2)}, u32[]{:S(2)}) collective-permute-start(bf16[4,1,64,1280]{3,2,1,0:T(8,128)(2,1)S(1)} %get-tuple-element.27), channel_id=1, source_target_pairs={{0,1},{1,0},{2,3},{3,2},{4,5},{5,4},{6,7},{7,6},{8,9},{9,8},{10,11... | collective-permute-start | bytes 1966088 | tf_op jit(solution)/shard_map/ppermute | solution.py:279
  (1 other events, 0.8 us)
Sparse Core Ops, SparseCore 0:
  23.7 69.7 all-gather.1
